TPU v7x, 32 devices: a whole 2x2x4 slice. The times are simulated.
32 devices in a mesh: row: 4 (over y, x), col: 8 (over z, core).
Axes of the slice: x: 2, y: 2, z: 4, core: 2. Of those that a mesh axis runs over, the one named last changes fastest.
Arguments:
- allele_doses: int32 [4096, 65536], P('row', 'col'), may hold values from 0 to 2
- disease_status: int32 [4096], P('row'), may hold values from 0 to 1
- walker_cloud: float32 [64, 65536], P(None, 'col'), may hold values from -21 to 21
- normal_perturbations: float32 [2, 64, 65536], P(None, None, 'col'), may hold values from -6 to 6
- approval_flags: int32 [2, 64], replicated, may hold values 0 or 1
- present_heat: float32 [1], replicated, may hold values from 0.85 to 0.92
- heat_advance: float32 [1], replicated, may hold values from 0.02 to 0.08
- drift_magnitude: float32 [1], replicated, may hold values from 0.8 to 1.2
Outputs:
- particles_out: float32 [64, 65536], P(None, 'col')
- log_weights: float32 [64], replicated
- mean_loglik: float32 [64], replicated
All inputs are finite; a program needn't handle non-finite values.
Results may differ from a plain program's by a relative error of at most 0.0035.
Values may be sent and summed in bfloat16 or wider, within the bound.
No kernel may reach another device: no remote copies, remote signals or barrier semaphores. Data moves between devices by JAX's collectives and lax.ppermute only.
A program may use at most 128 MiB of HBM per device.

v0:
```python
import jax
import jax.numpy as jnp
from jax import lax
from jax.sharding import PartitionSpec as P

P_SIZE = 65536


CLIP_FLOOR = 4.0
SHRINKAGE_LEVEL = 0.5


def contract_cols(left, right):
    return lax.dot_general(
        left, right, (((1,), (1,)), ((), ())), preferred_element_type=jnp.float32
    )


def contract_rows(left, right):
    return lax.dot_general(
        left, right, (((0,), (0,)), ((), ())), preferred_element_type=jnp.float32
    )


def local(
    allele_doses,
    disease_status,
    walker_cloud,
    normal_perturbations,
    approval_flags,
    present_heat,
    heat_advance,
    drift_magnitude,
):
    reciprocal_square = float(P_SIZE) ** (-0.5)
    centered = (allele_doses - 1).astype(jnp.bfloat16)
    outcome_all = disease_status.astype(jnp.float32)
    local_rows = centered.shape[0]
    total_rows = local_rows * lax.axis_size("row")
    upcoming_heat = present_heat[0] + heat_advance[0]
    stepped = drift_magnitude[0]

    def logits_of(regression_weight):
        coef_bf = regression_weight.astype(jnp.bfloat16)
        partial_sum = contract_cols(centered, coef_bf)
        return lax.psum(partial_sum, "col") * reciprocal_square

    def loglik_of(linear_predictor):
        shard_partial_total = jnp.sum(
            outcome_all[:, None] * linear_predictor - jax.nn.softplus(linear_predictor), axis=0
        )
        return lax.psum(shard_partial_total, "row")

    linear_predictor = logits_of(walker_cloud)
    loglik = loglik_of(linear_predictor)
    scaled = heat_advance[0] * loglik
    clipped = jnp.maximum(scaled - jnp.max(scaled), -CLIP_FLOOR)
    log_weights = clipped - jnp.log(jnp.sum(jnp.exp(clipped)))
    weights = jnp.exp(log_weights)
    center = jnp.sum(weights[:, None] * walker_cloud, axis=0)
    spread = jnp.sum(weights[:, None] * (walker_cloud - center[None, :]) ** 2, axis=0) + 1e-06
    spread_total = lax.psum(jnp.sum(spread), "col")
    precond = spread / (spread_total / P_SIZE)
    regression_weight = walker_cloud
    for move in range(2):
        residual_bf = (outcome_all[:, None] - jax.nn.sigmoid(linear_predictor)).astype(jnp.bfloat16)
        likgrad_partial_sum = contract_rows(residual_bf, centered)
        fitness_slope = lax.psum(likgrad_partial_sum.astype(jnp.bfloat16), "row").astype(
            jnp.float32
        )
        slope_vector = (
            upcoming_heat * reciprocal_square * fitness_slope
            - SHRINKAGE_LEVEL
            * regression_weight
            / jnp.sqrt(regression_weight * regression_weight + 1.0)
        )
        proposal = (
            regression_weight
            + stepped * precond[None, :] * slope_vector
            + jnp.sqrt(2.0 * stepped * precond)[None, :] * normal_perturbations[move]
        )
        regression_weight = jnp.where(
            approval_flags[move][:, None] == 1, proposal, regression_weight
        )
        linear_predictor = logits_of(regression_weight)
    mean_loglik = loglik_of(linear_predictor) / total_rows
    return (regression_weight, log_weights, mean_loglik)


def solution(mesh):
    placed = (P("row", "col"), P("row"), P(None, "col"), P(None, None, "col"), P(), P(), P(), P())
    return jax.shard_map(
        local, mesh=mesh, in_specs=placed, out_specs=(P(None, "col"), P(), P()), check_vma=False
    )
```

profile of v0, /device:TPU:0, one launch (start us, length us, event | category | flops | bytes accessed | tf_op | source)
XLA Modules:
  0.0 379.1 jit_solution(17181125565428796703)
XLA Ops:
  7.2 0.0 all-reduce.6.cloned.1.call-start
  7.2 12.5 %add_convert_fusion = bf16[1024,8192]{1,0:T(8,128)(2,1)S(1)} fusion(s32[1024,8192]{1,0:T(8,128)} %param.8), kind=kLoop, calls=%fused_computation | loop fusion | flops 16777216 | bytes 50331648 | tf_op jit(solution)/shard_map/convert_element_type | solution.py:36
  19.8 5.7 %copy-done = bf16[1024,8192]{1,0:T(8,128)(2,1)} copy-done((bf16[1024,8192]{1,0:T(8,128)(2,1)}, bf16[1024,8192]{1,0:T(8,128)(2,1)S(1)}, u32[]{:S(2)}) %copy-start) | copy-done | bytes 16777240
  25.5 5.9 %fusion.8 = f32[1024,64]{0,1:T(8,128)} fusion(bf16[1024,8192]{1,0:T(8,128)(2,1)S(1)} %add_convert_fusion, f32[64,8192]{1,0:T(8,128)S(1)} %copy-done.1), kind=kOutput, calls=%fused_computation.15 | convolution fusion | flops 1074266112 | bytes 19136512 | tf_op jit(solution)/shard_map/dot_general | solution.py:14
  31.4 0.0 all-reduce.6.cloned.1.call-update
  31.4 0.0 all-reduce.8.cloned.1.call-start
  33.5 55.8 %all-reduce.6.cloned.1.call-done = f32[1024,64]{0,1:T(8,128)} async-done(((f32[1024,64]{0,1:T(8,128)}), f32[1024,64]{0,1:T(8,128)}) %all-reduce.6.cloned.1.call-update) | async-done | bytes 262160 | tf_op jit(solution)/shard_map/psum | solution.py:46
  89.2 1.2 fusion.11
  90.5 9.8 %psum.57 = f32[64]{0:T(128)S(1)} all-reduce(f32[64]{0:T(128)S(1)} %fusion.11), channel_id=1, replica_groups=mesh['row'=4,'col'=8] {'row'}, use_global_device_ids=true, to_apply=%region_2.3 | all-reduce | flops 64 | bytes 512 | tf_op jit(solution)/shard_map/psum | solution.py:52
  100.3 9.9 %convolution_convert_fusion.1 = bf16[64,8192]{1,0:T(8,128)(2,1)} fusion(bf16[1024,8192]{1,0:T(8,128)(2,1)} %copy-done, f32[1024,64]{0,1:T(8,128)} %all-reduce.6.cloned.1.call-done, f32[1024]{0:T(1024)S(1)} %convert_element_type.35), kind=kOutput, calls=%fused_computation.2 | convolution fusion | flops 1074659328 | bytes 18092032 | tf_op jit(solution)/shard_map/dot_general | solution.py:20
  110.2 0.0 all-reduce.10.cloned.1.call-start
  110.2 0.7 multiply_reduce_fusion.2
  110.9 1.3 exponential_reduce_fusion
  112.9 1.2 fusion.25
  114.1 0.3 multiply_reduce_fusion.1
  114.4 0.3 multiply_reduce_fusion
  114.7 0.6 add_reduce_fusion
  115.4 14.4 %psum.58 = f32[]{:T(128)} all-reduce(f32[]{:T(128)} %add_reduce_fusion), channel_id=1, replica_groups=mesh['row'=4,'col'=8] {'col'}, use_global_device_ids=true, to_apply=%region_8.9 | all-reduce | flops 1 | bytes 8 | tf_op jit(solution)/shard_map/psum | solution.py:62
  130.3 29.8 %all-reduce.8.cloned.1.call-done = bf16[64,8192]{1,0:T(8,128)(2,1)} async-done(((bf16[64,8192]{1,0:T(8,128)(2,1)}), bf16[64,8192]{1,0:T(8,128)(2,1)}) %all-reduce.8.cloned.1.call-update) | async-done | bytes 1048592 | tf_op jit(solution)/shard_map/psum | solution.py:68
  160.1 12.6 %fusion.6 = f32[1024,64]{0,1:T(8,128)} fusion(bf16[1024,8192]{1,0:T(8,128)(2,1)} %copy-done, f32[64,8192]{1,0:T(8,128)S(1)} %copy-done.1, f32[2,64,8192]{2,1,0:T(8,128)} %param.11, bf16[64,8192]{1,0:T(8,128)(2,1)} %all-reduce.8.cloned.1.call-done, f32[8192]{0:T(1024)S(1)} %get-tuple-element.6, f32[]{:T(128)S(6)} %mul.145, f32[8192]{0:T(1024)S(1)} %get-tuple-element.5, ...), kind=kOutput, calls=%fused_computation.13 | convolution fusion | flops 1080557568 | bytes 22347844 | tf_op jit(solution)/shard_map/dot_general | solution.py:14
  172.8 0.0 all-reduce.12.cloned.1.call-start
  172.8 55.0 %all-reduce.10.cloned.1.call-done = f32[1024,64]{0,1:T(8,128)} async-done(((f32[1024,64]{0,1:T(8,128)}), f32[1024,64]{0,1:T(8,128)}) %all-reduce.10.cloned.1.call-update) | async-done | bytes 262160 | tf_op jit(solution)/shard_map/psum | solution.py:46
  227.8 9.9 %convolution_convert_fusion = bf16[64,8192]{1,0:T(8,128)(2,1)} fusion(bf16[1024,8192]{1,0:T(8,128)(2,1)} %copy-done, f32[1024,64]{0,1:T(8,128)} %all-reduce.10.cloned.1.call-done, f32[1024]{0:T(1024)S(1)} %convert_element_type.35), kind=kOutput, calls=%fused_computation.1 | convolution fusion | flops 1074659328 | bytes 18092032 | tf_op jit(solution)/shard_map/dot_general | solution.py:20
  237.6 0.0 all-reduce.14.cloned.1.call-start
  237.7 51.6 %all-reduce.12.cloned.1.call-done = bf16[64,8192]{1,0:T(8,128)(2,1)} async-done(((bf16[64,8192]{1,0:T(8,128)(2,1)}), bf16[64,8192]{1,0:T(8,128)(2,1)}) %all-reduce.12.cloned.1.call-update) | async-done | bytes 1048592 | tf_op jit(solution)/shard_map/psum | solution.py:68
  289.3 3.5 fusion.1
  292.9 1.3 copy-done.2
  294.2 11.7 %fusion.4 = f32[1024,64]{0,1:T(8,128)} fusion(bf16[1024,8192]{1,0:T(8,128)(2,1)} %copy-done, f32[64,8192]{1,0:T(8,128)S(1)} %fusion.1), kind=kOutput, calls=%fused_computation.11 | convolution fusion | flops 1074266112 | bytes 19136512 | tf_op jit(solution)/shard_map/dot_general | solution.py:14
  305.9 55.1 %all-reduce.14.cloned.1.call-done = f32[1024,64]{0,1:T(8,128)} async-done(((f32[1024,64]{0,1:T(8,128)}), f32[1024,64]{0,1:T(8,128)}) %all-reduce.14.cloned.1.call-update) | async-done | bytes 262160 | tf_op jit(solution)/shard_map/psum | solution.py:46
  361.0 1.2 fusion.13
  362.2 9.8 %psum.63 = f32[64]{0:T(128)S(1)} all-reduce(f32[64]{0:T(128)S(1)} %fusion.13), channel_id=1, replica_groups=mesh['row'=4,'col'=8] {'row'}, use_global_device_ids=true, to_apply=%region_14.15 | all-reduce | flops 64 | bytes 512 | tf_op jit(solution)/shard_map/psum | solution.py:52
  372.1 0.5 broadcast_multiply_fusion.2
  (18 shorter events, 0.1 us)
Async XLA Ops:
  7.2 18.3 %copy-start.1 = (f32[64,8192]{1,0:T(8,128)S(1)}, f32[64,8192]{1,0:T(8,128)}, u32[]{:S(2)}) copy-start(f32[64,8192]{1,0:T(8,128)} %param.10) | copy-start | bytes 6291460
  7.2 82.1 %all-reduce.6.cloned.1.call-start = ((), (), s32[]{:S(2)}) async-start(), calls=%async_computation | async-start | bytes 524288 | tf_op jit(solution)/shard_map/psum | solution.py:46
  19.7 5.7 %copy-start = (bf16[1024,8192]{1,0:T(8,128)(2,1)}, bf16[1024,8192]{1,0:T(8,128)(2,1)S(1)}, u32[]{:S(2)}) copy-start(bf16[1024,8192]{1,0:T(8,128)(2,1)S(1)} %add_convert_fusion) | copy-start | bytes 50331652
  25.5 6.0 %copy-start.4 = (s32[1024]{0:T(1024)S(1)}, s32[1024]{0:T(1024)}, u32[]{:S(2)}) copy-start(s32[1024]{0:T(1024)} %param.9) | copy-start | bytes 12292
  25.5 8.0 %copy-start.5 = (s32[2,64]{1,0:T(2,128)S(1)}, s32[2,64]{1,0:T(2,128)}, u32[]{:S(2)}) copy-start(s32[2,64]{1,0:T(2,128)} %param.12) | copy-start | bytes 1540
  31.4 128.7 %all-reduce.8.cloned.1.call-start = ((), (), s32[]{:S(2)}) async-start(), calls=%async_computation.1 | async-start | bytes 2097152 | tf_op jit(solution)/shard_map/psum | solution.py:68
  110.2 117.6 %all-reduce.10.cloned.1.call-start = ((), (), s32[]{:S(2)}) async-start(), calls=%async_computation.2 | async-start | bytes 524288 | tf_op jit(solution)/shard_map/psum | solution.py:46
  172.7 116.6 %copy-start.3 = (bf16[64,8192]{1,0:T(8,128)(2,1)S(1)}, bf16[64,8192]{1,0:T(8,128)(2,1)}, u32[]{:S(2)}) copy-start(bf16[64,8192]{1,0:T(8,128)(2,1)} %all-reduce.8.cloned.1.call-done) | copy-start | bytes 3145732
  172.8 116.6 %all-reduce.12.cloned.1.call-start = ((), (), s32[]{:S(2)}) async-start(), calls=%async_computation.3 | async-start | bytes 2097152 | tf_op jit(solution)/shard_map/psum | solution.py:68
  237.6 123.3 %all-reduce.14.cloned.1.call-start = ((), (), s32[]{:S(2)}) async-start(), calls=%async_computation.4 | async-start | bytes 524288 | tf_op jit(solution)/shard_map/psum | solution.py:46
  292.9 1.3 copy-start.2
Sparse Core Ops, SparseCore 0:
  31.5 57.6 all-reduce.5
  110.3 49.7 all-reduce.7
  172.9 54.8 all-reduce.9
  237.8 51.5 all-reduce.11
  306.0 54.9 all-reduce.13
where the time goes:
time: 380 us; the launch traced here: 379 us
  waiting for transfers between devices  247 us (65%)
  matrix products  49.9 us (13%)
  blocking collectives  34.1 us (9%)
  other arithmetic  23.5 us (6%)
  between operations  17.1 us (5%)
  local copies, waits for them, and re-layouts  7.04 us (2%)
    psum x3, waiting for transfers between devices, logits_of(): return lax.psum(partial_sum, 'col') * reciprocal_square  166 us
    psum x2, waiting for transfers between devices, local(): lax.psum(likgrad_partial_sum.astype(jnp.bfloat16), 'row')  81.4 us
    dot_general x3, matrix products, contract_cols(): lax.dot_general(left, right, (((1,), (1,)), ((), ())), preferred_element_...  30.2 us
    dot_general x2, matrix products, contract_rows(): lax.dot_general(left, right, (((0,), (0,)), ((), ())), preferred_element_...  19.7 us
    psum x2, blocking collectives, loglik_of(): return lax.psum(shard_partial_total, 'row')  19.7 us
    psum x1, blocking collectives, local(): spread_total = lax.psum(jnp.sum(spread), 'col')  14.4 us
    convert_element_type x1, other arithmetic, local(): centered = (allele_doses - 1).astype(jnp.bfloat16)  12.5 us
  transfers between devices with their start and end apart: 5, of which 5 were waited for; matrix products, arithmetic and copies ran while one was open for 1% of the time, Pallas kernels for 0%

commit v1 on v0

v1 whole, which is shorter than its diff:
```python
import functools

import jax
import jax.numpy as jnp
from jax import lax
from jax.experimental import pallas as pl
from jax.experimental.pallas import tpu as pltpu
from jax.sharding import PartitionSpec as P

CLIP_FLOOR = 4.0
SHRINKAGE_LEVEL = 0.5
F32 = jnp.float32
BF16 = jnp.bfloat16
VMEM = pl.BlockSpec(memory_space=pltpu.VMEM)
SMEM = pl.BlockSpec(memory_space=pltpu.SMEM)
HBM = pl.BlockSpec(memory_space=pltpu.HBM)
MIB = 1 << 20
LANES = 128
CHUNKS = 2
PIECES = 2


def rows_dot(left, right):
    return lax.dot_general(left, right, (((1,), (1,)), ((), ())), preferred_element_type=F32)


def tile_of(size, most):
    while size % most:
        most //= 2
    return most


def params(mib):
    return pltpu.CompilerParams(vmem_limit_bytes=mib * MIB)


def cost(flops):
    return pl.CostEstimate(flops=flops, bytes_accessed=0, transcendentals=0)


def as_lanes(value):
    high = value.astype(BF16)
    rest = value - high.astype(F32)
    middle = rest.astype(BF16)
    low = (rest - middle.astype(F32)).astype(BF16)
    lane = lax.broadcasted_iota(jnp.int32, (value.shape[0], LANES), 1)
    zero = jnp.zeros((value.shape[0], LANES), F32)
    out = jnp.where(lane == 0, high.astype(F32), zero)
    out = jnp.where(lane == 1, middle.astype(F32), out)
    return jnp.where(lane == 2, low.astype(F32), out).astype(BF16)


def flipped(value):
    size = max(value.shape)
    diagonal = lax.broadcasted_iota(jnp.int32, (size, size), 0) == lax.broadcasted_iota(
        jnp.int32, (size, size), 1
    )
    return jnp.sum(
        jnp.where(diagonal, value, 0.0), axis=int(value.shape[0] == 1), keepdims=True
    )


def from_lanes(lanes):
    return jnp.sum(lanes.astype(F32), axis=1, keepdims=True)


def center_kernel(block, with_gram, core, doses, cloud, centered, mine, other, cloud_bf, logits, gram):
    step = pl.program_id(0)
    variants = doses.shape[1]
    people = logits.shape[1]
    half = people // 2

    @pl.when(step == 0)
    def _():
        cloud_bf[...] = cloud[...].astype(BF16)

    if with_gram:

        @pl.when(step == 0)
        def _():
            width = tile_of(variants, 1024)
            total = None
            for start in range(0, variants, width):
                c = cloud[:, start : start + width]
                c = c - jnp.mean(c, axis=0, keepdims=True)
                high = c.astype(BF16)
                low = (c - high.astype(F32)).astype(BF16)
                term = rows_dot(high, high) + 2.0 * rows_dot(high, low)
                total = term if total is None else total + term
            gram[...] = jnp.zeros(gram.shape, F32)
            gram[:, : total.shape[1]] = total

    width = tile_of(variants, 2048)
    total = None
    for start in range(0, variants, width):
        part = (doses[:, start : start + width] - 1).astype(F32).astype(BF16)
        centered[pl.ds(pl.multiple_of(step * block, block), block), start : start + width] = part
        term = rows_dot(part, cloud_bf[:, start : start + width])
        total = term if total is None else total + term
    logits[:, pl.ds(pl.multiple_of(step * block, block), block)] = total.T

    @pl.when(step == pl.num_programs(0) - 1)
    def _():
        first = core[0]
        mine[:, :half] = logits[:, pl.ds(pl.multiple_of(first * half, half), half)]
        other[:, :half] = logits[:, pl.ds(pl.multiple_of((1 - first) * half, half), half)]
        if with_gram:
            mine[:, half:] = gram[...]
            other[:, half:] = gram[...]


def center_and_first_logits(chunk, core, doses, cloud):
    variants = doses.shape[1]
    people = doses.shape[0] // CHUNKS
    particles = cloud.shape[0]
    block = min(256, people)
    steps = people // block
    with_gram = chunk == 0
    lanes = people // 2 + (LANES if with_gram else 0)
    exchanged = jax.ShapeDtypeStruct((particles, lanes), F32)
    return pl.pallas_call(
        functools.partial(center_kernel, block, with_gram),
        grid=(steps,),
        in_specs=[
            SMEM,
            pl.BlockSpec((block, variants), lambda i: (chunk * steps + i, 0)),
            pl.BlockSpec((particles, variants), lambda i: (0, 0), pipeline_mode=pl.Buffered(1)),
        ],
        out_specs=[VMEM, VMEM, VMEM],
        out_shape=[pltpu.VMEM((people, variants), BF16), exchanged, exchanged],
        scratch_shapes=[
            pltpu.VMEM((particles, variants), BF16),
            pltpu.VMEM((particles, people), F32),
            pltpu.VMEM((particles, LANES), F32),
        ],
        compiler_params=params(28),
        cost_estimate=cost(16 * particles * people * variants),
        name="center_and_first_logits",
    )(core, doses, cloud)


def residual_kernel(parts, people, chunks, scale, earlier, tail, gram, loglik_as, core, status, *refs):
    sent, refs = refs[:parts], list(refs[parts:])
    before = refs.pop(0) if earlier else None
    half = people // 2
    outcome = jnp.concatenate(
        [
            status[:, pl.ds(pl.multiple_of(chunk * people + core[0] * half, half), half)]
            for chunk in chunks
        ],
        axis=1,
    ).astype(F32)
    share = half * len(chunks)
    values = tree_sum([ref[...].astype(F32) for ref in sent])
    logits = values[:, :share] * scale
    residual = refs.pop(0)
    residual[:, :share] = (outcome - jax.nn.sigmoid(logits)).astype(BF16)
    if loglik_as or tail:
        softplus = jnp.maximum(logits, 0.0) + jnp.log1p(jnp.exp(-jnp.abs(logits)))
        loglik = jnp.sum(outcome * logits - softplus, axis=1, keepdims=True)
        if earlier:
            loglik = loglik + before[...]
        if tail:
            residual[:, share:] = as_lanes(loglik)
        if loglik_as:
            refs.pop(0)[...] = loglik if loglik_as == "column" else flipped(loglik)
    if gram:
        refs.pop(0)[...] = values[:, share:]


def residual_of(scale, core, status, chunks, sent, earlier=None, tail=False, gram=False, loglik_as=None):
    particles = sent[0].shape[0]
    people = status.shape[1] // CHUNKS
    share = people // 2 * len(chunks)
    out_shape = [jax.ShapeDtypeStruct((particles, share + (LANES if tail else 0)), BF16)]
    if loglik_as:
        shape = (particles, 1) if loglik_as == "column" else (1, particles)
        out_shape.append(jax.ShapeDtypeStruct(shape, F32))
    if gram:
        out_shape.append(jax.ShapeDtypeStruct((particles, LANES), F32))
    operands = [core, status, *sent] + ([earlier] if earlier is not None else [])
    return pl.pallas_call(
        functools.partial(
            residual_kernel, len(sent), people, chunks, scale, earlier is not None, tail, gram, loglik_as
        ),
        in_specs=[SMEM] + [VMEM] * (len(operands) - 1),
        out_specs=[VMEM] * len(out_shape),
        out_shape=out_shape,
        compiler_params=params(12),
        name="residual",
    )(*operands)


def gradient_kernel(count, first, columns, tail, core, *refs):
    pairs, centered = refs[: 2 * count], refs[2 * count : 2 * count + CHUNKS]
    grad, residual = refs[2 * count + CHUNKS :]
    people = centered[0].shape[0]
    half = people // 2
    mine = core[0]
    for chunk in range(CHUNKS):
        own, other = (pairs[2 * chunk], pairs[2 * chunk + 1]) if count == CHUNKS else pairs
        at = 0 if count == CHUNKS else chunk * half
        base = chunk * people
        residual[:, pl.ds(pl.multiple_of(base + mine * half, half), half)] = own[:, at : at + half]
        residual[:, pl.ds(pl.multiple_of(base + (1 - mine) * half, half), half)] = other[
            :, at : at + half
        ]
    width = tile_of(columns, 512)
    for start in range(0, columns, width):
        here = slice(first + start, first + start + width)
        grad[:, start : start + width] = sum(
            jnp.dot(
                residual[:, chunk * people : (chunk + 1) * people],
                centered[chunk][:, here],
                preferred_element_type=F32,
            )
            for chunk in range(CHUNKS)
        ).astype(BF16)
    if tail:
        grad[:, columns:] = as_lanes(from_lanes(own[:, half:]) + from_lanes(other[:, half:]))


def gradient(first, columns, tail, core, pairs, centered):
    particles = pairs[0].shape[0]
    people = sum(c.shape[0] for c in centered)
    return pl.pallas_call(
        functools.partial(gradient_kernel, len(pairs) // 2, first, columns, tail),
        in_specs=[SMEM] + [VMEM] * (len(pairs) + CHUNKS),
        out_specs=VMEM,
        out_shape=jax.ShapeDtypeStruct((particles, columns + (LANES if tail else 0)), BF16),
        scratch_shapes=[pltpu.VMEM((particles, people), BF16)],
        compiler_params=params(8),
        cost_estimate=cost(8 * particles * people * columns),
        name="gradient",
    )(core, *pairs, *centered)


def pair_sum_kernel(columns, tail, left, right, out):
    total = left[:, :columns].astype(F32) + right[:, :columns].astype(F32)
    out[:, :columns] = total.astype(BF16)
    if tail:
        out[:, columns:] = as_lanes(from_lanes(left[:, columns:]) + from_lanes(right[:, columns:]))


def pair_sum(columns, tail, left, right):
    return pl.pallas_call(
        functools.partial(pair_sum_kernel, columns, tail),
        in_specs=[VMEM, VMEM],
        out_specs=VMEM,
        out_shape=jax.ShapeDtypeStruct(left.shape, BF16),
        compiler_params=params(8),
        name="pair_sum",
    )(left, right)


def weigh(total_variants, heat_advance, loglik, gram):
    scaled = heat_advance * loglik
    clipped = jnp.maximum(scaled - jnp.max(scaled, axis=0, keepdims=True), -CLIP_FLOOR)
    log_weights = clipped - jnp.log(jnp.sum(jnp.exp(clipped), axis=0, keepdims=True))
    weights = jnp.exp(log_weights)
    particles = loglik.shape[0]
    gram = gram[:, :particles]
    diagonal = lax.broadcasted_iota(jnp.int32, gram.shape, 0) == lax.broadcasted_iota(
        jnp.int32, gram.shape, 1
    )
    square = jnp.sum(jnp.where(diagonal, gram * weights, 0.0), axis=0, keepdims=True)
    mixed = jnp.sum(weights * gram, axis=0, keepdims=True) * flipped(weights)
    total = jnp.sum(square - mixed, axis=1, keepdims=True)
    return log_weights, weights, total / total_variants + 1e-06


def update_kernel(first, move, total_variants, core, old_heat, advance, drift_ref, flags, cloud, noise, *refs):
    known, refs = refs[0], refs[1:]
    centered, refs = refs[:CHUNKS], refs[CHUNKS:]
    grads, refs = refs[: 2 * PIECES], list(refs[2 * PIECES :])
    moved, mine, other = refs[:3]
    refs = refs[3:]
    if first:
        log_weights_out, size_out = refs[:2]
        refs = refs[2:]
    c_buffer, noise_buffer, total, in_sems, out_sems = refs
    particles, variants = cloud.shape
    people = centered[0].shape[0]
    width = tile_of(variants // PIECES, 2048)
    steps = variants // width

    def load(step):
        here = pl.ds(step * width, width)
        return (
            pltpu.make_async_copy(cloud.at[:, here], c_buffer.at[:, here], in_sems.at[0, step]),
            pltpu.make_async_copy(noise.at[move, :, here], noise_buffer.at[:, here], in_sems.at[1, step]),
        )

    def store(step):
        here = pl.ds(step * width, width)
        return pltpu.make_async_copy(c_buffer.at[:, here], moved.at[:, here], out_sems.at[step])

    for step in range(steps):
        for copy in load(step):
            copy.start()
    heat = (old_heat[0] + advance[0]) * float(total_variants) ** (-0.5)
    drift = drift_ref[0]
    approved = flipped(flags[move : move + 1, :].astype(F32)) > 0.5
    columns = variants // PIECES
    if first:
        loglik = from_lanes(grads[0][:, columns:]) + from_lanes(grads[1][:, columns:])
        log_weights, weights, mean_spread = weigh(total_variants, advance[0], loglik, known[...])
        log_weights_out[...] = flipped(log_weights)
        factor = drift / mean_spread
    for step in range(steps):
        piece, begin = divmod(step * width, columns)
        for copy in load(step):
            copy.wait()
        chosen = []
        narrow = tile_of(width, 512)
        for start in range(step * width, (step + 1) * width, narrow):
            here = slice(start, start + narrow)
            local = slice(start - piece * columns, start - piece * columns + narrow)
            c = c_buffer[:, here]
            if first:
                center = jnp.sum(weights * c, axis=0, keepdims=True)
                spread = jnp.sum(weights * (c - center) ** 2, axis=0, keepdims=True) + 1e-06
                size = spread * factor
                size_out[:, here] = size
            else:
                size = known[:, here]
            slope = grads[2 * piece][:, local].astype(F32) + grads[2 * piece + 1][:, local].astype(F32)
            rise = heat * slope - SHRINKAGE_LEVEL * c * lax.rsqrt(c * c + 1.0)
            proposal = c + size * rise + jnp.sqrt(2.0 * size) * noise_buffer[:, here]
            c = jnp.where(approved, proposal, c)
            c_buffer[:, here] = c
            chosen.append(c.astype(BF16))
        store(step).start()
        chosen = jnp.concatenate(chosen, axis=1)
        for chunk in range(CHUNKS):
            rows = slice(chunk * people, (chunk + 1) * people)
            term = rows_dot(centered[chunk][:, step * width : (step + 1) * width], chosen)
            total[rows, :] = term if step == 0 else total[rows, :] + term
    half = people // 2
    here = core[0]
    for chunk in range(CHUNKS):
        out = slice(chunk * half, (chunk + 1) * half)
        base = chunk * people
        mine[:, out] = total[pl.ds(pl.multiple_of(base + here * half, half), half), :].T
        other[:, out] = total[pl.ds(pl.multiple_of(base + (1 - here) * half, half), half), :].T
    for step in range(steps):
        store(step).wait()


def update_and_logits(first, move, total_variants, core, scalars, flags, cloud, noise, known, centered, grads):
    particles, variants = cloud.shape
    people = sum(c.shape[0] for c in centered)
    steps = variants // tile_of(variants // PIECES, 2048)
    exchanged = jax.ShapeDtypeStruct((particles, people // 2), F32)
    out_shape = [jax.ShapeDtypeStruct((particles, variants), F32), exchanged, exchanged]
    if first:
        out_shape.append(jax.ShapeDtypeStruct((1, particles), F32))
        out_shape.append(jax.ShapeDtypeStruct((1, variants), F32))
    return pl.pallas_call(
        functools.partial(update_kernel, first, move, total_variants),
        in_specs=[SMEM] * 4 + [VMEM, HBM, HBM] + [VMEM] * (1 + CHUNKS + len(grads)),
        out_specs=[HBM] + [VMEM] * (len(out_shape) - 1),
        out_shape=out_shape,
        scratch_shapes=[
            pltpu.VMEM((particles, variants), F32),
            pltpu.VMEM((particles, variants), F32),
            pltpu.VMEM((people, particles), F32),
            pltpu.SemaphoreType.DMA((2, steps)),
            pltpu.SemaphoreType.DMA((steps,)),
        ],
        compiler_params=params(16),
        cost_estimate=cost(8 * particles * people * variants),
        name="update_and_logits",
    )(core, *scalars, flags, cloud, noise, known, *centered, *grads)


def swap(value, axis, distance):
    size = lax.axis_size(axis)
    return lax.ppermute(value, axis, [(i, i ^ distance) for i in range(size)])


def tree_sum(values):
    values = list(values)
    while len(values) > 1:
        values = [values[i] + values[i + 1] for i in range(0, len(values), 2)]
    return values[0]


def over_chips(mine, other, link):
    mine = (mine + swap(other, "col", 1)).astype(link)
    return [mine] + [swap(mine, "col", d) for d in range(2, lax.axis_size("col"), 2)]


def sum_small(value):
    value = value + swap(value, "col", 1)
    size = lax.axis_size("row")
    return tree_sum([value] + [swap(value, "row", d) for d in range(1, size)])


def local(
    allele_doses,
    disease_status,
    walker_cloud,
    normal_perturbations,
    approval_flags,
    present_heat,
    heat_advance,
    drift_magnitude,
):
    people, variants = allele_doses.shape
    total_variants = variants * lax.axis_size("col")
    total_people = people * lax.axis_size("row")
    scale = float(total_variants) ** (-0.5)
    core = lax.axis_index("col") % 2
    core_ref = core.reshape(1)
    status = disease_status.reshape(1, people)
    scalars = (present_heat, heat_advance, drift_magnitude)
    row_bits = [1 << b for b in range(lax.axis_size("row").bit_length() - 1)]

    centered, pairs, loglik, gram = [], [], None, None
    for chunk in range(CHUNKS):
        part, mine, other = center_and_first_logits(chunk, core_ref, allele_doses, walker_cloud)
        centered.append(part)
        sent = over_chips(mine, other, F32)
        tail = chunk == CHUNKS - 1
        own, *extra = residual_of(
            scale,
            core_ref,
            status,
            (chunk,),
            sent,
            earlier=loglik,
            tail=tail,
            gram=chunk == 0,
            loglik_as=None if tail else "column",
        )
        if chunk == 0:
            gram = extra.pop()
        if not tail:
            (loglik,) = extra
        pairs += [own, swap(own, "col", 1)]

    moved, known = walker_cloud, gram
    columns = variants // PIECES
    for move in range(2):
        first = move == 0
        grads = []
        for piece in range(PIECES):
            tail = first and piece == 0
            grad = gradient(piece * columns, columns, tail, core_ref, pairs, centered)
            order = row_bits if piece % 2 == 0 else row_bits[::-1]
            for bit in order[:-1]:
                grad = pair_sum(columns, tail, grad, swap(grad, "row", bit))
            grads += [grad, swap(grad, "row", order[-1])]
        moved, mine, other, *extra = update_and_logits(
            first,
            move,
            total_variants,
            core_ref,
            scalars,
            approval_flags,
            moved,
            normal_perturbations,
            known,
            centered,
            grads,
        )
        if first:
            log_weights, known = extra
        sent = over_chips(mine, other, BF16)
        if first:
            (own,) = residual_of(scale, core_ref, status, tuple(range(CHUNKS)), sent)
            pairs = [own, swap(own, "col", 1)]
        else:
            _, loglik = residual_of(
                scale, core_ref, status, tuple(range(CHUNKS)), sent, loglik_as="row"
            )
    mean_loglik = sum_small(loglik) / total_people
    return (moved, log_weights[0], mean_loglik[0])


def solution(mesh):
    placed = (P("row", "col"), P("row"), P(None, "col"), P(None, None, "col"), P(), P(), P(), P())
    return jax.shard_map(
        local, mesh=mesh, in_specs=placed, out_specs=(P(None, "col"), P(), P()), check_vma=False
    )
```

time: 380 us -> 146 us (0.38)
  waiting for transfers between devices: 247 us -> 68.8 us
  matrix products: 49.9 us -> 0 us
  Pallas kernels: 0 us -> 37.3 us
  starting transfers between devices: 0.21 us -> 34.7 us
  blocking collectives: 34.1 us -> 0 us
  other arithmetic: 23.5 us -> 0.58 us
  between operations: 17.1 us -> 2.79 us
  local copies, waits for them, and re-layouts: 7.04 us -> 1.61 us
    psum x5 -> x0, waiting for transfers between devices: 247 us -> none  [the longest x3 166 us: logits_of(): return lax.psum(partial_sum, 'col') * reciprocal_square]
    ppermute x0 -> x31, waiting for transfers between devices: none -> 68.8 us  [swap(): return lax.ppermute(value, axis, [(i, i ^ distance) for i in range(size)])]
    dot_general x5 -> x0, matrix products: 49.9 us -> none  [the longest x3 30.2 us: contract_cols(): lax.dot_general(left, right, (((1,), (1,)), ((), ())), preferred_element_...]
    pallas_call x0 -> x16, Pallas kernels: none -> 37.3 us  [the longest x2 14.7 us: update_and_logits(): pl.pallas_call(functools.partial(update_kernel, first, move, total_varian...]
    ppermute x0 -> x31, starting transfers between devices: none -> 34.7 us  [swap(): return lax.ppermute(value, axis, [(i, i ^ distance) for i in range(size)])]
    psum x3 -> x0, blocking collectives: 34.1 us -> none  [the longest x2 19.7 us: loglik_of(): return lax.psum(shard_partial_total, 'row')]
    convert_element_type x2, other arithmetic: 12.5 us -> 0.04 us  [over_chips(): mine = (mine + swap(other, 'col', 1)).astype(link)]
    unnamed x12 -> x10, local copies, waits for them, and re-layouts: 7.04 us -> 1.61 us
  transfers between devices with their start and end apart: 5 -> 31, of which waited for: 5 -> 24; matrix products, arithmetic and copies ran while one was open for 1% -> 0% of each run, Pallas kernels for 0% -> 8%
where the time goes in v1:
time: 146 us
  waiting for transfers between devices  68.8 us (47%)
  Pallas kernels  37.3 us (26%)
  starting transfers between devices  34.7 us (24%)
  between operations  2.79 us (2%)
  local copies, waits for them, and re-layouts  1.61 us (1%)
    ppermute x31, waiting for transfers between devices, swap(): return lax.ppermute(value, axis, [(i, i ^ distance) for i in range(size)])  68.8 us
    ppermute x31, starting transfers between devices, swap(): return lax.ppermute(value, axis, [(i, i ^ distance) for i in range(size)])  34.7 us
    pallas_call x2, Pallas kernels, update_and_logits(): pl.pallas_call(functools.partial(update_kernel, first, move, total_varian...  14.7 us
    pallas_call x2, Pallas kernels, center_and_first_logits(): pl.pallas_call(functools.partial(center_kernel, block, with_gram), grid=(...  14.4 us
    pallas_call x4, Pallas kernels, gradient(): pl.pallas_call(functools.partial(gradient_kernel, len(pairs) // 2, first,...  6.38 us
  transfers between devices with their start and end apart: 31, of which 24 were waited for; matrix products, arithmetic and copies ran while one was open for 0% of the time, Pallas kernels for 8%

profile of v1, /device:TPU:0, one launch (start us, length us, event | category | flops | bytes accessed | tf_op | source)
XLA Modules:
  0.0 145.9 jit_solution(11634785064866753515)
XLA Ops:
  0.7 1.6 %copy-done = f32[64,8192]{1,0:T(8,128)S(1)} copy-done((f32[64,8192]{1,0:T(8,128)S(1)}, f32[64,8192]{1,0:T(8,128)}, u32[]{:S(2)}) %copy-start) | copy-done | bytes 2097176
  2.2 7.2 %center_and_first_logits.2 = (bf16[512,8192]{1,0:T(8,128)(2,1)S(1)}, f32[64,384]{1,0:T(8,128)S(1)}, f32[64,384]{1,0:T(8,128)S(1)}) custom-call(s32[1]{0:T(128)} %bitcast.core, s32[1024,8192]{1,0:T(8,128)} %doses.3, f32[64,8192]{1,0:T(8,128)S(1)} %copy-done), custom_call_target="tpu_custom_call" | custom-call | flops 4294967296 | tf_op jit(solution)/shard_map/center_and_first_logits/pallas_call | solution.py:121
  10.9 5.0 %collective-permute-start.3 = (f32[64,384]{1,0:T(8,128)S(1)}, f32[64,384]{1,0:T(8,128)S(1)}, u32[]{:S(2)}, u32[]{:S(2)}) collective-permute-start(f32[64,384]{1,0:T(8,128)S(1)} %add.29.refs_0_), channel_id=1, source_target_pairs={{0,6},{1,7},{2,4},{3,5},{4,2},{5,3},{6,0},{7,1},{8,14},{9,15},{10,... | collective-permute-start | bytes 294920 | tf_op jit(solution)/shard_map/ppermute | solution.py:379
  15.9 7.2 %center_and_first_logits.3 = (bf16[512,8192]{1,0:T(8,128)(2,1)S(1)}, f32[64,256]{1,0:T(8,128)S(1)}, f32[64,256]{1,0:T(8,128)S(1)}) custom-call(s32[1]{0:T(128)} %bitcast.core, s32[1024,8192]{1,0:T(8,128)} %doses.3, f32[64,8192]{1,0:T(8,128)S(1)} %copy-done), custom_call_target="tpu_custom_call" | custom-call | flops 4294967296 | tf_op jit(solution)/shard_map/center_and_first_logits/pallas_call | solution.py:121
  24.5 3.3 %collective-permute-start.8 = (f32[64,256]{1,0:T(8,128)S(1)}, f32[64,256]{1,0:T(8,128)S(1)}, u32[]{:S(2)}, u32[]{:S(2)}) collective-permute-start(f32[64,256]{1,0:T(8,128)S(1)} %add.30.refs_0_), channel_id=1, source_target_pairs={{0,6},{1,7},{2,4},{3,5},{4,2},{5,3},{6,0},{7,1},{8,14},{9,15},{10,... | collective-permute-start | bytes 196616 | tf_op jit(solution)/shard_map/ppermute | solution.py:379
  28.9 2.4 %collective-permute-done.2.refs_2_ = f32[64,384]{1,0:T(8,128)S(1)} collective-permute-done((f32[64,384]{1,0:T(8,128)S(1)}, f32[64,384]{1,0:T(8,128)S(1)}, u32[]{:S(2)}, u32[]{:S(2)}) %collective-permute-start.2) | collective-permute-done | bytes 98336 | tf_op jit(solution)/shard_map/ppermute | solution.py:379
  31.4 1.3 collective-permute-done.8.refs_3_
  32.7 3.4 %collective-permute-done.7.refs_2_ = f32[64,256]{1,0:T(8,128)S(1)} collective-permute-done((f32[64,256]{1,0:T(8,128)S(1)}, f32[64,256]{1,0:T(8,128)S(1)}, u32[]{:S(2)}, u32[]{:S(2)}) %collective-permute-start.7) | collective-permute-done | bytes 65568 | tf_op jit(solution)/shard_map/ppermute | solution.py:379
  37.8 1.6 %gradient.4.left = bf16[64,4224]{1,0:T(8,128)(2,1)S(1)} custom-call(s32[1]{0:T(128)} %bitcast.core, bf16[64,256]{1,0:T(8,128)(2,1)S(1)} %get-tuple-element.26.refs_0_, bf16[64,256]{1,0:T(8,128)(2,1)S(1)} %collective-permute-done.4.refs_1_, bf16[64,384]{1,0:T(8,128)(2,1)S(1)} %residual.5.refs_2_, bf16[64,384]{1,0:T(8,128)(2,1)S(1)} %collective-permute-done.9.refs_3_, ...), custom_call_target="tpu_custom_call" | custom-call | flops 2147483648 | tf_op jit(solution)/shard_map/gradient/pallas_call | solution.py:226
  39.4 1.6 %collective-permute-start.10 = (bf16[64,4224]{1,0:T(8,128)(2,1)S(1)}, bf16[64,4224]{1,0:T(8,128)(2,1)S(1)}, u32[]{:S(2)}, u32[]{:S(2)}) collective-permute-start(bf16[64,4224]{1,0:T(8,128)(2,1)S(1)} %gradient.4.left), channel_id=1, source_target_pairs={{0,8},{8,0},{16,24},{24,16},{1,9},{9,1},{17,25},{25,17},{2,10},{10... | collective-permute-start | bytes 1622024 | tf_op jit(solution)/shard_map/ppermute | solution.py:379
  40.9 1.6 %gradient.5.left = bf16[64,4096]{1,0:T(8,128)(2,1)S(1)} custom-call(s32[1]{0:T(128)} %bitcast.core, bf16[64,256]{1,0:T(8,128)(2,1)S(1)} %get-tuple-element.26.refs_0_, bf16[64,256]{1,0:T(8,128)(2,1)S(1)} %collective-permute-done.4.refs_1_, bf16[64,384]{1,0:T(8,128)(2,1)S(1)} %residual.5.refs_2_, bf16[64,384]{1,0:T(8,128)(2,1)S(1)} %collective-permute-done.9.refs_3_, ...), custom_call_target="tpu_custom_call" | custom-call | flops 2147483648 | tf_op jit(solution)/shard_map/gradient/pallas_call | solution.py:226
  42.5 1.6 %collective-permute-start.12 = (bf16[64,4096]{1,0:T(8,128)(2,1)S(1)}, bf16[64,4096]{1,0:T(8,128)(2,1)S(1)}, u32[]{:S(2)}, u32[]{:S(2)}) collective-permute-start(bf16[64,4096]{1,0:T(8,128)(2,1)S(1)} %gradient.5.left), channel_id=1, source_target_pairs={{0,16},{8,24},{16,0},{24,8},{1,17},{9,25},{17,1},{25,9},{2,18},{10... | collective-permute-start | bytes 1572872 | tf_op jit(solution)/shard_map/ppermute | solution.py:379
  44.1 9.8 %collective-permute-done.10.right = bf16[64,4224]{1,0:T(8,128)(2,1)S(1)} collective-permute-done((bf16[64,4224]{1,0:T(8,128)(2,1)S(1)}, bf16[64,4224]{1,0:T(8,128)(2,1)S(1)}, u32[]{:S(2)}, u32[]{:S(2)}) %collective-permute-start.10) | collective-permute-done | bytes 540704 | tf_op jit(solution)/shard_map/ppermute | solution.py:379
  54.3 1.6 %collective-permute-start.11 = (bf16[64,4224]{1,0:T(8,128)(2,1)S(1)}, bf16[64,4224]{1,0:T(8,128)(2,1)S(1)}, u32[]{:S(2)}, u32[]{:S(2)}) collective-permute-start(bf16[64,4224]{1,0:T(8,128)(2,1)S(1)} %pair_sum.4.refs_3_), channel_id=1, source_target_pairs={{0,16},{8,24},{16,0},{24,8},{1,17},{9,25},{17,1},{25,9},{2,18},{10... | collective-permute-start | bytes 1622024 | tf_op jit(solution)/shard_map/ppermute | solution.py:379
  59.5 10.2 %collective-permute-done.13.refs_6_ = bf16[64,4096]{1,0:T(8,128)(2,1)S(1)} collective-permute-done((bf16[64,4096]{1,0:T(8,128)(2,1)S(1)}, bf16[64,4096]{1,0:T(8,128)(2,1)S(1)}, u32[]{:S(2)}, u32[]{:S(2)}) %collective-permute-start.13) | collective-permute-done | bytes 524320 | tf_op jit(solution)/shard_map/ppermute | solution.py:379
  69.8 8.5 %update_and_logits.2 = (f32[64,8192]{1,0:T(8,128)S(1)}, f32[64,512]{1,0:T(8,128)S(1)}, f32[64,512]{1,0:T(8,128)S(1)}, f32[1,64]{1,0:T(1,128)}, f32[1,8192]{1,0:T(1,128)S(1)}) custom-call(s32[1]{0:T(128)} %bitcast.core, f32[1]{0:T(128)S(6)} %copy.11.old_heat, f32[1]{0:T(128)S(6)} %copy.12.advance, f32[1]{0:T(128)S(6)} %copy.13.drift_ref, ...), custom_call_target="tpu_custom_call" | custom-call | flops 4294967296 | tf_op jit(solution)/shard_map/update_and_logits/pallas_call | solution.py:359
  78.3 1.3 collective-permute-done.14
  80.9 3.2 %collective-permute-start.15 = (bf16[64,512]{1,0:T(8,128)(2,1)S(1)}, bf16[64,512]{1,0:T(8,128)(2,1)S(1)}, u32[]{:S(2)}, u32[]{:S(2)}) collective-permute-start(bf16[64,512]{1,0:T(8,128)(2,1)S(1)} %add_convert_fusion.1.refs_0_), channel_id=1, source_target_pairs={{0,2},{1,3},{2,0},{3,1},{4,6},{5,7},{6,4},{7,5},{8,10},{9,11},{10,... | collective-permute-start | bytes 196616 | tf_op jit(solution)/shard_map/ppermute | solution.py:379
  84.1 2.4 %collective-permute-done.17.refs_3_ = bf16[64,512]{1,0:T(8,128)(2,1)S(1)} collective-permute-done((bf16[64,512]{1,0:T(8,128)(2,1)S(1)}, bf16[64,512]{1,0:T(8,128)(2,1)S(1)}, u32[]{:S(2)}, u32[]{:S(2)}) %collective-permute-start.17) | collective-permute-done | bytes 65568 | tf_op jit(solution)/shard_map/ppermute | solution.py:379
  86.5 2.0 %collective-permute-done.16.refs_2_ = bf16[64,512]{1,0:T(8,128)(2,1)S(1)} collective-permute-done((bf16[64,512]{1,0:T(8,128)(2,1)S(1)}, bf16[64,512]{1,0:T(8,128)(2,1)S(1)}, u32[]{:S(2)}, u32[]{:S(2)}) %collective-permute-start.16) | collective-permute-done | bytes 65568 | tf_op jit(solution)/shard_map/ppermute | solution.py:379
  89.9 1.6 %gradient.6.left = bf16[64,4096]{1,0:T(8,128)(2,1)S(1)} custom-call(s32[1]{0:T(128)} %bitcast.core, bf16[64,512]{1,0:T(8,128)(2,1)S(1)} %residual.6.refs_0_, bf16[64,512]{1,0:T(8,128)(2,1)S(1)} %collective-permute-done.18.refs_1_, bf16[512,8192]{1,0:T(8,128)(2,1)S(1)} %get-tuple-element.24.refs_4_.refs_1_.refs_2_, ...), custom_call_target="tpu_custom_call" | custom-call | flops 2147483648 | tf_op jit(solution)/shard_map/gradient/pallas_call | solution.py:226
  92.5 1.6 %gradient.7.left = bf16[64,4096]{1,0:T(8,128)(2,1)S(1)} custom-call(s32[1]{0:T(128)} %bitcast.core, bf16[64,512]{1,0:T(8,128)(2,1)S(1)} %residual.6.refs_0_, bf16[64,512]{1,0:T(8,128)(2,1)S(1)} %collective-permute-done.18.refs_1_, bf16[512,8192]{1,0:T(8,128)(2,1)S(1)} %get-tuple-element.24.refs_4_.refs_1_.refs_2_, ...), custom_call_target="tpu_custom_call" | custom-call | flops 2147483648 | tf_op jit(solution)/shard_map/gradient/pallas_call | solution.py:226
  95.3 10.3 %collective-permute-done.19.right = bf16[64,4096]{1,0:T(8,128)(2,1)S(1)} collective-permute-done((bf16[64,4096]{1,0:T(8,128)(2,1)S(1)}, bf16[64,4096]{1,0:T(8,128)(2,1)S(1)}, u32[]{:S(2)}, u32[]{:S(2)}) %collective-permute-start.19) | collective-permute-done | bytes 524320 | tf_op jit(solution)/shard_map/ppermute | solution.py:379
  105.7 1.6 %collective-permute-start.20 = (bf16[64,4096]{1,0:T(8,128)(2,1)S(1)}, bf16[64,4096]{1,0:T(8,128)(2,1)S(1)}, u32[]{:S(2)}, u32[]{:S(2)}) collective-permute-start(bf16[64,4096]{1,0:T(8,128)(2,1)S(1)} %pair_sum.6.refs_3_), channel_id=1, source_target_pairs={{0,16},{8,24},{16,0},{24,8},{1,17},{9,25},{17,1},{25,9},{2,18},{10... | collective-permute-start | bytes 1572872 | tf_op jit(solution)/shard_map/ppermute | solution.py:379
  109.4 9.7 %collective-permute-done.20.refs_4_ = bf16[64,4096]{1,0:T(8,128)(2,1)S(1)} collective-permute-done((bf16[64,4096]{1,0:T(8,128)(2,1)S(1)}, bf16[64,4096]{1,0:T(8,128)(2,1)S(1)}, u32[]{:S(2)}, u32[]{:S(2)}) %collective-permute-start.20) | collective-permute-done | bytes 524320 | tf_op jit(solution)/shard_map/ppermute | solution.py:379
  119.1 1.8 %collective-permute-done.22.refs_6_ = bf16[64,4096]{1,0:T(8,128)(2,1)S(1)} collective-permute-done((bf16[64,4096]{1,0:T(8,128)(2,1)S(1)}, bf16[64,4096]{1,0:T(8,128)(2,1)S(1)}, u32[]{:S(2)}, u32[]{:S(2)}) %collective-permute-start.22) | collective-permute-done | bytes 524320 | tf_op jit(solution)/shard_map/ppermute | solution.py:379
  120.9 6.2 %update_and_logits.3 = (f32[64,8192]{1,0:T(8,128)}, f32[64,512]{1,0:T(8,128)S(1)}, f32[64,512]{1,0:T(8,128)S(1)}) custom-call(s32[1]{0:T(128)} %bitcast.core, f32[1]{0:T(128)S(6)} %copy.11.old_heat, f32[1]{0:T(128)S(6)} %copy.12.advance, f32[1]{0:T(128)S(6)} %copy.13.drift_ref, s32[2,64]{1,0:T(2,128)S(1)} %copy-done.4, ...), custom_call_target="tpu_custom_call" | custom-call | flops 4294967296 | tf_op jit(solution)/shard_map/update_and_logits/pallas_call | solution.py:359
  127.2 1.3 collective-permute-done.23
  130.0 3.0 %collective-permute-start.24 = (bf16[64,512]{1,0:T(8,128)(2,1)S(1)}, bf16[64,512]{1,0:T(8,128)(2,1)S(1)}, u32[]{:S(2)}, u32[]{:S(2)}) collective-permute-start(bf16[64,512]{1,0:T(8,128)(2,1)S(1)} %add_convert_fusion.refs_0_), channel_id=1, source_target_pairs={{0,2},{1,3},{2,0},{3,1},{4,6},{5,7},{6,4},{7,5},{8,10},{9,11},{10,... | collective-permute-start | bytes 196616 | tf_op jit(solution)/shard_map/ppermute | solution.py:379
  133.0 2.4 %collective-permute-done.26.refs_3_ = bf16[64,512]{1,0:T(8,128)(2,1)S(1)} collective-permute-done((bf16[64,512]{1,0:T(8,128)(2,1)S(1)}, bf16[64,512]{1,0:T(8,128)(2,1)S(1)}, u32[]{:S(2)}, u32[]{:S(2)}) %collective-permute-start.26) | collective-permute-done | bytes 65568 | tf_op jit(solution)/shard_map/ppermute | solution.py:379
  135.4 2.0 %collective-permute-done.25.refs_2_ = bf16[64,512]{1,0:T(8,128)(2,1)S(1)} collective-permute-done((bf16[64,512]{1,0:T(8,128)(2,1)S(1)}, bf16[64,512]{1,0:T(8,128)(2,1)S(1)}, u32[]{:S(2)}, u32[]{:S(2)}) %collective-permute-start.25) | collective-permute-done | bytes 65568 | tf_op jit(solution)/shard_map/ppermute | solution.py:379
  139.3 2.0 %collective-permute-start.30 = (f32[1,64]{1,0:T(1,128)S(1)}, f32[1,64]{1,0:T(1,128)S(1)}, u32[]{:S(2)}, u32[]{:S(2)}) collective-permute-start(f32[1,64]{1,0:T(1,128)S(1)} %add.33), channel_id=1, source_target_pairs={{0,24},{8,16},{16,8},{24,0},{1,25},{9,17},{17,9},{25,1},{2,26},{10... | collective-permute-start | bytes 776 | tf_op jit(solution)/shard_map/ppermute | solution.py:379
  (62 shorter events, 23.0 us)
Async XLA Ops:
  9.4 1.5 %collective-permute-start = (f32[64,384]{1,0:T(8,128)S(1)}, f32[64,384]{1,0:T(8,128)S(1)}, u32[]{:S(2)}, u32[]{:S(2)}) collective-permute-start(f32[64,384]{1,0:T(8,128)S(1)} %get-tuple-element.22), channel_id=1, source_target_pairs={{0,1},{1,0},{2,3},{3,2},{4,5},{5,4},{6,7},{7,6},{8,9},{9,8},{10,11... | collective-permute-start | bytes 294920 | tf_op jit(solution)/shard_map/ppermute | solution.py:379
  10.9 16.8 %collective-permute-start.3 = (f32[64,384]{1,0:T(8,128)S(1)}, f32[64,384]{1,0:T(8,128)S(1)}, u32[]{:S(2)}, u32[]{:S(2)}) collective-permute-start(f32[64,384]{1,0:T(8,128)S(1)} %add.29.refs_0_), channel_id=1, source_target_pairs={{0,6},{1,7},{2,4},{3,5},{4,2},{5,3},{6,0},{7,1},{8,14},{9,15},{10,... | collective-permute-start | bytes 294920 | tf_op jit(solution)/shard_map/ppermute | solution.py:379
  23.1 1.3 collective-permute-start.5
  23.2 8.1 %collective-permute-start.2 = (f32[64,384]{1,0:T(8,128)S(1)}, f32[64,384]{1,0:T(8,128)S(1)}, u32[]{:S(2)}, u32[]{:S(2)}) collective-permute-start(f32[64,384]{1,0:T(8,128)S(1)} %add.29.refs_0_), channel_id=1, source_target_pairs={{0,4},{1,5},{2,6},{3,7},{4,0},{5,1},{6,2},{7,3},{8,12},{9,13},{10,... | collective-permute-start | bytes 294920 | tf_op jit(solution)/shard_map/ppermute | solution.py:379
  23.3 8.0 %collective-permute-start.1 = (f32[64,384]{1,0:T(8,128)S(1)}, f32[64,384]{1,0:T(8,128)S(1)}, u32[]{:S(2)}, u32[]{:S(2)}) collective-permute-start(f32[64,384]{1,0:T(8,128)S(1)} %add.29.refs_0_), channel_id=1, source_target_pairs={{0,2},{1,3},{2,0},{3,1},{4,6},{5,7},{6,4},{7,5},{8,10},{9,11},{10,... | collective-permute-start | bytes 294920 | tf_op jit(solution)/shard_map/ppermute | solution.py:379
  24.5 8.3 %collective-permute-start.8 = (f32[64,256]{1,0:T(8,128)S(1)}, f32[64,256]{1,0:T(8,128)S(1)}, u32[]{:S(2)}, u32[]{:S(2)}) collective-permute-start(f32[64,256]{1,0:T(8,128)S(1)} %add.30.refs_0_), channel_id=1, source_target_pairs={{0,6},{1,7},{2,4},{3,5},{4,2},{5,3},{6,0},{7,1},{8,14},{9,15},{10,... | collective-permute-start | bytes 196616 | tf_op jit(solution)/shard_map/ppermute | solution.py:379
  27.7 8.3 %collective-permute-start.7 = (f32[64,256]{1,0:T(8,128)S(1)}, f32[64,256]{1,0:T(8,128)S(1)}, u32[]{:S(2)}, u32[]{:S(2)}) collective-permute-start(f32[64,256]{1,0:T(8,128)S(1)} %add.30.refs_0_), channel_id=1, source_target_pairs={{0,4},{1,5},{2,6},{3,7},{4,0},{5,1},{6,2},{7,3},{8,12},{9,13},{10,... | collective-permute-start | bytes 196616 | tf_op jit(solution)/shard_map/ppermute | solution.py:379
  27.7 8.3 %collective-permute-start.6 = (f32[64,256]{1,0:T(8,128)S(1)}, f32[64,256]{1,0:T(8,128)S(1)}, u32[]{:S(2)}, u32[]{:S(2)}) collective-permute-start(f32[64,256]{1,0:T(8,128)S(1)} %add.30.refs_0_), channel_id=1, source_target_pairs={{0,2},{1,3},{2,0},{3,1},{4,6},{5,7},{6,4},{7,5},{8,10},{9,11},{10,... | collective-permute-start | bytes 196616 | tf_op jit(solution)/shard_map/ppermute | solution.py:379
  36.3 1.4 collective-permute-start.9
  36.5 1.3 collective-permute-start.4
  39.4 30.4 %copy-start.4 = (s32[2,64]{1,0:T(2,128)S(1)}, s32[2,64]{1,0:T(2,128)}, u32[]{:S(2)}) copy-start(s32[2,64]{1,0:T(2,128)} %flags.3) | copy-start | bytes 1540
  39.4 14.6 %collective-permute-start.10 = (bf16[64,4224]{1,0:T(8,128)(2,1)S(1)}, bf16[64,4224]{1,0:T(8,128)(2,1)S(1)}, u32[]{:S(2)}, u32[]{:S(2)}) collective-permute-start(bf16[64,4224]{1,0:T(8,128)(2,1)S(1)} %gradient.4.left), channel_id=1, source_target_pairs={{0,8},{8,0},{16,24},{24,16},{1,9},{9,1},{17,25},{25,17},{2,10},{10... | collective-permute-start | bytes 1622024 | tf_op jit(solution)/shard_map/ppermute | solution.py:379
  42.5 14.0 %collective-permute-start.12 = (bf16[64,4096]{1,0:T(8,128)(2,1)S(1)}, bf16[64,4096]{1,0:T(8,128)(2,1)S(1)}, u32[]{:S(2)}, u32[]{:S(2)}) collective-permute-start(bf16[64,4096]{1,0:T(8,128)(2,1)S(1)} %gradient.5.left), channel_id=1, source_target_pairs={{0,16},{8,24},{16,0},{24,8},{1,17},{9,25},{17,1},{25,9},{2,18},{10... | collective-permute-start | bytes 1572872 | tf_op jit(solution)/shard_map/ppermute | solution.py:379
  54.3 15.4 %collective-permute-start.11 = (bf16[64,4224]{1,0:T(8,128)(2,1)S(1)}, bf16[64,4224]{1,0:T(8,128)(2,1)S(1)}, u32[]{:S(2)}, u32[]{:S(2)}) collective-permute-start(bf16[64,4224]{1,0:T(8,128)(2,1)S(1)} %pair_sum.4.refs_3_), channel_id=1, source_target_pairs={{0,16},{8,24},{16,0},{24,8},{1,17},{9,25},{17,1},{25,9},{2,18},{10... | collective-permute-start | bytes 1622024 | tf_op jit(solution)/shard_map/ppermute | solution.py:379
  56.6 13.1 %collective-permute-start.13 = (bf16[64,4096]{1,0:T(8,128)(2,1)S(1)}, bf16[64,4096]{1,0:T(8,128)(2,1)S(1)}, u32[]{:S(2)}, u32[]{:S(2)}) collective-permute-start(bf16[64,4096]{1,0:T(8,128)(2,1)S(1)} %pair_sum.5.refs_5_), channel_id=1, source_target_pairs={{0,8},{8,0},{16,24},{24,16},{1,9},{9,1},{17,25},{25,17},{2,10},{10... | collective-permute-start | bytes 1572872 | tf_op jit(solution)/shard_map/ppermute | solution.py:379
  78.2 1.4 collective-permute-start.14
  79.7 6.9 %collective-permute-start.17 = (bf16[64,512]{1,0:T(8,128)(2,1)S(1)}, bf16[64,512]{1,0:T(8,128)(2,1)S(1)}, u32[]{:S(2)}, u32[]{:S(2)}) collective-permute-start(bf16[64,512]{1,0:T(8,128)(2,1)S(1)} %add_convert_fusion.1.refs_0_), channel_id=1, source_target_pairs={{0,6},{1,7},{2,4},{3,5},{4,2},{5,3},{6,0},{7,1},{8,14},{9,15},{10,... | collective-permute-start | bytes 196616 | tf_op jit(solution)/shard_map/ppermute | solution.py:379
  80.9 7.6 %collective-permute-start.16 = (bf16[64,512]{1,0:T(8,128)(2,1)S(1)}, bf16[64,512]{1,0:T(8,128)(2,1)S(1)}, u32[]{:S(2)}, u32[]{:S(2)}) collective-permute-start(bf16[64,512]{1,0:T(8,128)(2,1)S(1)} %add_convert_fusion.1.refs_0_), channel_id=1, source_target_pairs={{0,4},{1,5},{2,6},{3,7},{4,0},{5,1},{6,2},{7,3},{8,12},{9,13},{10,... | collective-permute-start | bytes 196616 | tf_op jit(solution)/shard_map/ppermute | solution.py:379
  80.9 7.6 %collective-permute-start.15 = (bf16[64,512]{1,0:T(8,128)(2,1)S(1)}, bf16[64,512]{1,0:T(8,128)(2,1)S(1)}, u32[]{:S(2)}, u32[]{:S(2)}) collective-permute-start(bf16[64,512]{1,0:T(8,128)(2,1)S(1)} %add_convert_fusion.1.refs_0_), channel_id=1, source_target_pairs={{0,2},{1,3},{2,0},{3,1},{4,6},{5,7},{6,4},{7,5},{8,10},{9,11},{10,... | collective-permute-start | bytes 196616 | tf_op jit(solution)/shard_map/ppermute | solution.py:379
  88.6 1.3 collective-permute-start.18
  91.5 14.1 %collective-permute-start.19 = (bf16[64,4096]{1,0:T(8,128)(2,1)S(1)}, bf16[64,4096]{1,0:T(8,128)(2,1)S(1)}, u32[]{:S(2)}, u32[]{:S(2)}) collective-permute-start(bf16[64,4096]{1,0:T(8,128)(2,1)S(1)} %gradient.6.left), channel_id=1, source_target_pairs={{0,8},{8,0},{16,24},{24,16},{1,9},{9,1},{17,25},{25,17},{2,10},{10... | collective-permute-start | bytes 1572872 | tf_op jit(solution)/shard_map/ppermute | solution.py:379
  94.1 13.9 %collective-permute-start.21 = (bf16[64,4096]{1,0:T(8,128)(2,1)S(1)}, bf16[64,4096]{1,0:T(8,128)(2,1)S(1)}, u32[]{:S(2)}, u32[]{:S(2)}) collective-permute-start(bf16[64,4096]{1,0:T(8,128)(2,1)S(1)} %gradient.7.left), channel_id=1, source_target_pairs={{0,16},{8,24},{16,0},{24,8},{1,17},{9,25},{17,1},{25,9},{2,18},{10... | collective-permute-start | bytes 1572872 | tf_op jit(solution)/shard_map/ppermute | solution.py:379
  105.7 13.4 %collective-permute-start.20 = (bf16[64,4096]{1,0:T(8,128)(2,1)S(1)}, bf16[64,4096]{1,0:T(8,128)(2,1)S(1)}, u32[]{:S(2)}, u32[]{:S(2)}) collective-permute-start(bf16[64,4096]{1,0:T(8,128)(2,1)S(1)} %pair_sum.6.refs_3_), channel_id=1, source_target_pairs={{0,16},{8,24},{16,0},{24,8},{1,17},{9,25},{17,1},{25,9},{2,18},{10... | collective-permute-start | bytes 1572872 | tf_op jit(solution)/shard_map/ppermute | solution.py:379
  108.1 12.8 %collective-permute-start.22 = (bf16[64,4096]{1,0:T(8,128)(2,1)S(1)}, bf16[64,4096]{1,0:T(8,128)(2,1)S(1)}, u32[]{:S(2)}, u32[]{:S(2)}) collective-permute-start(bf16[64,4096]{1,0:T(8,128)(2,1)S(1)} %pair_sum.7.refs_5_), channel_id=1, source_target_pairs={{0,8},{8,0},{16,24},{24,16},{1,9},{9,1},{17,25},{25,17},{2,10},{10... | collective-permute-start | bytes 1572872 | tf_op jit(solution)/shard_map/ppermute | solution.py:379
  127.1 1.4 collective-permute-start.23
  128.6 6.9 %collective-permute-start.26 = (bf16[64,512]{1,0:T(8,128)(2,1)S(1)}, bf16[64,512]{1,0:T(8,128)(2,1)S(1)}, u32[]{:S(2)}, u32[]{:S(2)}) collective-permute-start(bf16[64,512]{1,0:T(8,128)(2,1)S(1)} %add_convert_fusion.refs_0_), channel_id=1, source_target_pairs={{0,6},{1,7},{2,4},{3,5},{4,2},{5,3},{6,0},{7,1},{8,14},{9,15},{10,... | collective-permute-start | bytes 196616 | tf_op jit(solution)/shard_map/ppermute | solution.py:379
  129.8 7.6 %collective-permute-start.25 = (bf16[64,512]{1,0:T(8,128)(2,1)S(1)}, bf16[64,512]{1,0:T(8,128)(2,1)S(1)}, u32[]{:S(2)}, u32[]{:S(2)}) collective-permute-start(bf16[64,512]{1,0:T(8,128)(2,1)S(1)} %add_convert_fusion.refs_0_), channel_id=1, source_target_pairs={{0,4},{1,5},{2,6},{3,7},{4,0},{5,1},{6,2},{7,3},{8,12},{9,13},{10,... | collective-permute-start | bytes 196616 | tf_op jit(solution)/shard_map/ppermute | solution.py:379
  130.0 7.4 %collective-permute-start.24 = (bf16[64,512]{1,0:T(8,128)(2,1)S(1)}, bf16[64,512]{1,0:T(8,128)(2,1)S(1)}, u32[]{:S(2)}, u32[]{:S(2)}) collective-permute-start(bf16[64,512]{1,0:T(8,128)(2,1)S(1)} %add_convert_fusion.refs_0_), channel_id=1, source_target_pairs={{0,2},{1,3},{2,0},{3,1},{4,6},{5,7},{6,4},{7,5},{8,10},{9,11},{10,... | collective-permute-start | bytes 196616 | tf_op jit(solution)/shard_map/ppermute | solution.py:379
  138.1 1.1 collective-permute-start.27
  139.3 4.4 %collective-permute-start.30 = (f32[1,64]{1,0:T(1,128)S(1)}, f32[1,64]{1,0:T(1,128)S(1)}, u32[]{:S(2)}, u32[]{:S(2)}) collective-permute-start(f32[1,64]{1,0:T(1,128)S(1)} %add.33), channel_id=1, source_target_pairs={{0,24},{8,16},{16,8},{24,0},{1,25},{9,17},{17,9},{25,1},{2,26},{10... | collective-permute-start | bytes 776 | tf_op jit(solution)/shard_map/ppermute | solution.py:379
  141.3 3.5 %collective-permute-start.29 = (f32[1,64]{1,0:T(1,128)S(1)}, f32[1,64]{1,0:T(1,128)S(1)}, u32[]{:S(2)}, u32[]{:S(2)}) collective-permute-start(f32[1,64]{1,0:T(1,128)S(1)} %add.33), channel_id=1, source_target_pairs={{0,16},{8,24},{16,0},{24,8},{1,17},{9,25},{17,1},{25,9},{2,18},{10... | collective-permute-start | bytes 776 | tf_op jit(solution)/shard_map/ppermute | solution.py:379
  141.8 3.5 %collective-permute-start.28 = (f32[1,64]{1,0:T(1,128)S(1)}, f32[1,64]{1,0:T(1,128)S(1)}, u32[]{:S(2)}, u32[]{:S(2)}) collective-permute-start(f32[1,64]{1,0:T(1,128)S(1)} %add.33), channel_id=1, source_target_pairs={{0,8},{8,0},{16,24},{24,16},{1,9},{9,1},{17,25},{25,17},{2,10},{10... | collective-permute-start | bytes 776 | tf_op jit(solution)/shard_map/ppermute | solution.py:379
  (4 other events, 78.0 us)

commit v2 on v1

v2 whole, which is shorter than its diff:
```python
import functools

import jax
import jax.numpy as jnp
from jax import lax
from jax.experimental import pallas as pl
from jax.experimental.pallas import tpu as pltpu
from jax.sharding import PartitionSpec as P

CLIP_FLOOR = 4.0
SHRINKAGE_LEVEL = 0.5
F32 = jnp.float32
BF16 = jnp.bfloat16
VMEM = pl.BlockSpec(memory_space=pltpu.VMEM)
SMEM = pl.BlockSpec(memory_space=pltpu.SMEM)
HBM = pl.BlockSpec(memory_space=pltpu.HBM)
KEEP, SEND = 0, 1
MIB = 1 << 20
LANES = 128
CHUNKS = 1
PIECES = 4


def core_of():
    return lax.rem(lax.axis_index("col"), 2)


def row_bits():
    return [1 << b for b in range(lax.axis_size("row").bit_length() - 1)]


def half_of(which, piece, variants):
    columns = variants // PIECES
    bits = row_bits()
    bit = jnp.where(lax.rem(jnp.int32(piece), 2) == 0, bits[0], bits[-1])
    own = lax.rem(lax.div(lax.axis_index("row"), bit), 2)
    chosen = own if which == KEEP else 1 - own
    return pl.multiple_of(piece * columns + chosen * (columns // 2), columns // 2)


def rows_dot(left, right):
    return lax.dot_general(left, right, (((1,), (1,)), ((), ())), preferred_element_type=F32)


def tile_of(size, most):
    while size % most:
        most //= 2
    return most


def params(mib):
    return pltpu.CompilerParams(vmem_limit_bytes=mib * MIB)


def cost(flops):
    return pl.CostEstimate(flops=flops, bytes_accessed=0, transcendentals=0)


def as_lanes(value):
    high = value.astype(BF16)
    rest = value - high.astype(F32)
    middle = rest.astype(BF16)
    low = (rest - middle.astype(F32)).astype(BF16)
    lane = lax.broadcasted_iota(jnp.int32, (value.shape[0], LANES), 1)
    zero = jnp.zeros((value.shape[0], LANES), F32)
    out = jnp.where(lane == 0, high.astype(F32), zero)
    out = jnp.where(lane == 1, middle.astype(F32), out)
    return jnp.where(lane == 2, low.astype(F32), out).astype(BF16)


def flipped(value):
    size = max(value.shape)
    diagonal = lax.broadcasted_iota(jnp.int32, (size, size), 0) == lax.broadcasted_iota(
        jnp.int32, (size, size), 1
    )
    return jnp.sum(
        jnp.where(diagonal, value, 0.0), axis=int(value.shape[0] == 1), keepdims=True
    )


def from_lanes(lanes):
    return jnp.sum(lanes.astype(F32), axis=1, keepdims=True)


def center_kernel(block, with_gram, doses, cloud, _, centered, mine, other, cloud_bf, logits, gram):
    step = pl.program_id(0)
    variants = doses.shape[1]
    people = logits.shape[1]
    half = people // 2

    @pl.when(step == 0)
    def _():
        cloud_bf[...] = cloud[...].astype(BF16)

    if with_gram:

        @pl.when(step == 0)
        def _():
            width = tile_of(variants, 1024)
            total = None
            for start in range(0, variants, width):
                c = cloud[:, start : start + width]
                c = c - jnp.mean(c, axis=0, keepdims=True)
                high = c.astype(BF16)
                low = (c - high.astype(F32)).astype(BF16)
                term = rows_dot(high, high) + 2.0 * rows_dot(high, low)
                total = term if total is None else total + term
            gram[...] = jnp.zeros(gram.shape, F32)
            gram[:, : total.shape[1]] = total

    width = tile_of(variants, 2048)
    total = None
    for start in range(0, variants, width):
        part = (doses[:, start : start + width] - 1).astype(F32).astype(BF16)
        centered[pl.ds(pl.multiple_of(step * block, block), block), start : start + width] = part
        term = rows_dot(part, cloud_bf[:, start : start + width])
        total = term if total is None else total + term
    logits[:, pl.ds(pl.multiple_of(step * block, block), block)] = total.T

    @pl.when(step == pl.num_programs(0) - 1)
    def _():
        first = core_of()
        mine[:, :half] = logits[:, pl.ds(pl.multiple_of(first * half, half), half)]
        other[:, :half] = logits[:, pl.ds(pl.multiple_of((1 - first) * half, half), half)]
        if with_gram:
            mine[:, half:] = gram[...]
            other[:, half:] = gram[...]


def center_and_first_logits(chunk, doses, cloud, scalars):
    variants = doses.shape[1]
    people = doses.shape[0] // CHUNKS
    particles = cloud.shape[0]
    block = min(256, people)
    steps = people // block
    with_gram = chunk == 0
    lanes = people // 2 + (LANES if with_gram else 0)
    exchanged = jax.ShapeDtypeStruct((particles, lanes), F32)
    return pl.pallas_call(
        functools.partial(center_kernel, block, with_gram),
        grid=(steps,),
        in_specs=[
            pl.BlockSpec((block, variants), lambda i: (chunk * steps + i, 0)),
            pl.BlockSpec((particles, variants), lambda i: (0, 0), pipeline_mode=pl.Buffered(1)),
            VMEM,
        ],
        out_specs=[VMEM, VMEM, VMEM],
        out_shape=[pltpu.VMEM((people, variants), BF16), exchanged, exchanged],
        scratch_shapes=[
            pltpu.VMEM((particles, variants), BF16),
            pltpu.VMEM((particles, people), F32),
            pltpu.VMEM((particles, LANES), F32),
        ],
        compiler_params=params(28),
        cost_estimate=cost(16 * particles * people * variants),
        name="center_and_first_logits",
    )(doses, cloud, scalars)


def residual_kernel(parts, people, chunks, scale, earlier, tail, gram, loglik_as, status, *refs):
    sent, refs = refs[:parts], list(refs[parts:])
    before = refs.pop(0) if earlier else None
    half = people // 2
    outcome = jnp.concatenate(
        [
            status[:, pl.ds(pl.multiple_of(chunk * people + core_of() * half, half), half)]
            for chunk in chunks
        ],
        axis=1,
    ).astype(F32)
    share = half * len(chunks)
    values = tree_sum([ref[...].astype(F32) for ref in sent])
    logits = values[:, :share] * scale
    residual = refs.pop(0)
    residual[:, :share] = (outcome - jax.nn.sigmoid(logits)).astype(BF16)
    if loglik_as or tail:
        softplus = jnp.maximum(logits, 0.0) + jnp.log1p(jnp.exp(-jnp.abs(logits)))
        loglik = jnp.sum(outcome * logits - softplus, axis=1, keepdims=True)
        if earlier:
            loglik = loglik + before[...]
        if tail:
            residual[:, share:] = as_lanes(loglik)
        if loglik_as:
            refs.pop(0)[...] = loglik if loglik_as == "column" else flipped(loglik)
    if gram:
        refs.pop(0)[...] = values[:, share:]


def residual_of(scale, status, chunks, sent, earlier=None, tail=False, gram=False, loglik_as=None):
    particles = sent[0].shape[0]
    people = status.shape[1] // CHUNKS
    share = people // 2 * len(chunks)
    out_shape = [jax.ShapeDtypeStruct((particles, share + (LANES if tail else 0)), BF16)]
    if loglik_as:
        shape = (particles, 1) if loglik_as == "column" else (1, particles)
        out_shape.append(jax.ShapeDtypeStruct(shape, F32))
    if gram:
        out_shape.append(jax.ShapeDtypeStruct((particles, LANES), F32))
    operands = [status, *sent] + ([earlier] if earlier is not None else [])
    return pl.pallas_call(
        functools.partial(
            residual_kernel, len(sent), people, chunks, scale, earlier is not None, tail, gram, loglik_as
        ),
        in_specs=[VMEM] * len(operands),
        out_specs=[VMEM] * len(out_shape),
        out_shape=out_shape,
        compiler_params=params(12),
        name="residual",
    )(*operands)


def gradient_kernel(count, which, piece, tail, *refs):
    pairs, centered = refs[: 2 * count], refs[2 * count : 2 * count + CHUNKS]
    grad, residual = refs[2 * count + CHUNKS :]
    people, variants = centered[0].shape
    half = people // 2
    mine = core_of()
    for chunk in range(CHUNKS):
        own, other = (pairs[2 * chunk], pairs[2 * chunk + 1]) if count == CHUNKS else pairs
        at = 0 if count == CHUNKS else chunk * half
        base = chunk * people
        residual[:, pl.ds(pl.multiple_of(base + mine * half, half), half)] = own[:, at : at + half]
        residual[:, pl.ds(pl.multiple_of(base + (1 - mine) * half, half), half)] = other[
            :, at : at + half
        ]
    columns = variants // 2 // PIECES
    width = tile_of(columns, 512)
    first = half_of(which, piece, variants)
    for start in range(0, columns, width):
        grad[:, start : start + width] = sum(
            jnp.dot(
                residual[:, chunk * people : (chunk + 1) * people],
                centered[chunk][:, pl.ds(pl.multiple_of(first + start, width), width)],
                preferred_element_type=F32,
            )
            for chunk in range(CHUNKS)
        ).astype(BF16)
    if tail:
        grad[:, columns:] = as_lanes(from_lanes(own[:, half:]) + from_lanes(other[:, half:]))


def gradient(which, piece, pairs, centered, tail):
    particles = pairs[0].shape[0]
    people = sum(c.shape[0] for c in centered)
    columns = centered[0].shape[1] // 2 // PIECES
    return pl.pallas_call(
        functools.partial(gradient_kernel, len(pairs) // 2, which, piece, tail),
        in_specs=[VMEM] * (len(pairs) + CHUNKS),
        out_specs=VMEM,
        out_shape=jax.ShapeDtypeStruct((particles, columns + (LANES if tail else 0)), BF16),
        scratch_shapes=[pltpu.VMEM((particles, people), BF16)],
        compiler_params=params(8),
        cost_estimate=cost(8 * particles * people * columns),
        name="gradient",
    )(*pairs, *centered)


def pair_sum_kernel(columns, tail, left, right, out):
    total = left[:, :columns].astype(F32) + right[:, :columns].astype(F32)
    out[:, :columns] = total.astype(BF16)
    if tail:
        out[:, columns:] = as_lanes(from_lanes(left[:, columns:]) + from_lanes(right[:, columns:]))


def pair_sum(columns, tail, left, right):
    return pl.pallas_call(
        functools.partial(pair_sum_kernel, columns, tail),
        in_specs=[VMEM, VMEM],
        out_specs=VMEM,
        out_shape=jax.ShapeDtypeStruct((left.shape[0], columns + (LANES if tail else 0)), BF16),
        compiler_params=params(8),
        name="pair_sum",
    )(left, right)


def weigh(total_variants, heat_advance, loglik, gram):
    scaled = heat_advance * loglik
    clipped = jnp.maximum(scaled - jnp.max(scaled, axis=0, keepdims=True), -CLIP_FLOOR)
    log_weights = clipped - jnp.log(jnp.sum(jnp.exp(clipped), axis=0, keepdims=True))
    weights = jnp.exp(log_weights)
    particles = loglik.shape[0]
    gram = gram[:, :particles]
    diagonal = lax.broadcasted_iota(jnp.int32, gram.shape, 0) == lax.broadcasted_iota(
        jnp.int32, gram.shape, 1
    )
    square = jnp.sum(jnp.where(diagonal, gram * weights, 0.0), axis=0, keepdims=True)
    mixed = jnp.sum(weights * gram, axis=0, keepdims=True) * flipped(weights)
    total = jnp.sum(square - mixed, axis=1, keepdims=True)
    return log_weights, weights, total / total_variants + 1e-06


def update_kernel(which, move, total_variants, scalars, flags, noise, *refs):
    refs = list(refs)
    centered = [refs.pop(0) for _ in range(CHUNKS)]
    grads = [refs.pop(0) for _ in range(PIECES)]
    cloud = refs.pop(0)
    start_first, last = move == 0, move == 1
    people, variants = centered[0].shape
    columns = variants // 2
    advance = scalars[:, 1:2]
    heat = (scalars[:, 0:1] + advance) * float(total_variants) ** (-0.5)
    approved = flipped(flags[move : move + 1, :].astype(F32)) > 0.5
    if start_first and which == KEEP:
        gram, arrived, held = refs.pop(0), refs.pop(0), refs.pop(0)
    elif start_first:
        weights, factor = refs.pop(0)[...], refs.pop(0)[...]
    else:
        size_in = refs.pop(0)
    before = refs.pop(0) if which == SEND else None
    if last and which == SEND:
        refs.pop(0)
    moved = refs.pop(0)
    if start_first:
        size_out = refs.pop(0)
        if which == KEEP:
            log_weights_out, weights_out, factor_out = refs.pop(0), refs.pop(0), refs.pop(0)
            loglik = from_lanes(held[:, columns // PIECES :]) + from_lanes(arrived[:, columns // PIECES :])
            log_weights, weights, mean_spread = weigh(total_variants, advance, loglik, gram[...])
            log_weights_out[...] = flipped(log_weights)
            weights_out[...] = weights
            factor = scalars[:, 2:3] / mean_spread
            factor_out[...] = factor
    if which == KEEP:
        total = refs.pop(0)
    else:
        mine, other, total = refs.pop(0), refs.pop(0), refs.pop(0)
    if last:
        buffer, sems = refs
    copies = []
    width = tile_of(columns // PIECES, 2048)
    narrow = tile_of(width, 512)
    at_block = []
    for piece in range(PIECES):
        first = half_of(which, piece, variants)
        at_block += [first + start for start in range(0, columns // PIECES, width)]
    for block, first in enumerate(at_block):
        chosen = []
        for start in range(block * width, (block + 1) * width, narrow):
            there = pl.ds(pl.multiple_of(first + start - block * width, narrow), narrow)
            here = slice(start, start + narrow)
            c = cloud[:, there] if start_first else cloud[:, here]
            if start_first:
                center = jnp.sum(weights * c, axis=0, keepdims=True)
                spread = jnp.sum(weights * (c - center) ** 2, axis=0, keepdims=True) + 1e-06
                size = spread * factor
                size_out[:, here] = size
            else:
                size = size_in[:, here]
            piece, at = divmod(start, columns // PIECES)
            slope = grads[piece][:, at : at + narrow].astype(F32)
            rise = heat * slope - SHRINKAGE_LEVEL * c * lax.rsqrt(c * c + 1.0)
            proposal = c + size * rise + jnp.sqrt(2.0 * size) * noise[move, :, there]
            c = jnp.where(approved, proposal, c)
            (buffer if last else moved)[:, here] = c
            chosen.append(c.astype(BF16))
        there = pl.ds(pl.multiple_of(first, width), width)
        if last:
            copies.append(
                pltpu.make_async_copy(
                    buffer.at[:, pl.ds(block * width, width)], moved.at[:, there], sems.at[block]
                )
            )
            copies[-1].start()
        chosen = jnp.concatenate(chosen, axis=1)
        for chunk in range(CHUNKS):
            rows = slice(chunk * people, (chunk + 1) * people)
            term = rows_dot(centered[chunk][:, there], chosen)
            if block > 0:
                term = total[rows, :] + term
            elif which == SEND:
                term = before[rows, :] + term
            total[rows, :] = term
    if which == SEND:
        half = people // 2
        here = core_of()
        for chunk in range(CHUNKS):
            out = slice(chunk * half, (chunk + 1) * half)
            base = chunk * people
            mine[:, out] = total[pl.ds(pl.multiple_of(base + here * half, half), half), :].T
            other[:, out] = total[pl.ds(pl.multiple_of(base + (1 - here) * half, half), half), :].T
    for copy in copies:
        copy.wait()


def update(which, move, total_variants, fixed, centered, grads, cloud, extra, before, moved):
    flags = fixed[1]
    particles, variants = flags.shape[1], centered[0].shape[1]
    people = sum(c.shape[0] for c in centered)
    columns = variants // 2
    operands = [*fixed, *centered, *grads, cloud, *extra]
    if before is not None:
        operands.append(before)
    aliases = {}
    if moved is not None:
        aliases = {len(operands): 0}
        operands.append(moved)
    last = move == 1
    out_shape = [jax.ShapeDtypeStruct((particles, variants if last else columns), F32)]
    if not last:
        out_shape.append(jax.ShapeDtypeStruct((1, columns), F32))
        if which == KEEP:
            out_shape.append(jax.ShapeDtypeStruct((1, particles), F32))
            out_shape.append(jax.ShapeDtypeStruct((particles, 1), F32))
            out_shape.append(jax.ShapeDtypeStruct((1, 1), F32))
    scratch = []
    if which == KEEP:
        out_shape.append(jax.ShapeDtypeStruct((people, particles), F32))
    else:
        out_shape += [jax.ShapeDtypeStruct((particles, people // 2), F32)] * 2
        scratch.append(pltpu.VMEM((people, particles), F32))
    if last:
        blocks = columns // tile_of(columns // PIECES, 2048)
        scratch += [pltpu.VMEM((particles, columns), F32), pltpu.SemaphoreType.DMA((blocks,))]
    specs = [VMEM] * len(operands)
    if moved is not None:
        specs[-1] = HBM
    return pl.pallas_call(
        functools.partial(update_kernel, which, move, total_variants),
        in_specs=specs,
        out_specs=[HBM if last else VMEM] + [VMEM] * (len(out_shape) - 1),
        out_shape=out_shape,
        input_output_aliases=aliases,
        scratch_shapes=scratch,
        compiler_params=params(12),
        cost_estimate=cost(8 * particles * people * columns),
        name="update_and_logits",
    )(*operands)


def swap(value, axis, distance):
    size = lax.axis_size(axis)
    return lax.ppermute(value, axis, [(i, i ^ distance) for i in range(size)])


def tree_sum(values):
    values = list(values)
    while len(values) > 1:
        values = [values[i] + values[i + 1] for i in range(0, len(values), 2)]
    return values[0]


def swap_over_rows(value, piece, stage):
    rows, columns = lax.axis_size("row"), lax.axis_size("col")
    bits = row_bits()
    order = (bits[stage], bits[::-1][stage])
    return lax.ppermute(
        value,
        ("row", "col"),
        [
            (row * columns + col, (row ^ order[piece % 2]) * columns + col)
            for row in range(rows)
            for col in range(columns)
        ],
    )


def over_chips(mine, other, link):
    mine = (mine + swap(other, "col", 1)).astype(link)
    return [mine] + [swap(mine, "col", d) for d in range(2, lax.axis_size("col"), 2)]


def over_chips_by_stages(mine, other):
    mine = mine + swap(other, "col", 1)
    size = lax.axis_size("col")
    bits = [1 << b for b in range(1, size.bit_length() - 1)]
    for stage, order in enumerate(zip(bits, bits[::-1])):
        arrived = lax.ppermute(mine, "col", [(i, i ^ order[i % 2]) for i in range(size)])
        if stage < len(bits) - 1:
            mine = mine + arrived
    return [mine, arrived]


def sum_small(value):
    value = value + swap(value, "col", 1)
    size = lax.axis_size("row")
    return tree_sum([value] + [swap(value, "row", d) for d in range(1, size)])


def local(
    allele_doses,
    disease_status,
    walker_cloud,
    normal_perturbations,
    approval_flags,
    present_heat,
    heat_advance,
    drift_magnitude,
):
    people, variants = allele_doses.shape
    total_variants = variants * lax.axis_size("col")
    total_people = people * lax.axis_size("row")
    scale = float(total_variants) ** (-0.5)
    status = disease_status.reshape(1, people)
    scalars = jnp.concatenate([present_heat, heat_advance, drift_magnitude])[None, :]

    centered, pairs, loglik, gram, sent = [], [], None, None, None
    for chunk in range(CHUNKS + 1):
        if chunk < CHUNKS:
            part, mine, other = center_and_first_logits(chunk, allele_doses, walker_cloud, scalars)
            centered.append(part)
        if chunk > 0:
            if chunk < CHUNKS:
                (mine, other), sent = lax.optimization_barrier(((mine, other), sent))
            tail = chunk == CHUNKS
            own, *extra = residual_of(
                scale,
                status,
                (chunk - 1,),
                sent,
                earlier=loglik,
                tail=tail,
                gram=chunk == 1,
                loglik_as=None if tail else "column",
            )
            if chunk == 1:
                gram = extra.pop()
            if not tail:
                (loglik,) = extra
            pairs += [own, swap(own, "col", 1)]
        if chunk < CHUNKS:
            sent = over_chips_by_stages(mine, other)

    width = variants // 2 // PIECES
    fixed = (scalars, approval_flags, normal_perturbations)
    stages = len(row_bits())
    pieces = range(PIECES)
    for move in range(2):
        first = move == 0
        tails = [first and piece == 0 for piece in pieces]
        arrived = [
            swap_over_rows(gradient(SEND, piece, pairs, centered, tails[piece]), piece, 0)
            for piece in pieces
        ]
        held = [gradient(KEEP, piece, pairs, centered, tails[piece]) for piece in pieces]
        for stage in range(1, stages):
            held = [pair_sum(width, *each) for each in zip(tails, held, arrived)]
            arrived = [swap_over_rows(each, piece, stage) for piece, each in enumerate(held)]
        summed = [pair_sum(width, False, *each) for each in zip(held, arrived)]
        arriving = [swap_over_rows(each, piece, 0) for piece, each in enumerate(summed)]
        if first:
            c_kept, size_kept, log_weights, weights, factor, total = update(
                KEEP, move, total_variants, fixed, centered, summed, walker_cloud,
                [gram, arrived[0], held[0]], None, None,
            )
            c_sent, size_sent, mine, other = update(
                SEND, move, total_variants, fixed, centered, arriving, walker_cloud,
                [weights, factor], total, None,
            )
        else:
            moved, total = update(
                KEEP, move, total_variants, fixed, centered, summed, c_kept, [size_kept], None, None
            )
            moved, mine, other = update(
                SEND, move, total_variants, fixed, centered, arriving, c_sent, [size_sent], total, moved
            )
        sent = over_chips(mine, other, BF16)
        if first:
            (own,) = residual_of(scale, status, tuple(range(CHUNKS)), sent)
            pairs = [own, swap(own, "col", 1)]
        else:
            _, loglik = residual_of(
                scale, status, tuple(range(CHUNKS)), sent, loglik_as="row"
            )
    mean_loglik = sum_small(loglik) / total_people
    return (moved, log_weights[0], mean_loglik[0])


def solution(mesh):
    placed = (P("row", "col"), P("row"), P(None, "col"), P(None, None, "col"), P(), P(), P(), P())
    return jax.shard_map(
        local, mesh=mesh, in_specs=placed, out_specs=(P(None, "col"), P(), P()), check_vma=False
    )
```

time: 146 us -> 126 us (0.86)
  waiting for transfers between devices: 68.8 us -> 38.6 us
  starting transfers between devices: 34.7 us -> 46 us
  Pallas kernels: 37.3 us -> 35.8 us
    ppermute x31 -> x15, waiting for transfers between devices: 68.8 us -> 19.3 us  [swap(): return lax.ppermute(value, axis, [(i, i ^ distance) for i in range(size)])]
    ppermute x0 -> x26, starting transfers between devices: none -> 32.6 us  [the longest x24 27.1 us: swap_over_rows(): lax.ppermute(value, ('row', 'col'), [(row * columns + col, (row ^ order[p...]
    ppermute x31 -> x15, starting transfers between devices: 34.7 us -> 13.4 us  [swap(): return lax.ppermute(value, axis, [(i, i ^ distance) for i in range(size)])]
    ppermute x0 -> x26, waiting for transfers between devices: none -> 19.3 us  [the longest x24 10.8 us: swap_over_rows(): lax.ppermute(value, ('row', 'col'), [(row * columns + col, (row ^ order[p...]
    pallas_call x2 -> x1, Pallas kernels: 14.4 us -> 13.1 us  [center_and_first_logits(): pl.pallas_call(functools.partial(center_kernel, block, with_gram), grid=(...]
    pallas_call x6 -> x20, Pallas kernels: 21 us -> 21 us  [the longest x4 13 us: update(): pl.pallas_call(functools.partial(update_kernel, which, move, total_varian...]
  transfers between devices with their start and end apart: 31 -> 41, of which waited for: 24 -> 21; matrix products, arithmetic and copies ran while one was open for 0% -> 0% of each run, Pallas kernels for 8% -> 11%
where the time goes in v2:
time: 126 us
  starting transfers between devices  46 us (37%)
  waiting for transfers between devices  38.6 us (31%)
  Pallas kernels  35.8 us (28%)
  between operations  2.93 us (2%)
  local copies, waits for them, and re-layouts  1.61 us (1%)
    ppermute x24, starting transfers between devices, swap_over_rows(): lax.ppermute(value, ('row', 'col'), [(row * columns + col, (row ^ order[p...  27.1 us
    ppermute x15, waiting for transfers between devices, swap(): return lax.ppermute(value, axis, [(i, i ^ distance) for i in range(size)])  19.3 us
    ppermute x15, starting transfers between devices, swap(): return lax.ppermute(value, axis, [(i, i ^ distance) for i in range(size)])  13.4 us
    pallas_call x1, Pallas kernels, center_and_first_logits(): pl.pallas_call(functools.partial(center_kernel, block, with_gram), grid=(...  13.1 us
    pallas_call x4, Pallas kernels, update(): pl.pallas_call(functools.partial(update_kernel, which, move, total_varian...  13 us
    ppermute x24, waiting for transfers between devices, swap_over_rows(): lax.ppermute(value, ('row', 'col'), [(row * columns + col, (row ^ order[p...  10.8 us
    ppermute x2, waiting for transfers between devices, over_chips_by_stages(): lax.ppermute(mine, 'col', [(i, i ^ order[i % 2]) for i in range(size)])  8.52 us
    pallas_call x16, Pallas kernels, gradient(): pl.pallas_call(functools.partial(gradient_kernel, len(pairs) // 2, which,...  8.08 us
  transfers between devices with their start and end apart: 41, of which 21 were waited for; matrix products, arithmetic and copies ran while one was open for 0% of the time, Pallas kernels for 11%

profile of v2, /device:TPU:0, one launch (start us, length us, event | category | flops | bytes accessed | tf_op | source)
XLA Modules:
  0.0 125.6 jit_solution(7693918955297074311)
XLA Ops:
  2.6 1.6 %copy-done.1 = f32[64,8192]{1,0:T(8,128)S(1)} copy-done((f32[64,8192]{1,0:T(8,128)S(1)}, f32[64,8192]{1,0:T(8,128)}, u32[]{:S(2)}) %copy-start.1) | copy-done | bytes 2097176
  4.2 13.1 %center_and_first_logits.1 = (bf16[1024,8192]{1,0:T(8,128)(2,1)S(1)}, f32[64,640]{1,0:T(8,128)S(1)}, f32[64,640]{1,0:T(8,128)S(1)}) custom-call(s32[1024,8192]{1,0:T(8,128)} %doses.1, f32[64,8192]{1,0:T(8,128)S(1)} %copy-done.1, f32[1,3]{1,0:T(1,128)S(1)} %maximum_bitcast_fusion._.scalars), custom_call_target="tpu_custom_call" | custom-call | flops 8589934592 | tf_op jit(solution)/shard_map/center_and_first_logits/pallas_call | solution.py:139
  18.9 3.0 %collective-permute-start.1 = (f32[64,640]{1,0:T(8,128)S(1)}, f32[64,640]{1,0:T(8,128)S(1)}, u32[]{:S(2)}, u32[]{:S(2)}) collective-permute-start(f32[64,640]{1,0:T(8,128)S(1)} %add.24), channel_id=1, source_target_pairs={{0,2},{1,5},{2,0},{3,7},{4,6},{5,1},{6,4},{7,3},{8,10},{9,13},{10,... | collective-permute-start | bytes 491528 | tf_op jit(solution)/shard_map/ppermute | solution.py:467
  21.9 4.6 %collective-permute-done.1 = f32[64,640]{1,0:T(8,128)S(1)} collective-permute-done((f32[64,640]{1,0:T(8,128)S(1)}, f32[64,640]{1,0:T(8,128)S(1)}, u32[]{:S(2)}, u32[]{:S(2)}) %collective-permute-start.1) | collective-permute-done | bytes 163872 | tf_op jit(solution)/shard_map/ppermute | solution.py:467
  26.5 2.6 %collective-permute-start.2 = (f32[64,640]{1,0:T(8,128)S(1)}, f32[64,640]{1,0:T(8,128)S(1)}, u32[]{:S(2)}, u32[]{:S(2)}) collective-permute-start(f32[64,640]{1,0:T(8,128)S(1)} %add.25.refs_0_), channel_id=1, source_target_pairs={{0,4},{1,3},{2,6},{3,1},{4,0},{5,7},{6,2},{7,5},{8,12},{9,11},{10,... | collective-permute-start | bytes 491528 | tf_op jit(solution)/shard_map/ppermute | solution.py:467
  29.1 3.9 %collective-permute-done.2.refs_1_ = f32[64,640]{1,0:T(8,128)S(1)} collective-permute-done((f32[64,640]{1,0:T(8,128)S(1)}, f32[64,640]{1,0:T(8,128)S(1)}, u32[]{:S(2)}, u32[]{:S(2)}) %collective-permute-start.2) | collective-permute-done | bytes 163872 | tf_op jit(solution)/shard_map/ppermute | solution.py:467
  35.0 3.1 %collective-permute-start.7 = (bf16[64,1024]{1,0:T(8,128)(2,1)S(1)}, bf16[64,1024]{1,0:T(8,128)(2,1)S(1)}, u32[]{:S(2)}, u32[]{:S(2)}) collective-permute-start(bf16[64,1024]{1,0:T(8,128)(2,1)S(1)} %gradient.19), channel_id=1, source_target_pairs={{0,16},{1,17},{2,18},{3,19},{4,20},{5,21},{6,22},{7,23},{8,24},{9,... | collective-permute-start | bytes 393224 | tf_op jit(solution)/shard_map/ppermute | solution.py:446
  38.6 1.6 %collective-permute-start.10 = (bf16[64,1024]{1,0:T(8,128)(2,1)S(1)}, bf16[64,1024]{1,0:T(8,128)(2,1)S(1)}, u32[]{:S(2)}, u32[]{:S(2)}) collective-permute-start(bf16[64,1024]{1,0:T(8,128)(2,1)S(1)} %gradient.21), channel_id=1, source_target_pairs={{0,8},{1,9},{2,10},{3,11},{4,12},{5,13},{6,14},{7,15},{8,0},{9,1},... | collective-permute-start | bytes 393224 | tf_op jit(solution)/shard_map/ppermute | solution.py:446
  43.3 3.7 %collective-permute-done.4.right = bf16[64,1152]{1,0:T(8,128)(2,1)S(1)} collective-permute-done((bf16[64,1152]{1,0:T(8,128)(2,1)S(1)}, bf16[64,1152]{1,0:T(8,128)(2,1)S(1)}, u32[]{:S(2)}, u32[]{:S(2)}) %collective-permute-start.4) | collective-permute-done | bytes 147488 | tf_op jit(solution)/shard_map/ppermute | solution.py:446
  47.2 1.4 %collective-permute-start.5 = (bf16[64,1152]{1,0:T(8,128)(2,1)S(1)}, bf16[64,1152]{1,0:T(8,128)(2,1)S(1)}, u32[]{:S(2)}, u32[]{:S(2)}) collective-permute-start(bf16[64,1152]{1,0:T(8,128)(2,1)S(1)} %pair_sum.16.left.refs_8_), channel_id=1, source_target_pairs={{0,16},{1,17},{2,18},{3,19},{4,20},{5,21},{6,22},{7,23},{8,24},{9,... | collective-permute-start | bytes 442376 | tf_op jit(solution)/shard_map/ppermute | solution.py:446
  50.0 1.6 %collective-permute-start.11 = (bf16[64,1024]{1,0:T(8,128)(2,1)S(1)}, bf16[64,1024]{1,0:T(8,128)(2,1)S(1)}, u32[]{:S(2)}, u32[]{:S(2)}) collective-permute-start(bf16[64,1024]{1,0:T(8,128)(2,1)S(1)} %pair_sum.20.left), channel_id=1, source_target_pairs={{0,16},{1,17},{2,18},{3,19},{4,20},{5,21},{6,22},{7,23},{8,24},{9,... | collective-permute-start | bytes 393224 | tf_op jit(solution)/shard_map/ppermute | solution.py:446
  52.2 3.0 %collective-permute-done.8.right = bf16[64,1024]{1,0:T(8,128)(2,1)S(1)} collective-permute-done((bf16[64,1024]{1,0:T(8,128)(2,1)S(1)}, bf16[64,1024]{1,0:T(8,128)(2,1)S(1)}, u32[]{:S(2)}, u32[]{:S(2)}) %collective-permute-start.8) | collective-permute-done | bytes 131104 | tf_op jit(solution)/shard_map/ppermute | solution.py:446
  58.2 2.1 %collective-permute-start.6 = (bf16[64,1024]{1,0:T(8,128)(2,1)S(1)}, bf16[64,1024]{1,0:T(8,128)(2,1)S(1)}, u32[]{:S(2)}, u32[]{:S(2)}) collective-permute-start(bf16[64,1024]{1,0:T(8,128)(2,1)S(1)} %pair_sum.17.refs_1_), channel_id=1, source_target_pairs={{0,8},{1,9},{2,10},{3,11},{4,12},{5,13},{6,14},{7,15},{8,0},{9,1},... | collective-permute-start | bytes 393224 | tf_op jit(solution)/shard_map/ppermute | solution.py:446
  60.3 3.3 %update_and_logits.4 = (f32[64,4096]{1,0:T(8,128)S(1)}, f32[1,4096]{1,0:T(1,128)S(1)}, f32[1,64]{1,0:T(1,128)}, f32[64,1]{1,0:T(8,128)S(1)}, f32[1,1]{1,0:T(1,128)}, /*index=5*/f32[1024,64]{1,0:T(8,128)S(1)}) custom-call(f32[1,3]{1,0:T(1,128)S(1)} %maximum_bitcast_fusion._.scalars, s32[2,64]{1,0:T(2,128)S(1)} %copy-done.3, f32[2,64,8192]{2,1,0:T(8,128)S(1)} %copy-done, ...), custom_call_target="tpu_custom_call" | custom-call | flops 2147483648 | tf_op jit(solution)/shard_map/update_and_logits/pallas_call | solution.py:417
  63.6 3.5 %update_and_logits.5 = (f32[64,4096]{1,0:T(8,128)S(1)}, f32[1,4096]{1,0:T(1,128)S(1)}, f32[64,512]{1,0:T(8,128)S(1)}, f32[64,512]{1,0:T(8,128)S(1)}) custom-call(f32[1,3]{1,0:T(1,128)S(1)} %maximum_bitcast_fusion._.scalars, s32[2,64]{1,0:T(2,128)S(1)} %copy-done.3, f32[2,64,8192]{2,1,0:T(8,128)S(1)} %copy-done, ...), custom_call_target="tpu_custom_call" | custom-call | flops 2147483648 | tf_op jit(solution)/shard_map/update_and_logits/pallas_call | solution.py:417
  67.2 1.3 %collective-permute-done.16 = f32[64,512]{1,0:T(8,128)S(1)} collective-permute-done((f32[64,512]{1,0:T(8,128)S(1)}, f32[64,512]{1,0:T(8,128)S(1)}, u32[]{:S(2)}, u32[]{:S(2)}) %collective-permute-start.16) | collective-permute-done | bytes 131104 | tf_op jit(solution)/shard_map/ppermute | solution.py:432
  68.6 3.6 %collective-permute-start.19 = (bf16[64,512]{1,0:T(8,128)(2,1)S(1)}, bf16[64,512]{1,0:T(8,128)(2,1)S(1)}, u32[]{:S(2)}, u32[]{:S(2)}) collective-permute-start(bf16[64,512]{1,0:T(8,128)(2,1)S(1)} %add_convert_fusion.1.refs_0_), channel_id=1, source_target_pairs={{0,6},{1,7},{2,4},{3,5},{4,2},{5,3},{6,0},{7,1},{8,14},{9,15},{10,... | collective-permute-start | bytes 196616 | tf_op jit(solution)/shard_map/ppermute | solution.py:432
  73.0 2.5 %collective-permute-done.19.refs_3_ = bf16[64,512]{1,0:T(8,128)(2,1)S(1)} collective-permute-done((bf16[64,512]{1,0:T(8,128)(2,1)S(1)}, bf16[64,512]{1,0:T(8,128)(2,1)S(1)}, u32[]{:S(2)}, u32[]{:S(2)}) %collective-permute-start.19) | collective-permute-done | bytes 65568 | tf_op jit(solution)/shard_map/ppermute | solution.py:432
  75.5 2.6 %collective-permute-done.18.refs_2_ = bf16[64,512]{1,0:T(8,128)(2,1)S(1)} collective-permute-done((bf16[64,512]{1,0:T(8,128)(2,1)S(1)}, bf16[64,512]{1,0:T(8,128)(2,1)S(1)}, u32[]{:S(2)}, u32[]{:S(2)}) %collective-permute-start.18) | collective-permute-done | bytes 65568 | tf_op jit(solution)/shard_map/ppermute | solution.py:432
  78.2 1.2 collective-permute-done.20.refs_1_
  79.9 1.7 %collective-permute-start.21 = (bf16[64,1024]{1,0:T(8,128)(2,1)S(1)}, bf16[64,1024]{1,0:T(8,128)(2,1)S(1)}, u32[]{:S(2)}, u32[]{:S(2)}) collective-permute-start(bf16[64,1024]{1,0:T(8,128)(2,1)S(1)} %gradient.25), channel_id=1, source_target_pairs={{0,8},{1,9},{2,10},{3,11},{4,12},{5,13},{6,14},{7,15},{8,0},{9,1},... | collective-permute-start | bytes 393224 | tf_op jit(solution)/shard_map/ppermute | solution.py:446
  90.4 1.6 %collective-permute-start.28 = (bf16[64,1024]{1,0:T(8,128)(2,1)S(1)}, bf16[64,1024]{1,0:T(8,128)(2,1)S(1)}, u32[]{:S(2)}, u32[]{:S(2)}) collective-permute-start(bf16[64,1024]{1,0:T(8,128)(2,1)S(1)} %pair_sum.28.left), channel_id=1, source_target_pairs={{0,16},{1,17},{2,18},{3,19},{4,20},{5,21},{6,22},{7,23},{8,24},{9,... | collective-permute-start | bytes 393224 | tf_op jit(solution)/shard_map/ppermute | solution.py:446
  92.4 2.1 %collective-permute-done.22.right = bf16[64,1024]{1,0:T(8,128)(2,1)S(1)} collective-permute-done((bf16[64,1024]{1,0:T(8,128)(2,1)S(1)}, bf16[64,1024]{1,0:T(8,128)(2,1)S(1)}, u32[]{:S(2)}, u32[]{:S(2)}) %collective-permute-start.22) | collective-permute-done | bytes 131104 | tf_op jit(solution)/shard_map/ppermute | solution.py:446
  96.8 1.7 %collective-permute-start.29 = (bf16[64,1024]{1,0:T(8,128)(2,1)S(1)}, bf16[64,1024]{1,0:T(8,128)(2,1)S(1)}, u32[]{:S(2)}, u32[]{:S(2)}) collective-permute-start(bf16[64,1024]{1,0:T(8,128)(2,1)S(1)} %pair_sum.29.refs_3_), channel_id=1, source_target_pairs={{0,8},{1,9},{2,10},{3,11},{4,12},{5,13},{6,14},{7,15},{8,0},{9,1},... | collective-permute-start | bytes 393224 | tf_op jit(solution)/shard_map/ppermute | solution.py:446
  99.4 3.1 %update_and_logits.6 = (f32[64,8192]{1,0:T(8,128)}, f32[1024,64]{1,0:T(8,128)S(1)}) custom-call(f32[1,3]{1,0:T(1,128)S(1)} %maximum_bitcast_fusion._.scalars, s32[2,64]{1,0:T(2,128)S(1)} %copy-done.3, f32[2,64,8192]{2,1,0:T(8,128)S(1)} %copy-done, bf16[1024,8192]{1,0:T(8,128)(2,1)S(1)} %get-tuple-element.24.refs_2_.refs_0_, ...), custom_call_target="tpu_custom_call" | custom-call | flops 2147483648 | tf_op jit(solution)/shard_map/update_and_logits/pallas_call | solution.py:417
  103.6 3.1 %update_and_logits.7 = (f32[64,8192]{1,0:T(8,128)}, f32[64,512]{1,0:T(8,128)S(1)}, f32[64,512]{1,0:T(8,128)S(1)}) custom-call(f32[1,3]{1,0:T(1,128)S(1)} %maximum_bitcast_fusion._.scalars, s32[2,64]{1,0:T(2,128)S(1)} %copy-done.3, f32[2,64,8192]{2,1,0:T(8,128)S(1)} %copy-done, ...), custom_call_target="tpu_custom_call", output_to_operand_aliasing={{0}: (11, {})} | custom-call | flops 2147483648 | tf_op jit(solution)/shard_map/update_and_logits/pallas_call | solution.py:417
  106.8 1.3 %collective-permute-done.33 = f32[64,512]{1,0:T(8,128)S(1)} collective-permute-done((f32[64,512]{1,0:T(8,128)S(1)}, f32[64,512]{1,0:T(8,128)S(1)}, u32[]{:S(2)}, u32[]{:S(2)}) %collective-permute-start.33) | collective-permute-done | bytes 131104 | tf_op jit(solution)/shard_map/ppermute | solution.py:432
  108.1 2.2 %collective-permute-start.36 = (bf16[64,512]{1,0:T(8,128)(2,1)S(1)}, bf16[64,512]{1,0:T(8,128)(2,1)S(1)}, u32[]{:S(2)}, u32[]{:S(2)}) collective-permute-start(bf16[64,512]{1,0:T(8,128)(2,1)S(1)} %add_convert_fusion.refs_0_), channel_id=1, source_target_pairs={{0,6},{1,7},{2,4},{3,5},{4,2},{5,3},{6,0},{7,1},{8,14},{9,15},{10,... | collective-permute-start | bytes 196616 | tf_op jit(solution)/shard_map/ppermute | solution.py:432
  110.7 1.8 %collective-permute-start.34 = (bf16[64,512]{1,0:T(8,128)(2,1)S(1)}, bf16[64,512]{1,0:T(8,128)(2,1)S(1)}, u32[]{:S(2)}, u32[]{:S(2)}) collective-permute-start(bf16[64,512]{1,0:T(8,128)(2,1)S(1)} %add_convert_fusion.refs_0_), channel_id=1, source_target_pairs={{0,2},{1,3},{2,0},{3,1},{4,6},{5,7},{6,4},{7,5},{8,10},{9,11},{10,... | collective-permute-start | bytes 196616 | tf_op jit(solution)/shard_map/ppermute | solution.py:432
  112.6 2.4 %collective-permute-done.36.refs_3_ = bf16[64,512]{1,0:T(8,128)(2,1)S(1)} collective-permute-done((bf16[64,512]{1,0:T(8,128)(2,1)S(1)}, bf16[64,512]{1,0:T(8,128)(2,1)S(1)}, u32[]{:S(2)}, u32[]{:S(2)}) %collective-permute-start.36) | collective-permute-done | bytes 65568 | tf_op jit(solution)/shard_map/ppermute | solution.py:432
  114.9 2.2 %collective-permute-done.35.refs_2_ = bf16[64,512]{1,0:T(8,128)(2,1)S(1)} collective-permute-done((bf16[64,512]{1,0:T(8,128)(2,1)S(1)}, bf16[64,512]{1,0:T(8,128)(2,1)S(1)}, u32[]{:S(2)}, u32[]{:S(2)}) %collective-permute-start.35) | collective-permute-done | bytes 65568 | tf_op jit(solution)/shard_map/ppermute | solution.py:432
  119.1 2.0 %collective-permute-start.40 = (f32[1,64]{1,0:T(1,128)S(1)}, f32[1,64]{1,0:T(1,128)S(1)}, u32[]{:S(2)}, u32[]{:S(2)}) collective-permute-start(f32[1,64]{1,0:T(1,128)S(1)} %add.28), channel_id=1, source_target_pairs={{0,24},{8,16},{16,8},{24,0},{1,25},{9,17},{17,9},{25,1},{2,26},{10... | collective-permute-start | bytes 776 | tf_op jit(solution)/shard_map/ppermute | solution.py:432
  (105 shorter events, 34.2 us)
Async XLA Ops:
  18.9 7.6 %collective-permute-start.1 = (f32[64,640]{1,0:T(8,128)S(1)}, f32[64,640]{1,0:T(8,128)S(1)}, u32[]{:S(2)}, u32[]{:S(2)}) collective-permute-start(f32[64,640]{1,0:T(8,128)S(1)} %add.24), channel_id=1, source_target_pairs={{0,2},{1,5},{2,0},{3,7},{4,6},{5,1},{6,4},{7,3},{8,10},{9,13},{10,... | collective-permute-start | bytes 491528 | tf_op jit(solution)/shard_map/ppermute | solution.py:467
  26.5 6.5 %collective-permute-start.2 = (f32[64,640]{1,0:T(8,128)S(1)}, f32[64,640]{1,0:T(8,128)S(1)}, u32[]{:S(2)}, u32[]{:S(2)}) collective-permute-start(f32[64,640]{1,0:T(8,128)S(1)} %add.25.refs_0_), channel_id=1, source_target_pairs={{0,4},{1,3},{2,6},{3,1},{4,0},{5,7},{6,2},{7,5},{8,12},{9,11},{10,... | collective-permute-start | bytes 491528 | tf_op jit(solution)/shard_map/ppermute | solution.py:467
  35.0 14.1 %collective-permute-start.7 = (bf16[64,1024]{1,0:T(8,128)(2,1)S(1)}, bf16[64,1024]{1,0:T(8,128)(2,1)S(1)}, u32[]{:S(2)}, u32[]{:S(2)}) collective-permute-start(bf16[64,1024]{1,0:T(8,128)(2,1)S(1)} %gradient.19), channel_id=1, source_target_pairs={{0,16},{1,17},{2,18},{3,19},{4,20},{5,21},{6,22},{7,23},{8,24},{9,... | collective-permute-start | bytes 393224 | tf_op jit(solution)/shard_map/ppermute | solution.py:446
  38.6 11.4 %collective-permute-start.10 = (bf16[64,1024]{1,0:T(8,128)(2,1)S(1)}, bf16[64,1024]{1,0:T(8,128)(2,1)S(1)}, u32[]{:S(2)}, u32[]{:S(2)}) collective-permute-start(bf16[64,1024]{1,0:T(8,128)(2,1)S(1)} %gradient.21), channel_id=1, source_target_pairs={{0,8},{1,9},{2,10},{3,11},{4,12},{5,13},{6,14},{7,15},{8,0},{9,1},... | collective-permute-start | bytes 393224 | tf_op jit(solution)/shard_map/ppermute | solution.py:446
  40.6 10.9 %collective-permute-start.13 = (bf16[64,1024]{1,0:T(8,128)(2,1)S(1)}, bf16[64,1024]{1,0:T(8,128)(2,1)S(1)}, u32[]{:S(2)}, u32[]{:S(2)}) collective-permute-start(bf16[64,1024]{1,0:T(8,128)(2,1)S(1)} %gradient.23), channel_id=1, source_target_pairs={{0,16},{1,17},{2,18},{3,19},{4,20},{5,21},{6,22},{7,23},{8,24},{9,... | collective-permute-start | bytes 393224 | tf_op jit(solution)/shard_map/ppermute | solution.py:446
  41.7 5.4 %collective-permute-start.4 = (bf16[64,1152]{1,0:T(8,128)(2,1)S(1)}, bf16[64,1152]{1,0:T(8,128)(2,1)S(1)}, u32[]{:S(2)}, u32[]{:S(2)}) collective-permute-start(bf16[64,1152]{1,0:T(8,128)(2,1)S(1)} %gradient.17), channel_id=1, source_target_pairs={{0,8},{1,9},{2,10},{3,11},{4,12},{5,13},{6,14},{7,15},{8,0},{9,1},... | collective-permute-start | bytes 442376 | tf_op jit(solution)/shard_map/ppermute | solution.py:446
  47.2 11.0 %collective-permute-start.5 = (bf16[64,1152]{1,0:T(8,128)(2,1)S(1)}, bf16[64,1152]{1,0:T(8,128)(2,1)S(1)}, u32[]{:S(2)}, u32[]{:S(2)}) collective-permute-start(bf16[64,1152]{1,0:T(8,128)(2,1)S(1)} %pair_sum.16.left.refs_8_), channel_id=1, source_target_pairs={{0,16},{1,17},{2,18},{3,19},{4,20},{5,21},{6,22},{7,23},{8,24},{9,... | collective-permute-start | bytes 442376 | tf_op jit(solution)/shard_map/ppermute | solution.py:446
  49.2 6.0 %collective-permute-start.8 = (bf16[64,1024]{1,0:T(8,128)(2,1)S(1)}, bf16[64,1024]{1,0:T(8,128)(2,1)S(1)}, u32[]{:S(2)}, u32[]{:S(2)}) collective-permute-start(bf16[64,1024]{1,0:T(8,128)(2,1)S(1)} %pair_sum.18.left), channel_id=1, source_target_pairs={{0,8},{1,9},{2,10},{3,11},{4,12},{5,13},{6,14},{7,15},{8,0},{9,1},... | collective-permute-start | bytes 393224 | tf_op jit(solution)/shard_map/ppermute | solution.py:446
  50.0 6.5 %collective-permute-start.11 = (bf16[64,1024]{1,0:T(8,128)(2,1)S(1)}, bf16[64,1024]{1,0:T(8,128)(2,1)S(1)}, u32[]{:S(2)}, u32[]{:S(2)}) collective-permute-start(bf16[64,1024]{1,0:T(8,128)(2,1)S(1)} %pair_sum.20.left), channel_id=1, source_target_pairs={{0,16},{1,17},{2,18},{3,19},{4,20},{5,21},{6,22},{7,23},{8,24},{9,... | collective-permute-start | bytes 393224 | tf_op jit(solution)/shard_map/ppermute | solution.py:446
  51.6 6.0 %collective-permute-start.14 = (bf16[64,1024]{1,0:T(8,128)(2,1)S(1)}, bf16[64,1024]{1,0:T(8,128)(2,1)S(1)}, u32[]{:S(2)}, u32[]{:S(2)}) collective-permute-start(bf16[64,1024]{1,0:T(8,128)(2,1)S(1)} %pair_sum.22.left), channel_id=1, source_target_pairs={{0,8},{1,9},{2,10},{3,11},{4,12},{5,13},{6,14},{7,15},{8,0},{9,1},... | collective-permute-start | bytes 393224 | tf_op jit(solution)/shard_map/ppermute | solution.py:446
  55.3 8.3 %collective-permute-start.9 = (bf16[64,1024]{1,0:T(8,128)(2,1)S(1)}, bf16[64,1024]{1,0:T(8,128)(2,1)S(1)}, u32[]{:S(2)}, u32[]{:S(2)}) collective-permute-start(bf16[64,1024]{1,0:T(8,128)(2,1)S(1)} %pair_sum.19.refs_2_), channel_id=1, source_target_pairs={{0,16},{1,17},{2,18},{3,19},{4,20},{5,21},{6,22},{7,23},{8,24},{9,... | collective-permute-start | bytes 393224 | tf_op jit(solution)/shard_map/ppermute | solution.py:446
  56.5 7.1 %collective-permute-start.12 = (bf16[64,1024]{1,0:T(8,128)(2,1)S(1)}, bf16[64,1024]{1,0:T(8,128)(2,1)S(1)}, u32[]{:S(2)}, u32[]{:S(2)}) collective-permute-start(bf16[64,1024]{1,0:T(8,128)(2,1)S(1)} %pair_sum.21.refs_3_), channel_id=1, source_target_pairs={{0,8},{1,9},{2,10},{3,11},{4,12},{5,13},{6,14},{7,15},{8,0},{9,1},... | collective-permute-start | bytes 393224 | tf_op jit(solution)/shard_map/ppermute | solution.py:446
  57.6 6.0 %collective-permute-start.15 = (bf16[64,1024]{1,0:T(8,128)(2,1)S(1)}, bf16[64,1024]{1,0:T(8,128)(2,1)S(1)}, u32[]{:S(2)}, u32[]{:S(2)}) collective-permute-start(bf16[64,1024]{1,0:T(8,128)(2,1)S(1)} %pair_sum.23.refs_4_), channel_id=1, source_target_pairs={{0,16},{1,17},{2,18},{3,19},{4,20},{5,21},{6,22},{7,23},{8,24},{9,... | collective-permute-start | bytes 393224 | tf_op jit(solution)/shard_map/ppermute | solution.py:446
  58.2 5.4 %collective-permute-start.6 = (bf16[64,1024]{1,0:T(8,128)(2,1)S(1)}, bf16[64,1024]{1,0:T(8,128)(2,1)S(1)}, u32[]{:S(2)}, u32[]{:S(2)}) collective-permute-start(bf16[64,1024]{1,0:T(8,128)(2,1)S(1)} %pair_sum.17.refs_1_), channel_id=1, source_target_pairs={{0,8},{1,9},{2,10},{3,11},{4,12},{5,13},{6,14},{7,15},{8,0},{9,1},... | collective-permute-start | bytes 393224 | tf_op jit(solution)/shard_map/ppermute | solution.py:446
  68.6 6.9 %collective-permute-start.19 = (bf16[64,512]{1,0:T(8,128)(2,1)S(1)}, bf16[64,512]{1,0:T(8,128)(2,1)S(1)}, u32[]{:S(2)}, u32[]{:S(2)}) collective-permute-start(bf16[64,512]{1,0:T(8,128)(2,1)S(1)} %add_convert_fusion.1.refs_0_), channel_id=1, source_target_pairs={{0,6},{1,7},{2,4},{3,5},{4,2},{5,3},{6,0},{7,1},{8,14},{9,15},{10,... | collective-permute-start | bytes 196616 | tf_op jit(solution)/shard_map/ppermute | solution.py:432
  72.1 5.9 %collective-permute-start.18 = (bf16[64,512]{1,0:T(8,128)(2,1)S(1)}, bf16[64,512]{1,0:T(8,128)(2,1)S(1)}, u32[]{:S(2)}, u32[]{:S(2)}) collective-permute-start(bf16[64,512]{1,0:T(8,128)(2,1)S(1)} %add_convert_fusion.1.refs_0_), channel_id=1, source_target_pairs={{0,4},{1,5},{2,6},{3,7},{4,0},{5,1},{6,2},{7,3},{8,12},{9,13},{10,... | collective-permute-start | bytes 196616 | tf_op jit(solution)/shard_map/ppermute | solution.py:432
  72.1 5.9 %collective-permute-start.17 = (bf16[64,512]{1,0:T(8,128)(2,1)S(1)}, bf16[64,512]{1,0:T(8,128)(2,1)S(1)}, u32[]{:S(2)}, u32[]{:S(2)}) collective-permute-start(bf16[64,512]{1,0:T(8,128)(2,1)S(1)} %add_convert_fusion.1.refs_0_), channel_id=1, source_target_pairs={{0,2},{1,3},{2,0},{3,1},{4,6},{5,7},{6,4},{7,5},{8,10},{9,11},{10,... | collective-permute-start | bytes 196616 | tf_op jit(solution)/shard_map/ppermute | solution.py:432
  79.9 8.0 %collective-permute-start.21 = (bf16[64,1024]{1,0:T(8,128)(2,1)S(1)}, bf16[64,1024]{1,0:T(8,128)(2,1)S(1)}, u32[]{:S(2)}, u32[]{:S(2)}) collective-permute-start(bf16[64,1024]{1,0:T(8,128)(2,1)S(1)} %gradient.25), channel_id=1, source_target_pairs={{0,8},{1,9},{2,10},{3,11},{4,12},{5,13},{6,14},{7,15},{8,0},{9,1},... | collective-permute-start | bytes 393224 | tf_op jit(solution)/shard_map/ppermute | solution.py:446
  82.2 7.1 %collective-permute-start.24 = (bf16[64,1024]{1,0:T(8,128)(2,1)S(1)}, bf16[64,1024]{1,0:T(8,128)(2,1)S(1)}, u32[]{:S(2)}, u32[]{:S(2)}) collective-permute-start(bf16[64,1024]{1,0:T(8,128)(2,1)S(1)} %gradient.27), channel_id=1, source_target_pairs={{0,16},{1,17},{2,18},{3,19},{4,20},{5,21},{6,22},{7,23},{8,24},{9,... | collective-permute-start | bytes 393224 | tf_op jit(solution)/shard_map/ppermute | solution.py:446
  83.2 7.1 %collective-permute-start.27 = (bf16[64,1024]{1,0:T(8,128)(2,1)S(1)}, bf16[64,1024]{1,0:T(8,128)(2,1)S(1)}, u32[]{:S(2)}, u32[]{:S(2)}) collective-permute-start(bf16[64,1024]{1,0:T(8,128)(2,1)S(1)} %gradient.29), channel_id=1, source_target_pairs={{0,8},{1,9},{2,10},{3,11},{4,12},{5,13},{6,14},{7,15},{8,0},{9,1},... | collective-permute-start | bytes 393224 | tf_op jit(solution)/shard_map/ppermute | solution.py:446
  84.8 7.2 %collective-permute-start.30 = (bf16[64,1024]{1,0:T(8,128)(2,1)S(1)}, bf16[64,1024]{1,0:T(8,128)(2,1)S(1)}, u32[]{:S(2)}, u32[]{:S(2)}) collective-permute-start(bf16[64,1024]{1,0:T(8,128)(2,1)S(1)} %gradient.31), channel_id=1, source_target_pairs={{0,16},{1,17},{2,18},{3,19},{4,20},{5,21},{6,22},{7,23},{8,24},{9,... | collective-permute-start | bytes 393224 | tf_op jit(solution)/shard_map/ppermute | solution.py:446
  88.0 6.5 %collective-permute-start.22 = (bf16[64,1024]{1,0:T(8,128)(2,1)S(1)}, bf16[64,1024]{1,0:T(8,128)(2,1)S(1)}, u32[]{:S(2)}, u32[]{:S(2)}) collective-permute-start(bf16[64,1024]{1,0:T(8,128)(2,1)S(1)} %pair_sum.24.left), channel_id=1, source_target_pairs={{0,16},{1,17},{2,18},{3,19},{4,20},{5,21},{6,22},{7,23},{8,24},{9,... | collective-permute-start | bytes 393224 | tf_op jit(solution)/shard_map/ppermute | solution.py:446
  89.3 6.4 %collective-permute-start.25 = (bf16[64,1024]{1,0:T(8,128)(2,1)S(1)}, bf16[64,1024]{1,0:T(8,128)(2,1)S(1)}, u32[]{:S(2)}, u32[]{:S(2)}) collective-permute-start(bf16[64,1024]{1,0:T(8,128)(2,1)S(1)} %pair_sum.26.left), channel_id=1, source_target_pairs={{0,8},{1,9},{2,10},{3,11},{4,12},{5,13},{6,14},{7,15},{8,0},{9,1},... | collective-permute-start | bytes 393224 | tf_op jit(solution)/shard_map/ppermute | solution.py:446
  90.4 6.4 %collective-permute-start.28 = (bf16[64,1024]{1,0:T(8,128)(2,1)S(1)}, bf16[64,1024]{1,0:T(8,128)(2,1)S(1)}, u32[]{:S(2)}, u32[]{:S(2)}) collective-permute-start(bf16[64,1024]{1,0:T(8,128)(2,1)S(1)} %pair_sum.28.left), channel_id=1, source_target_pairs={{0,16},{1,17},{2,18},{3,19},{4,20},{5,21},{6,22},{7,23},{8,24},{9,... | collective-permute-start | bytes 393224 | tf_op jit(solution)/shard_map/ppermute | solution.py:446
  92.0 6.5 %collective-permute-start.31 = (bf16[64,1024]{1,0:T(8,128)(2,1)S(1)}, bf16[64,1024]{1,0:T(8,128)(2,1)S(1)}, u32[]{:S(2)}, u32[]{:S(2)}) collective-permute-start(bf16[64,1024]{1,0:T(8,128)(2,1)S(1)} %pair_sum.30.left), channel_id=1, source_target_pairs={{0,8},{1,9},{2,10},{3,11},{4,12},{5,13},{6,14},{7,15},{8,0},{9,1},... | collective-permute-start | bytes 393224 | tf_op jit(solution)/shard_map/ppermute | solution.py:446
  94.5 8.0 %collective-permute-start.23 = (bf16[64,1024]{1,0:T(8,128)(2,1)S(1)}, bf16[64,1024]{1,0:T(8,128)(2,1)S(1)}, u32[]{:S(2)}, u32[]{:S(2)}) collective-permute-start(bf16[64,1024]{1,0:T(8,128)(2,1)S(1)} %pair_sum.25.refs_1_), channel_id=1, source_target_pairs={{0,8},{1,9},{2,10},{3,11},{4,12},{5,13},{6,14},{7,15},{8,0},{9,1},... | collective-permute-start | bytes 393224 | tf_op jit(solution)/shard_map/ppermute | solution.py:446
  95.7 6.8 %collective-permute-start.26 = (bf16[64,1024]{1,0:T(8,128)(2,1)S(1)}, bf16[64,1024]{1,0:T(8,128)(2,1)S(1)}, u32[]{:S(2)}, u32[]{:S(2)}) collective-permute-start(bf16[64,1024]{1,0:T(8,128)(2,1)S(1)} %pair_sum.27.refs_2_), channel_id=1, source_target_pairs={{0,16},{1,17},{2,18},{3,19},{4,20},{5,21},{6,22},{7,23},{8,24},{9,... | collective-permute-start | bytes 393224 | tf_op jit(solution)/shard_map/ppermute | solution.py:446
  96.8 5.9 %collective-permute-start.29 = (bf16[64,1024]{1,0:T(8,128)(2,1)S(1)}, bf16[64,1024]{1,0:T(8,128)(2,1)S(1)}, u32[]{:S(2)}, u32[]{:S(2)}) collective-permute-start(bf16[64,1024]{1,0:T(8,128)(2,1)S(1)} %pair_sum.29.refs_3_), channel_id=1, source_target_pairs={{0,8},{1,9},{2,10},{3,11},{4,12},{5,13},{6,14},{7,15},{8,0},{9,1},... | collective-permute-start | bytes 393224 | tf_op jit(solution)/shard_map/ppermute | solution.py:446
  98.5 5.0 %collective-permute-start.32 = (bf16[64,1024]{1,0:T(8,128)(2,1)S(1)}, bf16[64,1024]{1,0:T(8,128)(2,1)S(1)}, u32[]{:S(2)}, u32[]{:S(2)}) collective-permute-start(bf16[64,1024]{1,0:T(8,128)(2,1)S(1)} %pair_sum.31.refs_4_), channel_id=1, source_target_pairs={{0,16},{1,17},{2,18},{3,19},{4,20},{5,21},{6,22},{7,23},{8,24},{9,... | collective-permute-start | bytes 393224 | tf_op jit(solution)/shard_map/ppermute | solution.py:446
  108.1 6.8 %collective-permute-start.36 = (bf16[64,512]{1,0:T(8,128)(2,1)S(1)}, bf16[64,512]{1,0:T(8,128)(2,1)S(1)}, u32[]{:S(2)}, u32[]{:S(2)}) collective-permute-start(bf16[64,512]{1,0:T(8,128)(2,1)S(1)} %add_convert_fusion.refs_0_), channel_id=1, source_target_pairs={{0,6},{1,7},{2,4},{3,5},{4,2},{5,3},{6,0},{7,1},{8,14},{9,15},{10,... | collective-permute-start | bytes 196616 | tf_op jit(solution)/shard_map/ppermute | solution.py:432
  110.3 6.9 %collective-permute-start.35 = (bf16[64,512]{1,0:T(8,128)(2,1)S(1)}, bf16[64,512]{1,0:T(8,128)(2,1)S(1)}, u32[]{:S(2)}, u32[]{:S(2)}) collective-permute-start(bf16[64,512]{1,0:T(8,128)(2,1)S(1)} %add_convert_fusion.refs_0_), channel_id=1, source_target_pairs={{0,4},{1,5},{2,6},{3,7},{4,0},{5,1},{6,2},{7,3},{8,12},{9,13},{10,... | collective-permute-start | bytes 196616 | tf_op jit(solution)/shard_map/ppermute | solution.py:432
  110.7 6.5 %collective-permute-start.34 = (bf16[64,512]{1,0:T(8,128)(2,1)S(1)}, bf16[64,512]{1,0:T(8,128)(2,1)S(1)}, u32[]{:S(2)}, u32[]{:S(2)}) collective-permute-start(bf16[64,512]{1,0:T(8,128)(2,1)S(1)} %add_convert_fusion.refs_0_), channel_id=1, source_target_pairs={{0,2},{1,3},{2,0},{3,1},{4,6},{5,7},{6,4},{7,5},{8,10},{9,11},{10,... | collective-permute-start | bytes 196616 | tf_op jit(solution)/shard_map/ppermute | solution.py:432
  (13 other events, 74.8 us)

commit v3 on v2

--- a/solution.py
+++ b/solution.py
@@ -157,56 +157,52 @@
     )(doses, cloud, scalars)
 
 
-def residual_kernel(parts, people, chunks, scale, earlier, tail, gram, loglik_as, status, *refs):
-    sent, refs = refs[:parts], list(refs[parts:])
-    before = refs.pop(0) if earlier else None
-    half = people // 2
-    outcome = jnp.concatenate(
-        [
-            status[:, pl.ds(pl.multiple_of(chunk * people + core_of() * half, half), half)]
-            for chunk in chunks
-        ],
-        axis=1,
-    ).astype(F32)
-    share = half * len(chunks)
-    values = tree_sum([ref[...].astype(F32) for ref in sent])
-    logits = values[:, :share] * scale
-    residual = refs.pop(0)
-    residual[:, :share] = (outcome - jax.nn.sigmoid(logits)).astype(BF16)
-    if loglik_as or tail:
-        softplus = jnp.maximum(logits, 0.0) + jnp.log1p(jnp.exp(-jnp.abs(logits)))
-        loglik = jnp.sum(outcome * logits - softplus, axis=1, keepdims=True)
-        if earlier:
-            loglik = loglik + before[...]
-        if tail:
-            residual[:, share:] = as_lanes(loglik)
-        if loglik_as:
-            refs.pop(0)[...] = loglik if loglik_as == "column" else flipped(loglik)
-    if gram:
-        refs.pop(0)[...] = values[:, share:]
-
-
-def residual_of(scale, status, chunks, sent, earlier=None, tail=False, gram=False, loglik_as=None):
-    particles = sent[0].shape[0]
-    people = status.shape[1] // CHUNKS
-    share = people // 2 * len(chunks)
-    out_shape = [jax.ShapeDtypeStruct((particles, share + (LANES if tail else 0)), BF16)]
-    if loglik_as:
-        shape = (particles, 1) if loglik_as == "column" else (1, particles)
-        out_shape.append(jax.ShapeDtypeStruct(shape, F32))
-    if gram:
-        out_shape.append(jax.ShapeDtypeStruct((particles, LANES), F32))
-    operands = [status, *sent] + ([earlier] if earlier is not None else [])
+def residual_kernel(scale, tail, status, *refs):
+    sent, out = refs[:-1], refs[-1]
+    people = sent[0].shape[1]
+    outcome = outcome_of(status)
+    logits = tree_sum([ref[...].astype(F32) for ref in sent]) * scale
+    out[:, :people] = (outcome - jax.nn.sigmoid(logits)).astype(BF16)
+    if tail:
+        out[:, people:] = as_lanes(loglik_of(outcome, logits))
+
+
+def residual_of(scale, status, sent, tail=False):
+    particles, people = sent[0].shape
     return pl.pallas_call(
-        functools.partial(
-            residual_kernel, len(sent), people, chunks, scale, earlier is not None, tail, gram, loglik_as
-        ),
-        in_specs=[VMEM] * len(operands),
-        out_specs=[VMEM] * len(out_shape),
-        out_shape=out_shape,
-        compiler_params=params(12),
+        functools.partial(residual_kernel, scale, tail),
+        in_specs=[VMEM] * (1 + len(sent)),
+        out_specs=VMEM,
+        out_shape=jax.ShapeDtypeStruct((particles, people + (LANES if tail else 0)), BF16),
+        compiler_params=params(8),
         name="residual",
-    )(*operands)
+    )(status, *sent)
+
+
+def outcome_of(status):
+    half = status.shape[1] // 2
+    return status[:, pl.ds(pl.multiple_of(core_of() * half, half), half)].astype(F32)
+
+
+def loglik_of(outcome, logits):
+    softplus = jnp.maximum(logits, 0.0) + jnp.log1p(jnp.exp(-jnp.abs(logits)))
+    return jnp.sum(outcome * logits - softplus, axis=1, keepdims=True)
+
+
+def last_loglik_kernel(scale, status, *refs):
+    logits = tree_sum([ref[...].astype(F32) for ref in refs[:-1]]) * scale
+    refs[-1][...] = flipped(loglik_of(outcome_of(status), logits))
+
+
+def last_loglik(scale, status, sent):
+    return pl.pallas_call(
+        functools.partial(last_loglik_kernel, scale),
+        in_specs=[VMEM] * (1 + len(sent)),
+        out_specs=VMEM,
+        out_shape=jax.ShapeDtypeStruct((1, sent[0].shape[0]), F32),
+        compiler_params=params(8),
+        name="last_loglik",
+    )(status, *sent)
 
 
 def gradient_kernel(count, which, piece, tail, *refs):
@@ -289,7 +285,7 @@
     return log_weights, weights, total / total_variants + 1e-06
 
 
-def update_kernel(which, move, total_variants, scalars, flags, noise, *refs):
+def update_kernel(which, move, total_variants, chips, scalars, flags, noise, *refs):
     refs = list(refs)
     centered = [refs.pop(0) for _ in range(CHUNKS)]
     grads = [refs.pop(0) for _ in range(PIECES)]
@@ -301,7 +297,8 @@
     heat = (scalars[:, 0:1] + advance) * float(total_variants) ** (-0.5)
     approved = flipped(flags[move : move + 1, :].astype(F32)) > 0.5
     if start_first and which == KEEP:
-        gram, arrived, held = refs.pop(0), refs.pop(0), refs.pop(0)
+        gram = tree_sum([refs.pop(0)[...] for _ in range(chips)])
+        arrived, held = refs.pop(0), refs.pop(0)
     elif start_first:
         weights, factor = refs.pop(0)[...], refs.pop(0)[...]
     else:
@@ -315,7 +312,7 @@
         if which == KEEP:
             log_weights_out, weights_out, factor_out = refs.pop(0), refs.pop(0), refs.pop(0)
             loglik = from_lanes(held[:, columns // PIECES :]) + from_lanes(arrived[:, columns // PIECES :])
-            log_weights, weights, mean_spread = weigh(total_variants, advance, loglik, gram[...])
+            log_weights, weights, mean_spread = weigh(total_variants, advance, loglik, gram)
             log_weights_out[...] = flipped(log_weights)
             weights_out[...] = weights
             factor = scalars[:, 2:3] / mean_spread
@@ -415,7 +412,7 @@
     if moved is not None:
         specs[-1] = HBM
     return pl.pallas_call(
-        functools.partial(update_kernel, which, move, total_variants),
+        functools.partial(update_kernel, which, move, total_variants, lax.axis_size("col") // 2),
         in_specs=specs,
         out_specs=[HBM if last else VMEM] + [VMEM] * (len(out_shape) - 1),
         out_shape=out_shape,
@@ -454,20 +451,8 @@
     )
 
 
-def over_chips(mine, other, link):
-    mine = (mine + swap(other, "col", 1)).astype(link)
+def over_chips(mine):
     return [mine] + [swap(mine, "col", d) for d in range(2, lax.axis_size("col"), 2)]
-
-
-def over_chips_by_stages(mine, other):
-    mine = mine + swap(other, "col", 1)
-    size = lax.axis_size("col")
-    bits = [1 << b for b in range(1, size.bit_length() - 1)]
-    for stage, order in enumerate(zip(bits, bits[::-1])):
-        arrived = lax.ppermute(mine, "col", [(i, i ^ order[i % 2]) for i in range(size)])
-        if stage < len(bits) - 1:
-            mine = mine + arrived
-    return [mine, arrived]
 
 
 def sum_small(value):
@@ -493,32 +478,13 @@
     status = disease_status.reshape(1, people)
     scalars = jnp.concatenate([present_heat, heat_advance, drift_magnitude])[None, :]
 
-    centered, pairs, loglik, gram, sent = [], [], None, None, None
-    for chunk in range(CHUNKS + 1):
-        if chunk < CHUNKS:
-            part, mine, other = center_and_first_logits(chunk, allele_doses, walker_cloud, scalars)
-            centered.append(part)
-        if chunk > 0:
-            if chunk < CHUNKS:
-                (mine, other), sent = lax.optimization_barrier(((mine, other), sent))
-            tail = chunk == CHUNKS
-            own, *extra = residual_of(
-                scale,
-                status,
-                (chunk - 1,),
-                sent,
-                earlier=loglik,
-                tail=tail,
-                gram=chunk == 1,
-                loglik_as=None if tail else "column",
-            )
-            if chunk == 1:
-                gram = extra.pop()
-            if not tail:
-                (loglik,) = extra
-            pairs += [own, swap(own, "col", 1)]
-        if chunk < CHUNKS:
-            sent = over_chips_by_stages(mine, other)
+    part, mine, other = center_and_first_logits(0, allele_doses, walker_cloud, scalars)
+    centered = [part]
+    mine = mine + swap(other, "col", 1)
+    sent = over_chips((mine[:, : people // 2] * scale).astype(jnp.float16))
+    own = residual_of(1.0, status, [tree_sum([each.astype(F32) for each in sent])], tail=True)
+    pairs = [own, swap(own, "col", 1)]
+    gram = mine[:, people // 2 :]
 
     width = variants // 2 // PIECES
     fixed = (scalars, approval_flags, normal_perturbations)
@@ -532,6 +498,9 @@
             for piece in pieces
         ]
         held = [gradient(KEEP, piece, pairs, centered, tails[piece]) for piece in pieces]
+        if first:
+            gram, held = lax.optimization_barrier((gram, held))
+            grams = over_chips(gram)
         for stage in range(1, stages):
             held = [pair_sum(width, *each) for each in zip(tails, held, arrived)]
             arrived = [swap_over_rows(each, piece, stage) for piece, each in enumerate(held)]
@@ -540,7 +509,7 @@
         if first:
             c_kept, size_kept, log_weights, weights, factor, total = update(
                 KEEP, move, total_variants, fixed, centered, summed, walker_cloud,
-                [gram, arrived[0], held[0]], None, None,
+                [*grams, arrived[0], held[0]], None, None,
             )
             c_sent, size_sent, mine, other = update(
                 SEND, move, total_variants, fixed, centered, arriving, walker_cloud,
@@ -553,14 +522,11 @@
             moved, mine, other = update(
                 SEND, move, total_variants, fixed, centered, arriving, c_sent, [size_sent], total, moved
             )
-        sent = over_chips(mine, other, BF16)
+        sent = over_chips((mine + swap(other, "col", 1)).astype(BF16))
         if first:
-            (own,) = residual_of(scale, status, tuple(range(CHUNKS)), sent)
+            own = residual_of(scale, status, sent)
             pairs = [own, swap(own, "col", 1)]
-        else:
-            _, loglik = residual_of(
-                scale, status, tuple(range(CHUNKS)), sent, loglik_as="row"
-            )
+    loglik = last_loglik(scale, status, sent)
     mean_loglik = sum_small(loglik) / total_people
     return (moved, log_weights[0], mean_loglik[0])
 

time: 126 us -> 120 us (0.952)
  waiting for transfers between devices: 38.6 us -> 29.4 us
  starting transfers between devices: 46 us -> 49.7 us
    ppermute x15 -> x21, starting transfers between devices: 13.4 us -> 23.2 us  [swap(): return lax.ppermute(value, axis, [(i, i ^ distance) for i in range(size)])]
    ppermute x2 -> x0, waiting for transfers between devices: 8.52 us -> none  [over_chips_by_stages(): lax.ppermute(mine, 'col', [(i, i ^ order[i % 2]) for i in range(size)])]
    ppermute x24, waiting for transfers between devices: 10.8 us -> 4.28 us  [swap_over_rows(): lax.ppermute(value, ('row', 'col'), [(row * columns + col, (row ^ order[p...]
    ppermute x15 -> x21, waiting for transfers between devices: 19.3 us -> 25.2 us  [swap(): return lax.ppermute(value, axis, [(i, i ^ distance) for i in range(size)])]
    ppermute x2 -> x0, starting transfers between devices: 5.58 us -> none  [over_chips_by_stages(): lax.ppermute(mine, 'col', [(i, i ^ order[i % 2]) for i in range(size)])]
  transfers between devices with their start and end apart: 41 -> 45, of which waited for: 21 -> 23; matrix products, arithmetic and copies ran while one was open for 0% -> 0% of each run, Pallas kernels for 11% -> 12%
where the time goes in v3:
time: 120 us
  starting transfers between devices  49.7 us (41%)
  Pallas kernels  35.2 us (29%)
  waiting for transfers between devices  29.4 us (24%)
  between operations  2.98 us (2%)
  local copies, waits for them, and re-layouts  1.61 us (1%)
    ppermute x24, starting transfers between devices, swap_over_rows(): lax.ppermute(value, ('row', 'col'), [(row * columns + col, (row ^ order[p...  26.5 us
    ppermute x21, waiting for transfers between devices, swap(): return lax.ppermute(value, axis, [(i, i ^ distance) for i in range(size)])  25.2 us
    ppermute x21, starting transfers between devices, swap(): return lax.ppermute(value, axis, [(i, i ^ distance) for i in range(size)])  23.2 us
    pallas_call x1, Pallas kernels, center_and_first_logits(): pl.pallas_call(functools.partial(center_kernel, block, with_gram), grid=(...  13.1 us
    pallas_call x4, Pallas kernels, update(): pl.pallas_call(functools.partial(update_kernel, which, move, total_varian...  13 us
    pallas_call x16, Pallas kernels, gradient(): pl.pallas_call(functools.partial(gradient_kernel, len(pairs) // 2, which,...  8.08 us
    ppermute x24, waiting for transfers between devices, swap_over_rows(): lax.ppermute(value, ('row', 'col'), [(row * columns + col, (row ^ order[p...  4.28 us
  transfers between devices with their start and end apart: 45, of which 23 were waited for; matrix products, arithmetic and copies ran while one was open for 0% of the time, Pallas kernels for 12%

profile of v3, /device:TPU:0, one launch (start us, length us, event | category | flops | bytes accessed | tf_op | source)
XLA Modules:
  0.0 119.7 jit_solution(9821821793906964168)
XLA Ops:
  2.6 1.6 %copy-done.1 = f32[64,8192]{1,0:T(8,128)S(1)} copy-done((f32[64,8192]{1,0:T(8,128)S(1)}, f32[64,8192]{1,0:T(8,128)}, u32[]{:S(2)}) %copy-start.1) | copy-done | bytes 2097176
  4.2 13.1 %center_and_first_logits.1 = (bf16[1024,8192]{1,0:T(8,128)(2,1)S(1)}, f32[64,640]{1,0:T(8,128)S(1)}, f32[64,640]{1,0:T(8,128)S(1)}) custom-call(s32[1024,8192]{1,0:T(8,128)} %doses.1, f32[64,8192]{1,0:T(8,128)S(1)} %copy-done.1, f32[1,3]{1,0:T(1,128)S(1)} %maximum_bitcast_fusion._.scalars), custom_call_target="tpu_custom_call" | custom-call | flops 8589934592 | tf_op jit(solution)/shard_map/center_and_first_logits/pallas_call | solution.py:139
  18.9 4.0 %collective-permute-start.2 = (f16[64,512]{1,0:T(8,128)(2,1)S(1)}, f16[64,512]{1,0:T(8,128)(2,1)S(1)}, u32[]{:S(2)}, u32[]{:S(2)}) collective-permute-start(f16[64,512]{1,0:T(8,128)(2,1)S(1)} %fusion), channel_id=1, source_target_pairs={{0,4},{1,5},{2,6},{3,7},{4,0},{5,1},{6,2},{7,3},{8,12},{9,13},{10,... | collective-permute-start | bytes 196616 | tf_op jit(solution)/shard_map/ppermute | solution.py:429
  22.9 1.6 %collective-permute-start.1 = (f16[64,512]{1,0:T(8,128)(2,1)S(1)}, f16[64,512]{1,0:T(8,128)(2,1)S(1)}, u32[]{:S(2)}, u32[]{:S(2)}) collective-permute-start(f16[64,512]{1,0:T(8,128)(2,1)S(1)} %fusion), channel_id=1, source_target_pairs={{0,2},{1,3},{2,0},{3,1},{4,6},{5,7},{6,4},{7,5},{8,10},{9,11},{10,... | collective-permute-start | bytes 196616 | tf_op jit(solution)/shard_map/ppermute | solution.py:429
  24.5 1.8 %collective-permute-done.2 = f16[64,512]{1,0:T(8,128)(2,1)S(1)} collective-permute-done((f16[64,512]{1,0:T(8,128)(2,1)S(1)}, f16[64,512]{1,0:T(8,128)(2,1)S(1)}, u32[]{:S(2)}, u32[]{:S(2)}) %collective-permute-start.2) | collective-permute-done | bytes 65568 | tf_op jit(solution)/shard_map/ppermute | solution.py:429
  27.2 3.4 %collective-permute-done.3 = f16[64,512]{1,0:T(8,128)(2,1)S(1)} collective-permute-done((f16[64,512]{1,0:T(8,128)(2,1)S(1)}, f16[64,512]{1,0:T(8,128)(2,1)S(1)}, u32[]{:S(2)}, u32[]{:S(2)}) %collective-permute-start.3) | collective-permute-done | bytes 65568 | tf_op jit(solution)/shard_map/ppermute | solution.py:429
  32.6 1.6 %collective-permute-start.8 = (bf16[64,1024]{1,0:T(8,128)(2,1)S(1)}, bf16[64,1024]{1,0:T(8,128)(2,1)S(1)}, u32[]{:S(2)}, u32[]{:S(2)}) collective-permute-start(bf16[64,1024]{1,0:T(8,128)(2,1)S(1)} %gradient.21), channel_id=1, source_target_pairs={{0,16},{1,17},{2,18},{3,19},{4,20},{5,21},{6,22},{7,23},{8,24},{9,... | collective-permute-start | bytes 393224 | tf_op jit(solution)/shard_map/ppermute | solution.py:443
  34.7 1.6 %collective-permute-start.11 = (bf16[64,1024]{1,0:T(8,128)(2,1)S(1)}, bf16[64,1024]{1,0:T(8,128)(2,1)S(1)}, u32[]{:S(2)}, u32[]{:S(2)}) collective-permute-start(bf16[64,1024]{1,0:T(8,128)(2,1)S(1)} %gradient.22), channel_id=1, source_target_pairs={{0,8},{1,9},{2,10},{3,11},{4,12},{5,13},{6,14},{7,15},{8,0},{9,1},... | collective-permute-start | bytes 393224 | tf_op jit(solution)/shard_map/ppermute | solution.py:443
  40.5 1.6 %collective-permute-start.9 = (bf16[64,1024]{1,0:T(8,128)(2,1)S(1)}, bf16[64,1024]{1,0:T(8,128)(2,1)S(1)}, u32[]{:S(2)}, u32[]{:S(2)}) collective-permute-start(bf16[64,1024]{1,0:T(8,128)(2,1)S(1)} %pair_sum.18.left), channel_id=1, source_target_pairs={{0,8},{1,9},{2,10},{3,11},{4,12},{5,13},{6,14},{7,15},{8,0},{9,1},... | collective-permute-start | bytes 393224 | tf_op jit(solution)/shard_map/ppermute | solution.py:443
  42.1 1.6 %collective-permute-start.12 = (bf16[64,1024]{1,0:T(8,128)(2,1)S(1)}, bf16[64,1024]{1,0:T(8,128)(2,1)S(1)}, u32[]{:S(2)}, u32[]{:S(2)}) collective-permute-start(bf16[64,1024]{1,0:T(8,128)(2,1)S(1)} %pair_sum.20.left), channel_id=1, source_target_pairs={{0,16},{1,17},{2,18},{3,19},{4,20},{5,21},{6,22},{7,23},{8,24},{9,... | collective-permute-start | bytes 393224 | tf_op jit(solution)/shard_map/ppermute | solution.py:443
  48.2 2.1 %collective-permute-start.17 = (f32[64,128]{1,0:T(8,128)S(1)}, f32[64,128]{1,0:T(8,128)S(1)}, u32[]{:S(2)}, u32[]{:S(2)}) collective-permute-start(f32[64,128]{1,0:T(8,128)S(1)} %slice.8.refs_6_), channel_id=1, source_target_pairs={{0,2},{1,3},{2,0},{3,1},{4,6},{5,7},{6,4},{7,5},{8,10},{9,11},{10,... | collective-permute-start | bytes 98312 | tf_op jit(solution)/shard_map/ppermute | solution.py:429
  50.7 1.8 %collective-permute-start.10 = (bf16[64,1024]{1,0:T(8,128)(2,1)S(1)}, bf16[64,1024]{1,0:T(8,128)(2,1)S(1)}, u32[]{:S(2)}, u32[]{:S(2)}) collective-permute-start(bf16[64,1024]{1,0:T(8,128)(2,1)S(1)} %pair_sum.19.refs_2_), channel_id=1, source_target_pairs={{0,16},{1,17},{2,18},{3,19},{4,20},{5,21},{6,22},{7,23},{8,24},{9,... | collective-permute-start | bytes 393224 | tf_op jit(solution)/shard_map/ppermute | solution.py:443
  55.0 3.3 %update_and_logits.4 = (f32[64,4096]{1,0:T(8,128)S(1)}, f32[1,4096]{1,0:T(1,128)S(1)}, f32[1,64]{1,0:T(1,128)}, f32[64,1]{1,0:T(8,128)S(1)}, f32[1,1]{1,0:T(1,128)}, /*index=5*/f32[1024,64]{1,0:T(8,128)S(1)}) custom-call(f32[1,3]{1,0:T(1,128)S(1)} %maximum_bitcast_fusion._.scalars, s32[2,64]{1,0:T(2,128)S(1)} %copy-done.3, f32[2,64,8192]{2,1,0:T(8,128)S(1)} %copy-done, ...), custom_call_target="tpu_custom_call" | custom-call | flops 2147483648 | tf_op jit(solution)/shard_map/update_and_logits/pallas_call | solution.py:414
  59.5 3.5 %update_and_logits.5 = (f32[64,4096]{1,0:T(8,128)S(1)}, f32[1,4096]{1,0:T(1,128)S(1)}, f32[64,512]{1,0:T(8,128)S(1)}, f32[64,512]{1,0:T(8,128)S(1)}) custom-call(f32[1,3]{1,0:T(1,128)S(1)} %maximum_bitcast_fusion._.scalars, s32[2,64]{1,0:T(2,128)S(1)} %copy-done.3, f32[2,64,8192]{2,1,0:T(8,128)S(1)} %copy-done, ...), custom_call_target="tpu_custom_call" | custom-call | flops 2147483648 | tf_op jit(solution)/shard_map/update_and_logits/pallas_call | solution.py:414
  66.0 2.9 %collective-permute-start.21 = (bf16[64,512]{1,0:T(8,128)(2,1)S(1)}, bf16[64,512]{1,0:T(8,128)(2,1)S(1)}, u32[]{:S(2)}, u32[]{:S(2)}) collective-permute-start(bf16[64,512]{1,0:T(8,128)(2,1)S(1)} %add_convert_fusion.1.refs_0_), channel_id=1, source_target_pairs={{0,2},{1,3},{2,0},{3,1},{4,6},{5,7},{6,4},{7,5},{8,10},{9,11},{10,... | collective-permute-start | bytes 196616 | tf_op jit(solution)/shard_map/ppermute | solution.py:429
  68.9 2.4 %collective-permute-done.23.refs_3_ = bf16[64,512]{1,0:T(8,128)(2,1)S(1)} collective-permute-done((bf16[64,512]{1,0:T(8,128)(2,1)S(1)}, bf16[64,512]{1,0:T(8,128)(2,1)S(1)}, u32[]{:S(2)}, u32[]{:S(2)}) %collective-permute-start.23) | collective-permute-done | bytes 65568 | tf_op jit(solution)/shard_map/ppermute | solution.py:429
  71.3 2.0 %collective-permute-done.22.refs_2_ = bf16[64,512]{1,0:T(8,128)(2,1)S(1)} collective-permute-done((bf16[64,512]{1,0:T(8,128)(2,1)S(1)}, bf16[64,512]{1,0:T(8,128)(2,1)S(1)}, u32[]{:S(2)}, u32[]{:S(2)}) %collective-permute-start.22) | collective-permute-done | bytes 65568 | tf_op jit(solution)/shard_map/ppermute | solution.py:429
  76.1 1.9 %collective-permute-start.28 = (bf16[64,1024]{1,0:T(8,128)(2,1)S(1)}, bf16[64,1024]{1,0:T(8,128)(2,1)S(1)}, u32[]{:S(2)}, u32[]{:S(2)}) collective-permute-start(bf16[64,1024]{1,0:T(8,128)(2,1)S(1)} %gradient.27), channel_id=1, source_target_pairs={{0,16},{1,17},{2,18},{3,19},{4,20},{5,21},{6,22},{7,23},{8,24},{9,... | collective-permute-start | bytes 393224 | tf_op jit(solution)/shard_map/ppermute | solution.py:443
  84.2 1.4 %collective-permute-start.29 = (bf16[64,1024]{1,0:T(8,128)(2,1)S(1)}, bf16[64,1024]{1,0:T(8,128)(2,1)S(1)}, u32[]{:S(2)}, u32[]{:S(2)}) collective-permute-start(bf16[64,1024]{1,0:T(8,128)(2,1)S(1)} %pair_sum.26.left), channel_id=1, source_target_pairs={{0,8},{1,9},{2,10},{3,11},{4,12},{5,13},{6,14},{7,15},{8,0},{9,1},... | collective-permute-start | bytes 393224 | tf_op jit(solution)/shard_map/ppermute | solution.py:443
  86.0 1.7 %collective-permute-start.35 = (bf16[64,1024]{1,0:T(8,128)(2,1)S(1)}, bf16[64,1024]{1,0:T(8,128)(2,1)S(1)}, u32[]{:S(2)}, u32[]{:S(2)}) collective-permute-start(bf16[64,1024]{1,0:T(8,128)(2,1)S(1)} %pair_sum.30.left), channel_id=1, source_target_pairs={{0,8},{1,9},{2,10},{3,11},{4,12},{5,13},{6,14},{7,15},{8,0},{9,1},... | collective-permute-start | bytes 393224 | tf_op jit(solution)/shard_map/ppermute | solution.py:443
  87.6 2.0 %collective-permute-done.26.right = bf16[64,1024]{1,0:T(8,128)(2,1)S(1)} collective-permute-done((bf16[64,1024]{1,0:T(8,128)(2,1)S(1)}, bf16[64,1024]{1,0:T(8,128)(2,1)S(1)}, u32[]{:S(2)}, u32[]{:S(2)}) %collective-permute-start.26) | collective-permute-done | bytes 131104 | tf_op jit(solution)/shard_map/ppermute | solution.py:443
  90.4 1.5 %collective-permute-start.30 = (bf16[64,1024]{1,0:T(8,128)(2,1)S(1)}, bf16[64,1024]{1,0:T(8,128)(2,1)S(1)}, u32[]{:S(2)}, u32[]{:S(2)}) collective-permute-start(bf16[64,1024]{1,0:T(8,128)(2,1)S(1)} %pair_sum.27.refs_2_), channel_id=1, source_target_pairs={{0,16},{1,17},{2,18},{3,19},{4,20},{5,21},{6,22},{7,23},{8,24},{9,... | collective-permute-start | bytes 393224 | tf_op jit(solution)/shard_map/ppermute | solution.py:443
  92.8 1.9 %collective-permute-start.36 = (bf16[64,1024]{1,0:T(8,128)(2,1)S(1)}, bf16[64,1024]{1,0:T(8,128)(2,1)S(1)}, u32[]{:S(2)}, u32[]{:S(2)}) collective-permute-start(bf16[64,1024]{1,0:T(8,128)(2,1)S(1)} %pair_sum.31.refs_4_), channel_id=1, source_target_pairs={{0,16},{1,17},{2,18},{3,19},{4,20},{5,21},{6,22},{7,23},{8,24},{9,... | collective-permute-start | bytes 393224 | tf_op jit(solution)/shard_map/ppermute | solution.py:443
  94.7 3.1 %update_and_logits.6 = (f32[64,8192]{1,0:T(8,128)}, f32[1024,64]{1,0:T(8,128)S(1)}) custom-call(f32[1,3]{1,0:T(1,128)S(1)} %maximum_bitcast_fusion._.scalars, s32[2,64]{1,0:T(2,128)S(1)} %copy-done.3, f32[2,64,8192]{2,1,0:T(8,128)S(1)} %copy-done, bf16[1024,8192]{1,0:T(8,128)(2,1)S(1)} %get-tuple-element.26.refs_2_.refs_0_, ...), custom_call_target="tpu_custom_call" | custom-call | flops 2147483648 | tf_op jit(solution)/shard_map/update_and_logits/pallas_call | solution.py:414
  97.8 3.1 %update_and_logits.7 = (f32[64,8192]{1,0:T(8,128)}, f32[64,512]{1,0:T(8,128)S(1)}, f32[64,512]{1,0:T(8,128)S(1)}) custom-call(f32[1,3]{1,0:T(1,128)S(1)} %maximum_bitcast_fusion._.scalars, s32[2,64]{1,0:T(2,128)S(1)} %copy-done.3, f32[2,64,8192]{2,1,0:T(8,128)S(1)} %copy-done, ...), custom_call_target="tpu_custom_call", output_to_operand_aliasing={{0}: (11, {})} | custom-call | flops 2147483648 | tf_op jit(solution)/shard_map/update_and_logits/pallas_call | solution.py:414
  102.4 2.5 %collective-permute-start.40 = (bf16[64,512]{1,0:T(8,128)(2,1)S(1)}, bf16[64,512]{1,0:T(8,128)(2,1)S(1)}, u32[]{:S(2)}, u32[]{:S(2)}) collective-permute-start(bf16[64,512]{1,0:T(8,128)(2,1)S(1)} %add_convert_fusion.refs_0_), channel_id=1, source_target_pairs={{0,6},{1,7},{2,4},{3,5},{4,2},{5,3},{6,0},{7,1},{8,14},{9,15},{10,... | collective-permute-start | bytes 196616 | tf_op jit(solution)/shard_map/ppermute | solution.py:429
  104.9 2.0 %collective-permute-start.38 = (bf16[64,512]{1,0:T(8,128)(2,1)S(1)}, bf16[64,512]{1,0:T(8,128)(2,1)S(1)}, u32[]{:S(2)}, u32[]{:S(2)}) collective-permute-start(bf16[64,512]{1,0:T(8,128)(2,1)S(1)} %add_convert_fusion.refs_0_), channel_id=1, source_target_pairs={{0,2},{1,3},{2,0},{3,1},{4,6},{5,7},{6,4},{7,5},{8,10},{9,11},{10,... | collective-permute-start | bytes 196616 | tf_op jit(solution)/shard_map/ppermute | solution.py:429
  106.8 2.4 %collective-permute-done.40.refs_3_ = bf16[64,512]{1,0:T(8,128)(2,1)S(1)} collective-permute-done((bf16[64,512]{1,0:T(8,128)(2,1)S(1)}, bf16[64,512]{1,0:T(8,128)(2,1)S(1)}, u32[]{:S(2)}, u32[]{:S(2)}) %collective-permute-start.40) | collective-permute-done | bytes 65568 | tf_op jit(solution)/shard_map/ppermute | solution.py:429
  109.2 2.0 %collective-permute-done.39.refs_2_ = bf16[64,512]{1,0:T(8,128)(2,1)S(1)} collective-permute-done((bf16[64,512]{1,0:T(8,128)(2,1)S(1)}, bf16[64,512]{1,0:T(8,128)(2,1)S(1)}, u32[]{:S(2)}, u32[]{:S(2)}) %collective-permute-start.39) | collective-permute-done | bytes 65568 | tf_op jit(solution)/shard_map/ppermute | solution.py:429
  112.6 1.7 %collective-permute-start.44 = (f32[1,64]{1,0:T(1,128)S(1)}, f32[1,64]{1,0:T(1,128)S(1)}, u32[]{:S(2)}, u32[]{:S(2)}) collective-permute-start(f32[1,64]{1,0:T(1,128)S(1)} %add.36), channel_id=1, source_target_pairs={{0,24},{8,16},{16,8},{24,0},{1,25},{9,17},{17,9},{25,1},{2,26},{10... | collective-permute-start | bytes 776 | tf_op jit(solution)/shard_map/ppermute | solution.py:429
  114.3 1.4 %collective-permute-start.43 = (f32[1,64]{1,0:T(1,128)S(1)}, f32[1,64]{1,0:T(1,128)S(1)}, u32[]{:S(2)}, u32[]{:S(2)}) collective-permute-start(f32[1,64]{1,0:T(1,128)S(1)} %add.36), channel_id=1, source_target_pairs={{0,16},{8,24},{16,0},{24,8},{1,17},{9,25},{17,1},{25,9},{2,18},{10... | collective-permute-start | bytes 776 | tf_op jit(solution)/shard_map/ppermute | solution.py:429
  117.8 1.4 %collective-permute-done.42 = f32[1,64]{1,0:T(1,128)S(1)} collective-permute-done((f32[1,64]{1,0:T(1,128)S(1)}, f32[1,64]{1,0:T(1,128)S(1)}, u32[]{:S(2)}, u32[]{:S(2)}) %collective-permute-start.42) | collective-permute-done | bytes 288 | tf_op jit(solution)/shard_map/ppermute | solution.py:429
  (115 shorter events, 37.4 us)
Async XLA Ops:
  18.9 7.4 %collective-permute-start.2 = (f16[64,512]{1,0:T(8,128)(2,1)S(1)}, f16[64,512]{1,0:T(8,128)(2,1)S(1)}, u32[]{:S(2)}, u32[]{:S(2)}) collective-permute-start(f16[64,512]{1,0:T(8,128)(2,1)S(1)} %fusion), channel_id=1, source_target_pairs={{0,4},{1,5},{2,6},{3,7},{4,0},{5,1},{6,2},{7,3},{8,12},{9,13},{10,... | collective-permute-start | bytes 196616 | tf_op jit(solution)/shard_map/ppermute | solution.py:429
  24.5 6.1 %collective-permute-start.3 = (f16[64,512]{1,0:T(8,128)(2,1)S(1)}, f16[64,512]{1,0:T(8,128)(2,1)S(1)}, u32[]{:S(2)}, u32[]{:S(2)}) collective-permute-start(f16[64,512]{1,0:T(8,128)(2,1)S(1)} %fusion), channel_id=1, source_target_pairs={{0,6},{1,7},{2,4},{3,5},{4,2},{5,3},{6,0},{7,1},{8,14},{9,15},{10,... | collective-permute-start | bytes 196616 | tf_op jit(solution)/shard_map/ppermute | solution.py:429
  32.6 7.9 %collective-permute-start.8 = (bf16[64,1024]{1,0:T(8,128)(2,1)S(1)}, bf16[64,1024]{1,0:T(8,128)(2,1)S(1)}, u32[]{:S(2)}, u32[]{:S(2)}) collective-permute-start(bf16[64,1024]{1,0:T(8,128)(2,1)S(1)} %gradient.21), channel_id=1, source_target_pairs={{0,16},{1,17},{2,18},{3,19},{4,20},{5,21},{6,22},{7,23},{8,24},{9,... | collective-permute-start | bytes 393224 | tf_op jit(solution)/shard_map/ppermute | solution.py:443
  34.7 7.4 %collective-permute-start.11 = (bf16[64,1024]{1,0:T(8,128)(2,1)S(1)}, bf16[64,1024]{1,0:T(8,128)(2,1)S(1)}, u32[]{:S(2)}, u32[]{:S(2)}) collective-permute-start(bf16[64,1024]{1,0:T(8,128)(2,1)S(1)} %gradient.22), channel_id=1, source_target_pairs={{0,8},{1,9},{2,10},{3,11},{4,12},{5,13},{6,14},{7,15},{8,0},{9,1},... | collective-permute-start | bytes 393224 | tf_op jit(solution)/shard_map/ppermute | solution.py:443
  36.7 8.8 %collective-permute-start.14 = (bf16[64,1024]{1,0:T(8,128)(2,1)S(1)}, bf16[64,1024]{1,0:T(8,128)(2,1)S(1)}, u32[]{:S(2)}, u32[]{:S(2)}) collective-permute-start(bf16[64,1024]{1,0:T(8,128)(2,1)S(1)} %gradient.23), channel_id=1, source_target_pairs={{0,16},{1,17},{2,18},{3,19},{4,20},{5,21},{6,22},{7,23},{8,24},{9,... | collective-permute-start | bytes 393224 | tf_op jit(solution)/shard_map/ppermute | solution.py:443
  37.8 6.4 %collective-permute-start.5 = (bf16[64,1152]{1,0:T(8,128)(2,1)S(1)}, bf16[64,1152]{1,0:T(8,128)(2,1)S(1)}, u32[]{:S(2)}, u32[]{:S(2)}) collective-permute-start(bf16[64,1152]{1,0:T(8,128)(2,1)S(1)} %gradient.20), channel_id=1, source_target_pairs={{0,8},{1,9},{2,10},{3,11},{4,12},{5,13},{6,14},{7,15},{8,0},{9,1},... | collective-permute-start | bytes 442376 | tf_op jit(solution)/shard_map/ppermute | solution.py:443
  40.5 6.7 %collective-permute-start.9 = (bf16[64,1024]{1,0:T(8,128)(2,1)S(1)}, bf16[64,1024]{1,0:T(8,128)(2,1)S(1)}, u32[]{:S(2)}, u32[]{:S(2)}) collective-permute-start(bf16[64,1024]{1,0:T(8,128)(2,1)S(1)} %pair_sum.18.left), channel_id=1, source_target_pairs={{0,8},{1,9},{2,10},{3,11},{4,12},{5,13},{6,14},{7,15},{8,0},{9,1},... | collective-permute-start | bytes 393224 | tf_op jit(solution)/shard_map/ppermute | solution.py:443
  42.1 6.1 %collective-permute-start.12 = (bf16[64,1024]{1,0:T(8,128)(2,1)S(1)}, bf16[64,1024]{1,0:T(8,128)(2,1)S(1)}, u32[]{:S(2)}, u32[]{:S(2)}) collective-permute-start(bf16[64,1024]{1,0:T(8,128)(2,1)S(1)} %pair_sum.20.left), channel_id=1, source_target_pairs={{0,16},{1,17},{2,18},{3,19},{4,20},{5,21},{6,22},{7,23},{8,24},{9,... | collective-permute-start | bytes 393224 | tf_op jit(solution)/shard_map/ppermute | solution.py:443
  44.4 8.2 %collective-permute-start.6 = (bf16[64,1152]{1,0:T(8,128)(2,1)S(1)}, bf16[64,1152]{1,0:T(8,128)(2,1)S(1)}, u32[]{:S(2)}, u32[]{:S(2)}) collective-permute-start(bf16[64,1152]{1,0:T(8,128)(2,1)S(1)} %pair_sum.16.left.refs_11_), channel_id=1, source_target_pairs={{0,16},{1,17},{2,18},{3,19},{4,20},{5,21},{6,22},{7,23},{8,24},{9,... | collective-permute-start | bytes 442376 | tf_op jit(solution)/shard_map/ppermute | solution.py:443
  45.6 5.0 %collective-permute-start.15 = (bf16[64,1024]{1,0:T(8,128)(2,1)S(1)}, bf16[64,1024]{1,0:T(8,128)(2,1)S(1)}, u32[]{:S(2)}, u32[]{:S(2)}) collective-permute-start(bf16[64,1024]{1,0:T(8,128)(2,1)S(1)} %pair_sum.22.left), channel_id=1, source_target_pairs={{0,8},{1,9},{2,10},{3,11},{4,12},{5,13},{6,14},{7,15},{8,0},{9,1},... | collective-permute-start | bytes 393224 | tf_op jit(solution)/shard_map/ppermute | solution.py:443
  45.9 7.3 %collective-permute-start.19 = (f32[64,128]{1,0:T(8,128)S(1)}, f32[64,128]{1,0:T(8,128)S(1)}, u32[]{:S(2)}, u32[]{:S(2)}) collective-permute-start(f32[64,128]{1,0:T(8,128)S(1)} %slice.8.refs_6_), channel_id=1, source_target_pairs={{0,6},{1,7},{2,4},{3,5},{4,2},{5,3},{6,0},{7,1},{8,14},{9,15},{10,... | collective-permute-start | bytes 98312 | tf_op jit(solution)/shard_map/ppermute | solution.py:429
  47.2 7.3 %collective-permute-start.18 = (f32[64,128]{1,0:T(8,128)S(1)}, f32[64,128]{1,0:T(8,128)S(1)}, u32[]{:S(2)}, u32[]{:S(2)}) collective-permute-start(f32[64,128]{1,0:T(8,128)S(1)} %slice.8.refs_6_), channel_id=1, source_target_pairs={{0,4},{1,5},{2,6},{3,7},{4,0},{5,1},{6,2},{7,3},{8,12},{9,13},{10,... | collective-permute-start | bytes 98312 | tf_op jit(solution)/shard_map/ppermute | solution.py:429
  48.2 6.7 %collective-permute-start.17 = (f32[64,128]{1,0:T(8,128)S(1)}, f32[64,128]{1,0:T(8,128)S(1)}, u32[]{:S(2)}, u32[]{:S(2)}) collective-permute-start(f32[64,128]{1,0:T(8,128)S(1)} %slice.8.refs_6_), channel_id=1, source_target_pairs={{0,2},{1,3},{2,0},{3,1},{4,6},{5,7},{6,4},{7,5},{8,10},{9,11},{10,... | collective-permute-start | bytes 98312 | tf_op jit(solution)/shard_map/ppermute | solution.py:429
  50.7 7.6 %collective-permute-start.10 = (bf16[64,1024]{1,0:T(8,128)(2,1)S(1)}, bf16[64,1024]{1,0:T(8,128)(2,1)S(1)}, u32[]{:S(2)}, u32[]{:S(2)}) collective-permute-start(bf16[64,1024]{1,0:T(8,128)(2,1)S(1)} %pair_sum.19.refs_2_), channel_id=1, source_target_pairs={{0,16},{1,17},{2,18},{3,19},{4,20},{5,21},{6,22},{7,23},{8,24},{9,... | collective-permute-start | bytes 393224 | tf_op jit(solution)/shard_map/ppermute | solution.py:443
  52.5 5.7 %collective-permute-start.13 = (bf16[64,1024]{1,0:T(8,128)(2,1)S(1)}, bf16[64,1024]{1,0:T(8,128)(2,1)S(1)}, u32[]{:S(2)}, u32[]{:S(2)}) collective-permute-start(bf16[64,1024]{1,0:T(8,128)(2,1)S(1)} %pair_sum.21.refs_3_), channel_id=1, source_target_pairs={{0,8},{1,9},{2,10},{3,11},{4,12},{5,13},{6,14},{7,15},{8,0},{9,1},... | collective-permute-start | bytes 393224 | tf_op jit(solution)/shard_map/ppermute | solution.py:443
  64.5 6.9 %collective-permute-start.23 = (bf16[64,512]{1,0:T(8,128)(2,1)S(1)}, bf16[64,512]{1,0:T(8,128)(2,1)S(1)}, u32[]{:S(2)}, u32[]{:S(2)}) collective-permute-start(bf16[64,512]{1,0:T(8,128)(2,1)S(1)} %add_convert_fusion.1.refs_0_), channel_id=1, source_target_pairs={{0,6},{1,7},{2,4},{3,5},{4,2},{5,3},{6,0},{7,1},{8,14},{9,15},{10,... | collective-permute-start | bytes 196616 | tf_op jit(solution)/shard_map/ppermute | solution.py:429
  65.8 7.5 %collective-permute-start.22 = (bf16[64,512]{1,0:T(8,128)(2,1)S(1)}, bf16[64,512]{1,0:T(8,128)(2,1)S(1)}, u32[]{:S(2)}, u32[]{:S(2)}) collective-permute-start(bf16[64,512]{1,0:T(8,128)(2,1)S(1)} %add_convert_fusion.1.refs_0_), channel_id=1, source_target_pairs={{0,4},{1,5},{2,6},{3,7},{4,0},{5,1},{6,2},{7,3},{8,12},{9,13},{10,... | collective-permute-start | bytes 196616 | tf_op jit(solution)/shard_map/ppermute | solution.py:429
  66.0 7.3 %collective-permute-start.21 = (bf16[64,512]{1,0:T(8,128)(2,1)S(1)}, bf16[64,512]{1,0:T(8,128)(2,1)S(1)}, u32[]{:S(2)}, u32[]{:S(2)}) collective-permute-start(bf16[64,512]{1,0:T(8,128)(2,1)S(1)} %add_convert_fusion.1.refs_0_), channel_id=1, source_target_pairs={{0,2},{1,3},{2,0},{3,1},{4,6},{5,7},{6,4},{7,5},{8,10},{9,11},{10,... | collective-permute-start | bytes 196616 | tf_op jit(solution)/shard_map/ppermute | solution.py:429
  75.2 8.0 %collective-permute-start.25 = (bf16[64,1024]{1,0:T(8,128)(2,1)S(1)}, bf16[64,1024]{1,0:T(8,128)(2,1)S(1)}, u32[]{:S(2)}, u32[]{:S(2)}) collective-permute-start(bf16[64,1024]{1,0:T(8,128)(2,1)S(1)} %gradient.25), channel_id=1, source_target_pairs={{0,8},{1,9},{2,10},{3,11},{4,12},{5,13},{6,14},{7,15},{8,0},{9,1},... | collective-permute-start | bytes 393224 | tf_op jit(solution)/shard_map/ppermute | solution.py:443
  76.1 8.0 %collective-permute-start.28 = (bf16[64,1024]{1,0:T(8,128)(2,1)S(1)}, bf16[64,1024]{1,0:T(8,128)(2,1)S(1)}, u32[]{:S(2)}, u32[]{:S(2)}) collective-permute-start(bf16[64,1024]{1,0:T(8,128)(2,1)S(1)} %gradient.27), channel_id=1, source_target_pairs={{0,16},{1,17},{2,18},{3,19},{4,20},{5,21},{6,22},{7,23},{8,24},{9,... | collective-permute-start | bytes 393224 | tf_op jit(solution)/shard_map/ppermute | solution.py:443
  78.5 7.1 %collective-permute-start.31 = (bf16[64,1024]{1,0:T(8,128)(2,1)S(1)}, bf16[64,1024]{1,0:T(8,128)(2,1)S(1)}, u32[]{:S(2)}, u32[]{:S(2)}) collective-permute-start(bf16[64,1024]{1,0:T(8,128)(2,1)S(1)} %gradient.29), channel_id=1, source_target_pairs={{0,8},{1,9},{2,10},{3,11},{4,12},{5,13},{6,14},{7,15},{8,0},{9,1},... | collective-permute-start | bytes 393224 | tf_op jit(solution)/shard_map/ppermute | solution.py:443
  79.9 6.0 %collective-permute-start.34 = (bf16[64,1024]{1,0:T(8,128)(2,1)S(1)}, bf16[64,1024]{1,0:T(8,128)(2,1)S(1)}, u32[]{:S(2)}, u32[]{:S(2)}) collective-permute-start(bf16[64,1024]{1,0:T(8,128)(2,1)S(1)} %gradient.31), channel_id=1, source_target_pairs={{0,16},{1,17},{2,18},{3,19},{4,20},{5,21},{6,22},{7,23},{8,24},{9,... | collective-permute-start | bytes 393224 | tf_op jit(solution)/shard_map/ppermute | solution.py:443
  83.2 6.4 %collective-permute-start.26 = (bf16[64,1024]{1,0:T(8,128)(2,1)S(1)}, bf16[64,1024]{1,0:T(8,128)(2,1)S(1)}, u32[]{:S(2)}, u32[]{:S(2)}) collective-permute-start(bf16[64,1024]{1,0:T(8,128)(2,1)S(1)} %pair_sum.24.left), channel_id=1, source_target_pairs={{0,16},{1,17},{2,18},{3,19},{4,20},{5,21},{6,22},{7,23},{8,24},{9,... | collective-permute-start | bytes 393224 | tf_op jit(solution)/shard_map/ppermute | solution.py:443
  84.2 6.2 %collective-permute-start.29 = (bf16[64,1024]{1,0:T(8,128)(2,1)S(1)}, bf16[64,1024]{1,0:T(8,128)(2,1)S(1)}, u32[]{:S(2)}, u32[]{:S(2)}) collective-permute-start(bf16[64,1024]{1,0:T(8,128)(2,1)S(1)} %pair_sum.26.left), channel_id=1, source_target_pairs={{0,8},{1,9},{2,10},{3,11},{4,12},{5,13},{6,14},{7,15},{8,0},{9,1},... | collective-permute-start | bytes 393224 | tf_op jit(solution)/shard_map/ppermute | solution.py:443
  85.7 6.2 %collective-permute-start.32 = (bf16[64,1024]{1,0:T(8,128)(2,1)S(1)}, bf16[64,1024]{1,0:T(8,128)(2,1)S(1)}, u32[]{:S(2)}, u32[]{:S(2)}) collective-permute-start(bf16[64,1024]{1,0:T(8,128)(2,1)S(1)} %pair_sum.28.left), channel_id=1, source_target_pairs={{0,16},{1,17},{2,18},{3,19},{4,20},{5,21},{6,22},{7,23},{8,24},{9,... | collective-permute-start | bytes 393224 | tf_op jit(solution)/shard_map/ppermute | solution.py:443
  86.0 6.8 %collective-permute-start.35 = (bf16[64,1024]{1,0:T(8,128)(2,1)S(1)}, bf16[64,1024]{1,0:T(8,128)(2,1)S(1)}, u32[]{:S(2)}, u32[]{:S(2)}) collective-permute-start(bf16[64,1024]{1,0:T(8,128)(2,1)S(1)} %pair_sum.30.left), channel_id=1, source_target_pairs={{0,8},{1,9},{2,10},{3,11},{4,12},{5,13},{6,14},{7,15},{8,0},{9,1},... | collective-permute-start | bytes 393224 | tf_op jit(solution)/shard_map/ppermute | solution.py:443
  89.6 8.1 %collective-permute-start.27 = (bf16[64,1024]{1,0:T(8,128)(2,1)S(1)}, bf16[64,1024]{1,0:T(8,128)(2,1)S(1)}, u32[]{:S(2)}, u32[]{:S(2)}) collective-permute-start(bf16[64,1024]{1,0:T(8,128)(2,1)S(1)} %pair_sum.25.refs_1_), channel_id=1, source_target_pairs={{0,8},{1,9},{2,10},{3,11},{4,12},{5,13},{6,14},{7,15},{8,0},{9,1},... | collective-permute-start | bytes 393224 | tf_op jit(solution)/shard_map/ppermute | solution.py:443
  90.4 7.4 %collective-permute-start.30 = (bf16[64,1024]{1,0:T(8,128)(2,1)S(1)}, bf16[64,1024]{1,0:T(8,128)(2,1)S(1)}, u32[]{:S(2)}, u32[]{:S(2)}) collective-permute-start(bf16[64,1024]{1,0:T(8,128)(2,1)S(1)} %pair_sum.27.refs_2_), channel_id=1, source_target_pairs={{0,16},{1,17},{2,18},{3,19},{4,20},{5,21},{6,22},{7,23},{8,24},{9,... | collective-permute-start | bytes 393224 | tf_op jit(solution)/shard_map/ppermute | solution.py:443
  91.9 5.9 %collective-permute-start.33 = (bf16[64,1024]{1,0:T(8,128)(2,1)S(1)}, bf16[64,1024]{1,0:T(8,128)(2,1)S(1)}, u32[]{:S(2)}, u32[]{:S(2)}) collective-permute-start(bf16[64,1024]{1,0:T(8,128)(2,1)S(1)} %pair_sum.29.refs_3_), channel_id=1, source_target_pairs={{0,8},{1,9},{2,10},{3,11},{4,12},{5,13},{6,14},{7,15},{8,0},{9,1},... | collective-permute-start | bytes 393224 | tf_op jit(solution)/shard_map/ppermute | solution.py:443
  102.4 6.8 %collective-permute-start.40 = (bf16[64,512]{1,0:T(8,128)(2,1)S(1)}, bf16[64,512]{1,0:T(8,128)(2,1)S(1)}, u32[]{:S(2)}, u32[]{:S(2)}) collective-permute-start(bf16[64,512]{1,0:T(8,128)(2,1)S(1)} %add_convert_fusion.refs_0_), channel_id=1, source_target_pairs={{0,6},{1,7},{2,4},{3,5},{4,2},{5,3},{6,0},{7,1},{8,14},{9,15},{10,... | collective-permute-start | bytes 196616 | tf_op jit(solution)/shard_map/ppermute | solution.py:429
  104.9 6.3 %collective-permute-start.39 = (bf16[64,512]{1,0:T(8,128)(2,1)S(1)}, bf16[64,512]{1,0:T(8,128)(2,1)S(1)}, u32[]{:S(2)}, u32[]{:S(2)}) collective-permute-start(bf16[64,512]{1,0:T(8,128)(2,1)S(1)} %add_convert_fusion.refs_0_), channel_id=1, source_target_pairs={{0,4},{1,5},{2,6},{3,7},{4,0},{5,1},{6,2},{7,3},{8,12},{9,13},{10,... | collective-permute-start | bytes 196616 | tf_op jit(solution)/shard_map/ppermute | solution.py:429
  104.9 6.3 %collective-permute-start.38 = (bf16[64,512]{1,0:T(8,128)(2,1)S(1)}, bf16[64,512]{1,0:T(8,128)(2,1)S(1)}, u32[]{:S(2)}, u32[]{:S(2)}) collective-permute-start(bf16[64,512]{1,0:T(8,128)(2,1)S(1)} %add_convert_fusion.refs_0_), channel_id=1, source_target_pairs={{0,2},{1,3},{2,0},{3,1},{4,6},{5,7},{6,4},{7,5},{8,10},{9,11},{10,... | collective-permute-start | bytes 196616 | tf_op jit(solution)/shard_map/ppermute | solution.py:429
  (17 other events, 97.0 us)

commit v4 on v3

--- a/solution.py
+++ b/solution.py
@@ -17,6 +17,7 @@
 KEEP, SEND = 0, 1
 MIB = 1 << 20
 LANES = 128
+LOW_FACTOR = 2048.0
 CHUNKS = 1
 PIECES = 4
 
@@ -82,7 +83,7 @@
     return jnp.sum(lanes.astype(F32), axis=1, keepdims=True)
 
 
-def center_kernel(block, with_gram, doses, cloud, _, centered, mine, other, cloud_bf, logits, gram):
+def center_kernel(block, scale, total_variants, doses, cloud, _, centered, mine, other, cloud_bf, logits, gram):
     step = pl.program_id(0)
     variants = doses.shape[1]
     people = logits.shape[1]
@@ -92,21 +93,18 @@
     def _():
         cloud_bf[...] = cloud[...].astype(BF16)
 
-    if with_gram:
-
-        @pl.when(step == 0)
-        def _():
-            width = tile_of(variants, 1024)
-            total = None
-            for start in range(0, variants, width):
-                c = cloud[:, start : start + width]
-                c = c - jnp.mean(c, axis=0, keepdims=True)
-                high = c.astype(BF16)
-                low = (c - high.astype(F32)).astype(BF16)
-                term = rows_dot(high, high) + 2.0 * rows_dot(high, low)
-                total = term if total is None else total + term
-            gram[...] = jnp.zeros(gram.shape, F32)
-            gram[:, : total.shape[1]] = total
+    @pl.when(step == 0)
+    def _():
+        width = tile_of(variants, 1024)
+        total = None
+        for start in range(0, variants, width):
+            c = cloud[:, start : start + width]
+            c = c - jnp.mean(c, axis=0, keepdims=True)
+            high = c.astype(BF16)
+            low = (c - high.astype(F32)).astype(BF16)
+            term = rows_dot(high, high) + 2.0 * rows_dot(high, low)
+            total = term if total is None else total + term
+        gram[...] = total * (1.0 / total_variants)
 
     width = tile_of(variants, 2048)
     total = None
@@ -120,27 +118,24 @@
     @pl.when(step == pl.num_programs(0) - 1)
     def _():
         first = core_of()
-        mine[:, :half] = logits[:, pl.ds(pl.multiple_of(first * half, half), half)]
-        other[:, :half] = logits[:, pl.ds(pl.multiple_of((1 - first) * half, half), half)]
-        if with_gram:
-            mine[:, half:] = gram[...]
-            other[:, half:] = gram[...]
-
-
-def center_and_first_logits(chunk, doses, cloud, scalars):
+        for which, out in ((first, mine), (1 - first, other)):
+            out[:, :half] = logits[:, pl.ds(pl.multiple_of(which * half, half), half)] * scale
+            out[:, half : half + LANES // 2] = gram[...]
+            out[:, half + LANES // 2 :] = gram[...]
+
+
+def center_and_first_logits(scale, total_variants, doses, cloud, scalars):
     variants = doses.shape[1]
-    people = doses.shape[0] // CHUNKS
+    people = doses.shape[0]
     particles = cloud.shape[0]
     block = min(256, people)
     steps = people // block
-    with_gram = chunk == 0
-    lanes = people // 2 + (LANES if with_gram else 0)
-    exchanged = jax.ShapeDtypeStruct((particles, lanes), F32)
-    return pl.pallas_call(
-        functools.partial(center_kernel, block, with_gram),
+    exchanged = jax.ShapeDtypeStruct((particles, people // 2 + LANES), F32)
+    return pl.pallas_call(
+        functools.partial(center_kernel, block, scale, total_variants),
         grid=(steps,),
         in_specs=[
-            pl.BlockSpec((block, variants), lambda i: (chunk * steps + i, 0)),
+            pl.BlockSpec((block, variants), lambda i: (i, 0)),
             pl.BlockSpec((particles, variants), lambda i: (0, 0), pipeline_mode=pl.Buffered(1)),
             VMEM,
         ],
@@ -149,7 +144,7 @@
         scratch_shapes=[
             pltpu.VMEM((particles, variants), BF16),
             pltpu.VMEM((particles, people), F32),
-            pltpu.VMEM((particles, LANES), F32),
+            pltpu.VMEM((particles, particles), F32),
         ],
         compiler_params=params(28),
         cost_estimate=cost(16 * particles * people * variants),
@@ -157,23 +152,45 @@
     )(doses, cloud, scalars)
 
 
-def residual_kernel(scale, tail, status, *refs):
-    sent, out = refs[:-1], refs[-1]
-    people = sent[0].shape[1]
+def first_residual_kernel(status, values, out, gram):
+    people = status.shape[1] // 2
+    particles = gram.shape[0]
+    logits = values[:, :people]
     outcome = outcome_of(status)
-    logits = tree_sum([ref[...].astype(F32) for ref in sent]) * scale
     out[:, :people] = (outcome - jax.nn.sigmoid(logits)).astype(BF16)
-    if tail:
-        out[:, people:] = as_lanes(loglik_of(outcome, logits))
-
-
-def residual_of(scale, status, sent, tail=False):
-    particles, people = sent[0].shape
-    return pl.pallas_call(
-        functools.partial(residual_kernel, scale, tail),
+    out[:, people:] = as_lanes(loglik_of(outcome, logits))
+    middle = people + LANES // 2
+    gram[...] = values[:, people : people + particles] + values[:, middle : middle + particles] * (
+        1.0 / LOW_FACTOR
+    )
+
+
+def first_residual_of(status, values):
+    particles = values.shape[0]
+    return pl.pallas_call(
+        first_residual_kernel,
+        in_specs=[VMEM, VMEM],
+        out_specs=[VMEM, VMEM],
+        out_shape=[
+            jax.ShapeDtypeStruct(values.shape, BF16),
+            jax.ShapeDtypeStruct((particles, particles), F32),
+        ],
+        compiler_params=params(8),
+        name="first_residual",
+    )(status, values)
+
+
+def residual_kernel(scale, status, *refs):
+    logits = tree_sum([ref[...].astype(F32) for ref in refs[:-1]]) * scale
+    refs[-1][...] = (outcome_of(status) - jax.nn.sigmoid(logits)).astype(BF16)
+
+
+def residual_of(scale, status, sent):
+    return pl.pallas_call(
+        functools.partial(residual_kernel, scale),
         in_specs=[VMEM] * (1 + len(sent)),
         out_specs=VMEM,
-        out_shape=jax.ShapeDtypeStruct((particles, people + (LANES if tail else 0)), BF16),
+        out_shape=jax.ShapeDtypeStruct(sent[0].shape, BF16),
         compiler_params=params(8),
         name="residual",
     )(status, *sent)
@@ -269,7 +286,7 @@
     )(left, right)
 
 
-def weigh(total_variants, heat_advance, loglik, gram):
+def weigh(heat_advance, loglik, gram):
     scaled = heat_advance * loglik
     clipped = jnp.maximum(scaled - jnp.max(scaled, axis=0, keepdims=True), -CLIP_FLOOR)
     log_weights = clipped - jnp.log(jnp.sum(jnp.exp(clipped), axis=0, keepdims=True))
@@ -282,10 +299,10 @@
     square = jnp.sum(jnp.where(diagonal, gram * weights, 0.0), axis=0, keepdims=True)
     mixed = jnp.sum(weights * gram, axis=0, keepdims=True) * flipped(weights)
     total = jnp.sum(square - mixed, axis=1, keepdims=True)
-    return log_weights, weights, total / total_variants + 1e-06
-
-
-def update_kernel(which, move, total_variants, chips, scalars, flags, noise, *refs):
+    return log_weights, weights, total + 1e-06
+
+
+def update_kernel(which, move, total_variants, scalars, flags, noise, *refs):
     refs = list(refs)
     centered = [refs.pop(0) for _ in range(CHUNKS)]
     grads = [refs.pop(0) for _ in range(PIECES)]
@@ -297,8 +314,7 @@
     heat = (scalars[:, 0:1] + advance) * float(total_variants) ** (-0.5)
     approved = flipped(flags[move : move + 1, :].astype(F32)) > 0.5
     if start_first and which == KEEP:
-        gram = tree_sum([refs.pop(0)[...] for _ in range(chips)])
-        arrived, held = refs.pop(0), refs.pop(0)
+        gram, arrived, held = refs.pop(0), refs.pop(0), refs.pop(0)
     elif start_first:
         weights, factor = refs.pop(0)[...], refs.pop(0)[...]
     else:
@@ -312,7 +328,7 @@
         if which == KEEP:
             log_weights_out, weights_out, factor_out = refs.pop(0), refs.pop(0), refs.pop(0)
             loglik = from_lanes(held[:, columns // PIECES :]) + from_lanes(arrived[:, columns // PIECES :])
-            log_weights, weights, mean_spread = weigh(total_variants, advance, loglik, gram)
+            log_weights, weights, mean_spread = weigh(advance, loglik, gram[...])
             log_weights_out[...] = flipped(log_weights)
             weights_out[...] = weights
             factor = scalars[:, 2:3] / mean_spread
@@ -412,7 +428,7 @@
     if moved is not None:
         specs[-1] = HBM
     return pl.pallas_call(
-        functools.partial(update_kernel, which, move, total_variants, lax.axis_size("col") // 2),
+        functools.partial(update_kernel, which, move, total_variants),
         in_specs=specs,
         out_specs=[HBM if last else VMEM] + [VMEM] * (len(out_shape) - 1),
         out_shape=out_shape,
@@ -434,6 +450,18 @@
     while len(values) > 1:
         values = [values[i] + values[i + 1] for i in range(0, len(values), 2)]
     return values[0]
+
+
+def after(value, earlier):
+    return value if earlier is None else lax.optimization_barrier((value, earlier))[0]
+
+
+def pair_sums(tails, held, arrived, width):
+    sums = []
+    for piece, tail in enumerate(tails):
+        there = after(arrived[piece], sums[-1] if sums else None)
+        sums.append(pair_sum(width, tail, held[piece], there))
+    return sums
 
 
 def swap_over_rows(value, piece, stage):
@@ -478,13 +506,19 @@
     status = disease_status.reshape(1, people)
     scalars = jnp.concatenate([present_heat, heat_advance, drift_magnitude])[None, :]
 
-    part, mine, other = center_and_first_logits(0, allele_doses, walker_cloud, scalars)
+    part, mine, other = center_and_first_logits(
+        scale, total_variants, allele_doses, walker_cloud, scalars
+    )
     centered = [part]
-    mine = mine + swap(other, "col", 1)
-    sent = over_chips((mine[:, : people // 2] * scale).astype(jnp.float16))
-    own = residual_of(1.0, status, [tree_sum([each.astype(F32) for each in sent])], tail=True)
+    high, low = people // 2, people // 2 + LANES // 2
+    values = mine + swap(other, "col", 1)
+    lane = lax.broadcasted_iota(jnp.int32, values.shape, 1)
+    rounded = lax.reduce_precision(values, exponent_bits=5, mantissa_bits=10)
+    rest = (values - rounded) * LOW_FACTOR
+    values = jnp.where(lane < high, values, jnp.where(lane < low, rounded, rest))
+    sent = over_chips(values.astype(jnp.float16))
+    own, gram = first_residual_of(status, tree_sum([each.astype(F32) for each in sent]))
     pairs = [own, swap(own, "col", 1)]
-    gram = mine[:, people // 2 :]
 
     width = variants // 2 // PIECES
     fixed = (scalars, approval_flags, normal_perturbations)
@@ -493,23 +527,28 @@
     for move in range(2):
         first = move == 0
         tails = [first and piece == 0 for piece in pieces]
-        arrived = [
-            swap_over_rows(gradient(SEND, piece, pairs, centered, tails[piece]), piece, 0)
-            for piece in pieces
-        ]
-        held = [gradient(KEEP, piece, pairs, centered, tails[piece]) for piece in pieces]
-        if first:
-            gram, held = lax.optimization_barrier((gram, held))
-            grams = over_chips(gram)
+        sent_away = []
+        for piece in pieces:
+            there = after(pairs, sent_away[-1] if sent_away else None)
+            sent_away.append(gradient(SEND, piece, there, centered, tails[piece]))
+        arrived = [swap_over_rows(each, piece, 0) for piece, each in enumerate(sent_away)]
         for stage in range(1, stages):
-            held = [pair_sum(width, *each) for each in zip(tails, held, arrived)]
+            if stage == 1:
+                held = []
+                for piece in pieces:
+                    there = after(pairs, held[piece - 2] if piece > 1 else sent_away[-1])
+                    kept = gradient(KEEP, piece, there, centered, tails[piece])
+                    there = after(arrived[piece], held[-1] if held else None)
+                    held.append(pair_sum(width, tails[piece], kept, there))
+            else:
+                held = pair_sums(tails, held, arrived, width)
             arrived = [swap_over_rows(each, piece, stage) for piece, each in enumerate(held)]
-        summed = [pair_sum(width, False, *each) for each in zip(held, arrived)]
+        summed = pair_sums([False] * PIECES, held, arrived, width)
         arriving = [swap_over_rows(each, piece, 0) for piece, each in enumerate(summed)]
         if first:
             c_kept, size_kept, log_weights, weights, factor, total = update(
                 KEEP, move, total_variants, fixed, centered, summed, walker_cloud,
-                [*grams, arrived[0], held[0]], None, None,
+                [gram, arrived[0], held[0]], None, None,
             )
             c_sent, size_sent, mine, other = update(
                 SEND, move, total_variants, fixed, centered, arriving, walker_cloud,

time: 120 us -> 117 us (0.975)
  starting transfers between devices: 49.7 us -> 46 us
    ppermute x21 -> x18, starting transfers between devices: 23.2 us -> 19 us  [swap(): return lax.ppermute(value, axis, [(i, i ^ distance) for i in range(size)])]
    ppermute x21 -> x18, waiting for transfers between devices: 25.2 us -> 25.5 us  [swap(): return lax.ppermute(value, axis, [(i, i ^ distance) for i in range(size)])]
  transfers between devices with their start and end apart: 45 -> 42, of which waited for: 23 -> 20; matrix products, arithmetic and copies ran while one was open for 0% -> 0% of each run, Pallas kernels for 12% -> 12%
where the time goes in v4:
time: 117 us
  starting transfers between devices  46 us (39%)
  Pallas kernels  35.1 us (30%)
  waiting for transfers between devices  30.2 us (26%)
  between operations  2.93 us (3%)
  local copies, waits for them, and re-layouts  1.61 us (1%)
    ppermute x24, starting transfers between devices, swap_over_rows(): lax.ppermute(value, ('row', 'col'), [(row * columns + col, (row ^ order[p...  27 us
    ppermute x18, waiting for transfers between devices, swap(): return lax.ppermute(value, axis, [(i, i ^ distance) for i in range(size)])  25.5 us
    ppermute x18, starting transfers between devices, swap(): return lax.ppermute(value, axis, [(i, i ^ distance) for i in range(size)])  19 us
    pallas_call x1, Pallas kernels, center_and_first_logits(): pl.pallas_call(functools.partial(center_kernel, block, scale, total_varia...  13.1 us
    pallas_call x4, Pallas kernels, update(): pl.pallas_call(functools.partial(update_kernel, which, move, total_varian...  12.9 us
    pallas_call x16, Pallas kernels, gradient(): pl.pallas_call(functools.partial(gradient_kernel, len(pairs) // 2, which,...  8.05 us
    ppermute x24, waiting for transfers between devices, swap_over_rows(): lax.ppermute(value, ('row', 'col'), [(row * columns + col, (row ^ order[p...  4.73 us
  transfers between devices with their start and end apart: 42, of which 20 were waited for; matrix products, arithmetic and copies ran while one was open for 0% of the time, Pallas kernels for 12%

profile of v4, /device:TPU:0, one launch (start us, length us, event | category | flops | bytes accessed | tf_op | source)
XLA Modules:
  0.0 116.7 jit_solution(13693673034254716281)
XLA Ops:
  2.6 1.6 %copy-done.1 = f32[64,8192]{1,0:T(8,128)S(1)} copy-done((f32[64,8192]{1,0:T(8,128)S(1)}, f32[64,8192]{1,0:T(8,128)}, u32[]{:S(2)}) %copy-start.1) | copy-done | bytes 2097176
  4.2 13.1 %center_and_first_logits.1 = (bf16[1024,8192]{1,0:T(8,128)(2,1)S(1)}, f32[64,640]{1,0:T(8,128)S(1)}, f32[64,640]{1,0:T(8,128)S(1)}) custom-call(s32[1024,8192]{1,0:T(8,128)} %doses.1, f32[64,8192]{1,0:T(8,128)S(1)} %copy-done.1, f32[1,3]{1,0:T(1,128)S(1)} %maximum_bitcast_fusion._.scalars), custom_call_target="tpu_custom_call" | custom-call | flops 8589934592 | tf_op jit(solution)/shard_map/center_and_first_logits/pallas_call | solution.py:134
  19.0 5.0 %collective-permute-start.3 = (f16[64,640]{1,0:T(8,128)(2,1)S(1)}, f16[64,640]{1,0:T(8,128)(2,1)S(1)}, u32[]{:S(2)}, u32[]{:S(2)}) collective-permute-start(f16[64,640]{1,0:T(8,128)(2,1)S(1)} %fusion.1), channel_id=1, source_target_pairs={{0,6},{1,7},{2,4},{3,5},{4,2},{5,3},{6,0},{7,1},{8,14},{9,15},{10,... | collective-permute-start | bytes 245768 | tf_op jit(solution)/shard_map/ppermute | solution.py:445
  24.7 2.7 %collective-permute-done.3 = f16[64,640]{1,0:T(8,128)(2,1)S(1)} collective-permute-done((f16[64,640]{1,0:T(8,128)(2,1)S(1)}, f16[64,640]{1,0:T(8,128)(2,1)S(1)}, u32[]{:S(2)}, u32[]{:S(2)}) %collective-permute-start.3) | collective-permute-done | bytes 81952 | tf_op jit(solution)/shard_map/ppermute | solution.py:445
  27.4 3.8 %collective-permute-done.2 = f16[64,640]{1,0:T(8,128)(2,1)S(1)} collective-permute-done((f16[64,640]{1,0:T(8,128)(2,1)S(1)}, f16[64,640]{1,0:T(8,128)(2,1)S(1)}, u32[]{:S(2)}, u32[]{:S(2)}) %collective-permute-start.2) | collective-permute-done | bytes 81952 | tf_op jit(solution)/shard_map/ppermute | solution.py:445
  33.3 1.6 %collective-permute-start.5 = (bf16[64,1152]{1,0:T(8,128)(2,1)S(1)}, bf16[64,1152]{1,0:T(8,128)(2,1)S(1)}, u32[]{:S(2)}, u32[]{:S(2)}) collective-permute-start(bf16[64,1152]{1,0:T(8,128)(2,1)S(1)} %gradient.16), channel_id=1, source_target_pairs={{0,8},{1,9},{2,10},{3,11},{4,12},{5,13},{6,14},{7,15},{8,0},{9,1},... | collective-permute-start | bytes 442376 | tf_op jit(solution)/shard_map/ppermute | solution.py:471
  35.3 1.6 %collective-permute-start.8 = (bf16[64,1024]{1,0:T(8,128)(2,1)S(1)}, bf16[64,1024]{1,0:T(8,128)(2,1)S(1)}, u32[]{:S(2)}, u32[]{:S(2)}) collective-permute-start(bf16[64,1024]{1,0:T(8,128)(2,1)S(1)} %gradient.17), channel_id=1, source_target_pairs={{0,16},{1,17},{2,18},{3,19},{4,20},{5,21},{6,22},{7,23},{8,24},{9,... | collective-permute-start | bytes 393224 | tf_op jit(solution)/shard_map/ppermute | solution.py:471
  40.2 1.6 %collective-permute-start.6 = (bf16[64,1152]{1,0:T(8,128)(2,1)S(1)}, bf16[64,1152]{1,0:T(8,128)(2,1)S(1)}, u32[]{:S(2)}, u32[]{:S(2)}) collective-permute-start(bf16[64,1152]{1,0:T(8,128)(2,1)S(1)} %pair_sum.16.left.refs_8_), channel_id=1, source_target_pairs={{0,16},{1,17},{2,18},{3,19},{4,20},{5,21},{6,22},{7,23},{8,24},{9,... | collective-permute-start | bytes 442376 | tf_op jit(solution)/shard_map/ppermute | solution.py:471
  41.9 1.6 %collective-permute-start.9 = (bf16[64,1024]{1,0:T(8,128)(2,1)S(1)}, bf16[64,1024]{1,0:T(8,128)(2,1)S(1)}, u32[]{:S(2)}, u32[]{:S(2)}) collective-permute-start(bf16[64,1024]{1,0:T(8,128)(2,1)S(1)} %pair_sum.18.left), channel_id=1, source_target_pairs={{0,8},{1,9},{2,10},{3,11},{4,12},{5,13},{6,14},{7,15},{8,0},{9,1},... | collective-permute-start | bytes 393224 | tf_op jit(solution)/shard_map/ppermute | solution.py:471
  45.1 1.6 %collective-permute-start.15 = (bf16[64,1024]{1,0:T(8,128)(2,1)S(1)}, bf16[64,1024]{1,0:T(8,128)(2,1)S(1)}, u32[]{:S(2)}, u32[]{:S(2)}) collective-permute-start(bf16[64,1024]{1,0:T(8,128)(2,1)S(1)} %pair_sum.22.left), channel_id=1, source_target_pairs={{0,8},{1,9},{2,10},{3,11},{4,12},{5,13},{6,14},{7,15},{8,0},{9,1},... | collective-permute-start | bytes 393224 | tf_op jit(solution)/shard_map/ppermute | solution.py:471
  46.7 1.4 %collective-permute-done.6.right.refs_7_ = bf16[64,1152]{1,0:T(8,128)(2,1)S(1)} collective-permute-done((bf16[64,1152]{1,0:T(8,128)(2,1)S(1)}, bf16[64,1152]{1,0:T(8,128)(2,1)S(1)}, u32[]{:S(2)}, u32[]{:S(2)}) %collective-permute-start.6) | collective-permute-done | bytes 147488 | tf_op jit(solution)/shard_map/ppermute | solution.py:471
  48.1 1.4 %collective-permute-start.7 = (bf16[64,1024]{1,0:T(8,128)(2,1)S(1)}, bf16[64,1024]{1,0:T(8,128)(2,1)S(1)}, u32[]{:S(2)}, u32[]{:S(2)}) collective-permute-start(bf16[64,1024]{1,0:T(8,128)(2,1)S(1)} %pair_sum.17.refs_1_), channel_id=1, source_target_pairs={{0,8},{1,9},{2,10},{3,11},{4,12},{5,13},{6,14},{7,15},{8,0},{9,1},... | collective-permute-start | bytes 393224 | tf_op jit(solution)/shard_map/ppermute | solution.py:471
  50.1 1.5 %collective-permute-start.13 = (bf16[64,1024]{1,0:T(8,128)(2,1)S(1)}, bf16[64,1024]{1,0:T(8,128)(2,1)S(1)}, u32[]{:S(2)}, u32[]{:S(2)}) collective-permute-start(bf16[64,1024]{1,0:T(8,128)(2,1)S(1)} %pair_sum.21.refs_3_), channel_id=1, source_target_pairs={{0,8},{1,9},{2,10},{3,11},{4,12},{5,13},{6,14},{7,15},{8,0},{9,1},... | collective-permute-start | bytes 393224 | tf_op jit(solution)/shard_map/ppermute | solution.py:471
  52.8 3.2 %update_and_logits.4 = (f32[64,4096]{1,0:T(8,128)S(1)}, f32[1,4096]{1,0:T(1,128)S(1)}, f32[1,64]{1,0:T(1,128)}, f32[64,1]{1,0:T(8,128)S(1)}, f32[1,1]{1,0:T(1,128)}, /*index=5*/f32[1024,64]{1,0:T(8,128)S(1)}) custom-call(f32[1,3]{1,0:T(1,128)S(1)} %maximum_bitcast_fusion._.scalars, s32[2,64]{1,0:T(2,128)S(1)} %copy-done.3, f32[2,64,8192]{2,1,0:T(8,128)S(1)} %copy-done, ...), custom_call_target="tpu_custom_call" | custom-call | flops 2147483648 | tf_op jit(solution)/shard_map/update_and_logits/pallas_call | solution.py:430
  56.7 3.5 %update_and_logits.5 = (f32[64,4096]{1,0:T(8,128)S(1)}, f32[1,4096]{1,0:T(1,128)S(1)}, f32[64,512]{1,0:T(8,128)S(1)}, f32[64,512]{1,0:T(8,128)S(1)}) custom-call(f32[1,3]{1,0:T(1,128)S(1)} %maximum_bitcast_fusion._.scalars, s32[2,64]{1,0:T(2,128)S(1)} %copy-done.3, f32[2,64,8192]{2,1,0:T(8,128)S(1)} %copy-done, ...), custom_call_target="tpu_custom_call" | custom-call | flops 2147483648 | tf_op jit(solution)/shard_map/update_and_logits/pallas_call | solution.py:430
  60.3 1.3 %collective-permute-done.17 = f32[64,512]{1,0:T(8,128)S(1)} collective-permute-done((f32[64,512]{1,0:T(8,128)S(1)}, f32[64,512]{1,0:T(8,128)S(1)}, u32[]{:S(2)}, u32[]{:S(2)}) %collective-permute-start.17) | collective-permute-done | bytes 131104 | tf_op jit(solution)/shard_map/ppermute | solution.py:445
  61.7 2.5 %collective-permute-start.20 = (bf16[64,512]{1,0:T(8,128)(2,1)S(1)}, bf16[64,512]{1,0:T(8,128)(2,1)S(1)}, u32[]{:S(2)}, u32[]{:S(2)}) collective-permute-start(bf16[64,512]{1,0:T(8,128)(2,1)S(1)} %add_convert_fusion.1.refs_0_), channel_id=1, source_target_pairs={{0,6},{1,7},{2,4},{3,5},{4,2},{5,3},{6,0},{7,1},{8,14},{9,15},{10,... | collective-permute-start | bytes 196616 | tf_op jit(solution)/shard_map/ppermute | solution.py:445
  64.2 1.9 %collective-permute-start.18 = (bf16[64,512]{1,0:T(8,128)(2,1)S(1)}, bf16[64,512]{1,0:T(8,128)(2,1)S(1)}, u32[]{:S(2)}, u32[]{:S(2)}) collective-permute-start(bf16[64,512]{1,0:T(8,128)(2,1)S(1)} %add_convert_fusion.1.refs_0_), channel_id=1, source_target_pairs={{0,2},{1,3},{2,0},{3,1},{4,6},{5,7},{6,4},{7,5},{8,10},{9,11},{10,... | collective-permute-start | bytes 196616 | tf_op jit(solution)/shard_map/ppermute | solution.py:445
  66.1 2.4 %collective-permute-done.20.refs_3_ = bf16[64,512]{1,0:T(8,128)(2,1)S(1)} collective-permute-done((bf16[64,512]{1,0:T(8,128)(2,1)S(1)}, bf16[64,512]{1,0:T(8,128)(2,1)S(1)}, u32[]{:S(2)}, u32[]{:S(2)}) %collective-permute-start.20) | collective-permute-done | bytes 65568 | tf_op jit(solution)/shard_map/ppermute | solution.py:445
  68.5 2.1 %collective-permute-done.19.refs_2_ = bf16[64,512]{1,0:T(8,128)(2,1)S(1)} collective-permute-done((bf16[64,512]{1,0:T(8,128)(2,1)S(1)}, bf16[64,512]{1,0:T(8,128)(2,1)S(1)}, u32[]{:S(2)}, u32[]{:S(2)}) %collective-permute-start.19) | collective-permute-done | bytes 65568 | tf_op jit(solution)/shard_map/ppermute | solution.py:445
  72.4 1.5 %collective-permute-start.22 = (bf16[64,1024]{1,0:T(8,128)(2,1)S(1)}, bf16[64,1024]{1,0:T(8,128)(2,1)S(1)}, u32[]{:S(2)}, u32[]{:S(2)}) collective-permute-start(bf16[64,1024]{1,0:T(8,128)(2,1)S(1)} %gradient.24), channel_id=1, source_target_pairs={{0,8},{1,9},{2,10},{3,11},{4,12},{5,13},{6,14},{7,15},{8,0},{9,1},... | collective-permute-start | bytes 393224 | tf_op jit(solution)/shard_map/ppermute | solution.py:471
  80.6 1.4 %collective-permute-start.26 = (bf16[64,1024]{1,0:T(8,128)(2,1)S(1)}, bf16[64,1024]{1,0:T(8,128)(2,1)S(1)}, u32[]{:S(2)}, u32[]{:S(2)}) collective-permute-start(bf16[64,1024]{1,0:T(8,128)(2,1)S(1)} %pair_sum.26.left), channel_id=1, source_target_pairs={{0,8},{1,9},{2,10},{3,11},{4,12},{5,13},{6,14},{7,15},{8,0},{9,1},... | collective-permute-start | bytes 393224 | tf_op jit(solution)/shard_map/ppermute | solution.py:471
  84.9 1.5 %collective-permute-done.23.right = bf16[64,1024]{1,0:T(8,128)(2,1)S(1)} collective-permute-done((bf16[64,1024]{1,0:T(8,128)(2,1)S(1)}, bf16[64,1024]{1,0:T(8,128)(2,1)S(1)}, u32[]{:S(2)}, u32[]{:S(2)}) %collective-permute-start.23) | collective-permute-done | bytes 131104 | tf_op jit(solution)/shard_map/ppermute | solution.py:471
  87.5 1.3 %collective-permute-start.27 = (bf16[64,1024]{1,0:T(8,128)(2,1)S(1)}, bf16[64,1024]{1,0:T(8,128)(2,1)S(1)}, u32[]{:S(2)}, u32[]{:S(2)}) collective-permute-start(bf16[64,1024]{1,0:T(8,128)(2,1)S(1)} %pair_sum.27.refs_2_), channel_id=1, source_target_pairs={{0,16},{1,17},{2,18},{3,19},{4,20},{5,21},{6,22},{7,23},{8,24},{9,... | collective-permute-start | bytes 393224 | tf_op jit(solution)/shard_map/ppermute | solution.py:471
  91.0 3.1 %update_and_logits.6 = (f32[64,8192]{1,0:T(8,128)}, f32[1024,64]{1,0:T(8,128)S(1)}) custom-call(f32[1,3]{1,0:T(1,128)S(1)} %maximum_bitcast_fusion._.scalars, s32[2,64]{1,0:T(2,128)S(1)} %copy-done.3, f32[2,64,8192]{2,1,0:T(8,128)S(1)} %copy-done, bf16[1024,8192]{1,0:T(8,128)(2,1)S(1)} %get-tuple-element.59.refs_2_.refs_0_, ...), custom_call_target="tpu_custom_call" | custom-call | flops 2147483648 | tf_op jit(solution)/shard_map/update_and_logits/pallas_call | solution.py:430
  95.0 3.1 %update_and_logits.7 = (f32[64,8192]{1,0:T(8,128)}, f32[64,512]{1,0:T(8,128)S(1)}, f32[64,512]{1,0:T(8,128)S(1)}) custom-call(f32[1,3]{1,0:T(1,128)S(1)} %maximum_bitcast_fusion._.scalars, s32[2,64]{1,0:T(2,128)S(1)} %copy-done.3, f32[2,64,8192]{2,1,0:T(8,128)S(1)} %copy-done, ...), custom_call_target="tpu_custom_call", output_to_operand_aliasing={{0}: (11, {})} | custom-call | flops 2147483648 | tf_op jit(solution)/shard_map/update_and_logits/pallas_call | solution.py:430
  98.2 1.3 %collective-permute-done.34 = f32[64,512]{1,0:T(8,128)S(1)} collective-permute-done((f32[64,512]{1,0:T(8,128)S(1)}, f32[64,512]{1,0:T(8,128)S(1)}, u32[]{:S(2)}, u32[]{:S(2)}) %collective-permute-start.34) | collective-permute-done | bytes 131104 | tf_op jit(solution)/shard_map/ppermute | solution.py:445
  99.6 2.5 %collective-permute-start.37 = (bf16[64,512]{1,0:T(8,128)(2,1)S(1)}, bf16[64,512]{1,0:T(8,128)(2,1)S(1)}, u32[]{:S(2)}, u32[]{:S(2)}) collective-permute-start(bf16[64,512]{1,0:T(8,128)(2,1)S(1)} %add_convert_fusion.refs_0_), channel_id=1, source_target_pairs={{0,6},{1,7},{2,4},{3,5},{4,2},{5,3},{6,0},{7,1},{8,14},{9,15},{10,... | collective-permute-start | bytes 196616 | tf_op jit(solution)/shard_map/ppermute | solution.py:445
  102.1 2.0 %collective-permute-start.35 = (bf16[64,512]{1,0:T(8,128)(2,1)S(1)}, bf16[64,512]{1,0:T(8,128)(2,1)S(1)}, u32[]{:S(2)}, u32[]{:S(2)}) collective-permute-start(bf16[64,512]{1,0:T(8,128)(2,1)S(1)} %add_convert_fusion.refs_0_), channel_id=1, source_target_pairs={{0,2},{1,3},{2,0},{3,1},{4,6},{5,7},{6,4},{7,5},{8,10},{9,11},{10,... | collective-permute-start | bytes 196616 | tf_op jit(solution)/shard_map/ppermute | solution.py:445
  104.0 2.4 %collective-permute-done.37.refs_3_ = bf16[64,512]{1,0:T(8,128)(2,1)S(1)} collective-permute-done((bf16[64,512]{1,0:T(8,128)(2,1)S(1)}, bf16[64,512]{1,0:T(8,128)(2,1)S(1)}, u32[]{:S(2)}, u32[]{:S(2)}) %collective-permute-start.37) | collective-permute-done | bytes 65568 | tf_op jit(solution)/shard_map/ppermute | solution.py:445
  106.4 2.0 %collective-permute-done.36.refs_2_ = bf16[64,512]{1,0:T(8,128)(2,1)S(1)} collective-permute-done((bf16[64,512]{1,0:T(8,128)(2,1)S(1)}, bf16[64,512]{1,0:T(8,128)(2,1)S(1)}, u32[]{:S(2)}, u32[]{:S(2)}) %collective-permute-start.36) | collective-permute-done | bytes 65568 | tf_op jit(solution)/shard_map/ppermute | solution.py:445
  109.8 1.9 %collective-permute-start.41 = (f32[1,64]{1,0:T(1,128)S(1)}, f32[1,64]{1,0:T(1,128)S(1)}, u32[]{:S(2)}, u32[]{:S(2)}) collective-permute-start(f32[1,64]{1,0:T(1,128)S(1)} %add.36), channel_id=1, source_target_pairs={{0,24},{8,16},{16,8},{24,0},{1,25},{9,17},{17,9},{25,1},{2,26},{10... | collective-permute-start | bytes 776 | tf_op jit(solution)/shard_map/ppermute | solution.py:445
  (108 shorter events, 34.5 us)
Async XLA Ops:
  19.0 8.4 %collective-permute-start.3 = (f16[64,640]{1,0:T(8,128)(2,1)S(1)}, f16[64,640]{1,0:T(8,128)(2,1)S(1)}, u32[]{:S(2)}, u32[]{:S(2)}) collective-permute-start(f16[64,640]{1,0:T(8,128)(2,1)S(1)} %fusion.1), channel_id=1, source_target_pairs={{0,6},{1,7},{2,4},{3,5},{4,2},{5,3},{6,0},{7,1},{8,14},{9,15},{10,... | collective-permute-start | bytes 245768 | tf_op jit(solution)/shard_map/ppermute | solution.py:445
  24.0 7.2 %collective-permute-start.2 = (f16[64,640]{1,0:T(8,128)(2,1)S(1)}, f16[64,640]{1,0:T(8,128)(2,1)S(1)}, u32[]{:S(2)}, u32[]{:S(2)}) collective-permute-start(f16[64,640]{1,0:T(8,128)(2,1)S(1)} %fusion.1), channel_id=1, source_target_pairs={{0,4},{1,5},{2,6},{3,7},{4,0},{5,1},{6,2},{7,3},{8,12},{9,13},{10,... | collective-permute-start | bytes 245768 | tf_op jit(solution)/shard_map/ppermute | solution.py:445
  24.0 7.2 %collective-permute-start.1 = (f16[64,640]{1,0:T(8,128)(2,1)S(1)}, f16[64,640]{1,0:T(8,128)(2,1)S(1)}, u32[]{:S(2)}, u32[]{:S(2)}) collective-permute-start(f16[64,640]{1,0:T(8,128)(2,1)S(1)} %fusion.1), channel_id=1, source_target_pairs={{0,2},{1,3},{2,0},{3,1},{4,6},{5,7},{6,4},{7,5},{8,10},{9,11},{10,... | collective-permute-start | bytes 245768 | tf_op jit(solution)/shard_map/ppermute | solution.py:445
  33.3 6.8 %collective-permute-start.5 = (bf16[64,1152]{1,0:T(8,128)(2,1)S(1)}, bf16[64,1152]{1,0:T(8,128)(2,1)S(1)}, u32[]{:S(2)}, u32[]{:S(2)}) collective-permute-start(bf16[64,1152]{1,0:T(8,128)(2,1)S(1)} %gradient.16), channel_id=1, source_target_pairs={{0,8},{1,9},{2,10},{3,11},{4,12},{5,13},{6,14},{7,15},{8,0},{9,1},... | collective-permute-start | bytes 442376 | tf_op jit(solution)/shard_map/ppermute | solution.py:471
  35.3 6.5 %collective-permute-start.8 = (bf16[64,1024]{1,0:T(8,128)(2,1)S(1)}, bf16[64,1024]{1,0:T(8,128)(2,1)S(1)}, u32[]{:S(2)}, u32[]{:S(2)}) collective-permute-start(bf16[64,1024]{1,0:T(8,128)(2,1)S(1)} %gradient.17), channel_id=1, source_target_pairs={{0,16},{1,17},{2,18},{3,19},{4,20},{5,21},{6,22},{7,23},{8,24},{9,... | collective-permute-start | bytes 393224 | tf_op jit(solution)/shard_map/ppermute | solution.py:471
  37.4 6.0 %collective-permute-start.11 = (bf16[64,1024]{1,0:T(8,128)(2,1)S(1)}, bf16[64,1024]{1,0:T(8,128)(2,1)S(1)}, u32[]{:S(2)}, u32[]{:S(2)}) collective-permute-start(bf16[64,1024]{1,0:T(8,128)(2,1)S(1)} %gradient.18), channel_id=1, source_target_pairs={{0,8},{1,9},{2,10},{3,11},{4,12},{5,13},{6,14},{7,15},{8,0},{9,1},... | collective-permute-start | bytes 393224 | tf_op jit(solution)/shard_map/ppermute | solution.py:471
  38.5 6.5 %collective-permute-start.14 = (bf16[64,1024]{1,0:T(8,128)(2,1)S(1)}, bf16[64,1024]{1,0:T(8,128)(2,1)S(1)}, u32[]{:S(2)}, u32[]{:S(2)}) collective-permute-start(bf16[64,1024]{1,0:T(8,128)(2,1)S(1)} %gradient.19), channel_id=1, source_target_pairs={{0,16},{1,17},{2,18},{3,19},{4,20},{5,21},{6,22},{7,23},{8,24},{9,... | collective-permute-start | bytes 393224 | tf_op jit(solution)/shard_map/ppermute | solution.py:471
  40.2 7.8 %collective-permute-start.6 = (bf16[64,1152]{1,0:T(8,128)(2,1)S(1)}, bf16[64,1152]{1,0:T(8,128)(2,1)S(1)}, u32[]{:S(2)}, u32[]{:S(2)}) collective-permute-start(bf16[64,1152]{1,0:T(8,128)(2,1)S(1)} %pair_sum.16.left.refs_8_), channel_id=1, source_target_pairs={{0,16},{1,17},{2,18},{3,19},{4,20},{5,21},{6,22},{7,23},{8,24},{9,... | collective-permute-start | bytes 442376 | tf_op jit(solution)/shard_map/ppermute | solution.py:471
  41.9 7.6 %collective-permute-start.9 = (bf16[64,1024]{1,0:T(8,128)(2,1)S(1)}, bf16[64,1024]{1,0:T(8,128)(2,1)S(1)}, u32[]{:S(2)}, u32[]{:S(2)}) collective-permute-start(bf16[64,1024]{1,0:T(8,128)(2,1)S(1)} %pair_sum.18.left), channel_id=1, source_target_pairs={{0,8},{1,9},{2,10},{3,11},{4,12},{5,13},{6,14},{7,15},{8,0},{9,1},... | collective-permute-start | bytes 393224 | tf_op jit(solution)/shard_map/ppermute | solution.py:471
  44.0 6.1 %collective-permute-start.12 = (bf16[64,1024]{1,0:T(8,128)(2,1)S(1)}, bf16[64,1024]{1,0:T(8,128)(2,1)S(1)}, u32[]{:S(2)}, u32[]{:S(2)}) collective-permute-start(bf16[64,1024]{1,0:T(8,128)(2,1)S(1)} %pair_sum.20.left), channel_id=1, source_target_pairs={{0,16},{1,17},{2,18},{3,19},{4,20},{5,21},{6,22},{7,23},{8,24},{9,... | collective-permute-start | bytes 393224 | tf_op jit(solution)/shard_map/ppermute | solution.py:471
  45.1 6.5 %collective-permute-start.15 = (bf16[64,1024]{1,0:T(8,128)(2,1)S(1)}, bf16[64,1024]{1,0:T(8,128)(2,1)S(1)}, u32[]{:S(2)}, u32[]{:S(2)}) collective-permute-start(bf16[64,1024]{1,0:T(8,128)(2,1)S(1)} %pair_sum.22.left), channel_id=1, source_target_pairs={{0,8},{1,9},{2,10},{3,11},{4,12},{5,13},{6,14},{7,15},{8,0},{9,1},... | collective-permute-start | bytes 393224 | tf_op jit(solution)/shard_map/ppermute | solution.py:471
  48.1 8.6 %collective-permute-start.7 = (bf16[64,1024]{1,0:T(8,128)(2,1)S(1)}, bf16[64,1024]{1,0:T(8,128)(2,1)S(1)}, u32[]{:S(2)}, u32[]{:S(2)}) collective-permute-start(bf16[64,1024]{1,0:T(8,128)(2,1)S(1)} %pair_sum.17.refs_1_), channel_id=1, source_target_pairs={{0,8},{1,9},{2,10},{3,11},{4,12},{5,13},{6,14},{7,15},{8,0},{9,1},... | collective-permute-start | bytes 393224 | tf_op jit(solution)/shard_map/ppermute | solution.py:471
  49.5 7.2 %collective-permute-start.10 = (bf16[64,1024]{1,0:T(8,128)(2,1)S(1)}, bf16[64,1024]{1,0:T(8,128)(2,1)S(1)}, u32[]{:S(2)}, u32[]{:S(2)}) collective-permute-start(bf16[64,1024]{1,0:T(8,128)(2,1)S(1)} %pair_sum.19.refs_2_), channel_id=1, source_target_pairs={{0,16},{1,17},{2,18},{3,19},{4,20},{5,21},{6,22},{7,23},{8,24},{9,... | collective-permute-start | bytes 393224 | tf_op jit(solution)/shard_map/ppermute | solution.py:471
  50.1 6.6 %collective-permute-start.13 = (bf16[64,1024]{1,0:T(8,128)(2,1)S(1)}, bf16[64,1024]{1,0:T(8,128)(2,1)S(1)}, u32[]{:S(2)}, u32[]{:S(2)}) collective-permute-start(bf16[64,1024]{1,0:T(8,128)(2,1)S(1)} %pair_sum.21.refs_3_), channel_id=1, source_target_pairs={{0,8},{1,9},{2,10},{3,11},{4,12},{5,13},{6,14},{7,15},{8,0},{9,1},... | collective-permute-start | bytes 393224 | tf_op jit(solution)/shard_map/ppermute | solution.py:471
  51.7 5.0 %collective-permute-start.16 = (bf16[64,1024]{1,0:T(8,128)(2,1)S(1)}, bf16[64,1024]{1,0:T(8,128)(2,1)S(1)}, u32[]{:S(2)}, u32[]{:S(2)}) collective-permute-start(bf16[64,1024]{1,0:T(8,128)(2,1)S(1)} %pair_sum.23.refs_4_), channel_id=1, source_target_pairs={{0,16},{1,17},{2,18},{3,19},{4,20},{5,21},{6,22},{7,23},{8,24},{9,... | collective-permute-start | bytes 393224 | tf_op jit(solution)/shard_map/ppermute | solution.py:471
  61.7 6.8 %collective-permute-start.20 = (bf16[64,512]{1,0:T(8,128)(2,1)S(1)}, bf16[64,512]{1,0:T(8,128)(2,1)S(1)}, u32[]{:S(2)}, u32[]{:S(2)}) collective-permute-start(bf16[64,512]{1,0:T(8,128)(2,1)S(1)} %add_convert_fusion.1.refs_0_), channel_id=1, source_target_pairs={{0,6},{1,7},{2,4},{3,5},{4,2},{5,3},{6,0},{7,1},{8,14},{9,15},{10,... | collective-permute-start | bytes 196616 | tf_op jit(solution)/shard_map/ppermute | solution.py:445
  64.2 6.3 %collective-permute-start.19 = (bf16[64,512]{1,0:T(8,128)(2,1)S(1)}, bf16[64,512]{1,0:T(8,128)(2,1)S(1)}, u32[]{:S(2)}, u32[]{:S(2)}) collective-permute-start(bf16[64,512]{1,0:T(8,128)(2,1)S(1)} %add_convert_fusion.1.refs_0_), channel_id=1, source_target_pairs={{0,4},{1,5},{2,6},{3,7},{4,0},{5,1},{6,2},{7,3},{8,12},{9,13},{10,... | collective-permute-start | bytes 196616 | tf_op jit(solution)/shard_map/ppermute | solution.py:445
  64.2 6.3 %collective-permute-start.18 = (bf16[64,512]{1,0:T(8,128)(2,1)S(1)}, bf16[64,512]{1,0:T(8,128)(2,1)S(1)}, u32[]{:S(2)}, u32[]{:S(2)}) collective-permute-start(bf16[64,512]{1,0:T(8,128)(2,1)S(1)} %add_convert_fusion.1.refs_0_), channel_id=1, source_target_pairs={{0,2},{1,3},{2,0},{3,1},{4,6},{5,7},{6,4},{7,5},{8,10},{9,11},{10,... | collective-permute-start | bytes 196616 | tf_op jit(solution)/shard_map/ppermute | solution.py:445
  72.4 7.0 %collective-permute-start.22 = (bf16[64,1024]{1,0:T(8,128)(2,1)S(1)}, bf16[64,1024]{1,0:T(8,128)(2,1)S(1)}, u32[]{:S(2)}, u32[]{:S(2)}) collective-permute-start(bf16[64,1024]{1,0:T(8,128)(2,1)S(1)} %gradient.24), channel_id=1, source_target_pairs={{0,8},{1,9},{2,10},{3,11},{4,12},{5,13},{6,14},{7,15},{8,0},{9,1},... | collective-permute-start | bytes 393224 | tf_op jit(solution)/shard_map/ppermute | solution.py:471
  74.4 6.1 %collective-permute-start.25 = (bf16[64,1024]{1,0:T(8,128)(2,1)S(1)}, bf16[64,1024]{1,0:T(8,128)(2,1)S(1)}, u32[]{:S(2)}, u32[]{:S(2)}) collective-permute-start(bf16[64,1024]{1,0:T(8,128)(2,1)S(1)} %gradient.25), channel_id=1, source_target_pairs={{0,16},{1,17},{2,18},{3,19},{4,20},{5,21},{6,22},{7,23},{8,24},{9,... | collective-permute-start | bytes 393224 | tf_op jit(solution)/shard_map/ppermute | solution.py:471
  75.9 6.1 %collective-permute-start.28 = (bf16[64,1024]{1,0:T(8,128)(2,1)S(1)}, bf16[64,1024]{1,0:T(8,128)(2,1)S(1)}, u32[]{:S(2)}, u32[]{:S(2)}) collective-permute-start(bf16[64,1024]{1,0:T(8,128)(2,1)S(1)} %gradient.26), channel_id=1, source_target_pairs={{0,8},{1,9},{2,10},{3,11},{4,12},{5,13},{6,14},{7,15},{8,0},{9,1},... | collective-permute-start | bytes 393224 | tf_op jit(solution)/shard_map/ppermute | solution.py:471
  77.1 7.1 %collective-permute-start.31 = (bf16[64,1024]{1,0:T(8,128)(2,1)S(1)}, bf16[64,1024]{1,0:T(8,128)(2,1)S(1)}, u32[]{:S(2)}, u32[]{:S(2)}) collective-permute-start(bf16[64,1024]{1,0:T(8,128)(2,1)S(1)} %gradient.27), channel_id=1, source_target_pairs={{0,16},{1,17},{2,18},{3,19},{4,20},{5,21},{6,22},{7,23},{8,24},{9,... | collective-permute-start | bytes 393224 | tf_op jit(solution)/shard_map/ppermute | solution.py:471
  79.5 7.0 %collective-permute-start.23 = (bf16[64,1024]{1,0:T(8,128)(2,1)S(1)}, bf16[64,1024]{1,0:T(8,128)(2,1)S(1)}, u32[]{:S(2)}, u32[]{:S(2)}) collective-permute-start(bf16[64,1024]{1,0:T(8,128)(2,1)S(1)} %pair_sum.24.left), channel_id=1, source_target_pairs={{0,16},{1,17},{2,18},{3,19},{4,20},{5,21},{6,22},{7,23},{8,24},{9,... | collective-permute-start | bytes 393224 | tf_op jit(solution)/shard_map/ppermute | solution.py:471
  80.6 6.9 %collective-permute-start.26 = (bf16[64,1024]{1,0:T(8,128)(2,1)S(1)}, bf16[64,1024]{1,0:T(8,128)(2,1)S(1)}, u32[]{:S(2)}, u32[]{:S(2)}) collective-permute-start(bf16[64,1024]{1,0:T(8,128)(2,1)S(1)} %pair_sum.26.left), channel_id=1, source_target_pairs={{0,8},{1,9},{2,10},{3,11},{4,12},{5,13},{6,14},{7,15},{8,0},{9,1},... | collective-permute-start | bytes 393224 | tf_op jit(solution)/shard_map/ppermute | solution.py:471
  82.5 6.2 %collective-permute-start.29 = (bf16[64,1024]{1,0:T(8,128)(2,1)S(1)}, bf16[64,1024]{1,0:T(8,128)(2,1)S(1)}, u32[]{:S(2)}, u32[]{:S(2)}) collective-permute-start(bf16[64,1024]{1,0:T(8,128)(2,1)S(1)} %pair_sum.28.left), channel_id=1, source_target_pairs={{0,16},{1,17},{2,18},{3,19},{4,20},{5,21},{6,22},{7,23},{8,24},{9,... | collective-permute-start | bytes 393224 | tf_op jit(solution)/shard_map/ppermute | solution.py:471
  84.3 5.7 %collective-permute-start.32 = (bf16[64,1024]{1,0:T(8,128)(2,1)S(1)}, bf16[64,1024]{1,0:T(8,128)(2,1)S(1)}, u32[]{:S(2)}, u32[]{:S(2)}) collective-permute-start(bf16[64,1024]{1,0:T(8,128)(2,1)S(1)} %pair_sum.30.left), channel_id=1, source_target_pairs={{0,8},{1,9},{2,10},{3,11},{4,12},{5,13},{6,14},{7,15},{8,0},{9,1},... | collective-permute-start | bytes 393224 | tf_op jit(solution)/shard_map/ppermute | solution.py:471
  86.5 8.5 %collective-permute-start.24 = (bf16[64,1024]{1,0:T(8,128)(2,1)S(1)}, bf16[64,1024]{1,0:T(8,128)(2,1)S(1)}, u32[]{:S(2)}, u32[]{:S(2)}) collective-permute-start(bf16[64,1024]{1,0:T(8,128)(2,1)S(1)} %pair_sum.25.refs_1_), channel_id=1, source_target_pairs={{0,8},{1,9},{2,10},{3,11},{4,12},{5,13},{6,14},{7,15},{8,0},{9,1},... | collective-permute-start | bytes 393224 | tf_op jit(solution)/shard_map/ppermute | solution.py:471
  87.5 7.5 %collective-permute-start.27 = (bf16[64,1024]{1,0:T(8,128)(2,1)S(1)}, bf16[64,1024]{1,0:T(8,128)(2,1)S(1)}, u32[]{:S(2)}, u32[]{:S(2)}) collective-permute-start(bf16[64,1024]{1,0:T(8,128)(2,1)S(1)} %pair_sum.27.refs_2_), channel_id=1, source_target_pairs={{0,16},{1,17},{2,18},{3,19},{4,20},{5,21},{6,22},{7,23},{8,24},{9,... | collective-permute-start | bytes 393224 | tf_op jit(solution)/shard_map/ppermute | solution.py:471
  88.8 6.2 %collective-permute-start.30 = (bf16[64,1024]{1,0:T(8,128)(2,1)S(1)}, bf16[64,1024]{1,0:T(8,128)(2,1)S(1)}, u32[]{:S(2)}, u32[]{:S(2)}) collective-permute-start(bf16[64,1024]{1,0:T(8,128)(2,1)S(1)} %pair_sum.29.refs_3_), channel_id=1, source_target_pairs={{0,8},{1,9},{2,10},{3,11},{4,12},{5,13},{6,14},{7,15},{8,0},{9,1},... | collective-permute-start | bytes 393224 | tf_op jit(solution)/shard_map/ppermute | solution.py:471
  99.6 6.8 %collective-permute-start.37 = (bf16[64,512]{1,0:T(8,128)(2,1)S(1)}, bf16[64,512]{1,0:T(8,128)(2,1)S(1)}, u32[]{:S(2)}, u32[]{:S(2)}) collective-permute-start(bf16[64,512]{1,0:T(8,128)(2,1)S(1)} %add_convert_fusion.refs_0_), channel_id=1, source_target_pairs={{0,6},{1,7},{2,4},{3,5},{4,2},{5,3},{6,0},{7,1},{8,14},{9,15},{10,... | collective-permute-start | bytes 196616 | tf_op jit(solution)/shard_map/ppermute | solution.py:445
  102.1 6.3 %collective-permute-start.36 = (bf16[64,512]{1,0:T(8,128)(2,1)S(1)}, bf16[64,512]{1,0:T(8,128)(2,1)S(1)}, u32[]{:S(2)}, u32[]{:S(2)}) collective-permute-start(bf16[64,512]{1,0:T(8,128)(2,1)S(1)} %add_convert_fusion.refs_0_), channel_id=1, source_target_pairs={{0,4},{1,5},{2,6},{3,7},{4,0},{5,1},{6,2},{7,3},{8,12},{9,13},{10,... | collective-permute-start | bytes 196616 | tf_op jit(solution)/shard_map/ppermute | solution.py:445
  102.1 6.3 %collective-permute-start.35 = (bf16[64,512]{1,0:T(8,128)(2,1)S(1)}, bf16[64,512]{1,0:T(8,128)(2,1)S(1)}, u32[]{:S(2)}, u32[]{:S(2)}) collective-permute-start(bf16[64,512]{1,0:T(8,128)(2,1)S(1)} %add_convert_fusion.refs_0_), channel_id=1, source_target_pairs={{0,2},{1,3},{2,0},{3,1},{4,6},{5,7},{6,4},{7,5},{8,10},{9,11},{10,... | collective-permute-start | bytes 196616 | tf_op jit(solution)/shard_map/ppermute | solution.py:445
  (14 other events, 70.4 us)

commit v5 on v4

--- a/solution.py
+++ b/solution.py
@@ -315,8 +315,6 @@
     approved = flipped(flags[move : move + 1, :].astype(F32)) > 0.5
     if start_first and which == KEEP:
         gram, arrived, held = refs.pop(0), refs.pop(0), refs.pop(0)
-    elif start_first:
-        weights, factor = refs.pop(0)[...], refs.pop(0)[...]
     else:
         size_in = refs.pop(0)
     before = refs.pop(0) if which == SEND else None
@@ -324,15 +322,26 @@
         refs.pop(0)
     moved = refs.pop(0)
     if start_first:
-        size_out = refs.pop(0)
         if which == KEEP:
-            log_weights_out, weights_out, factor_out = refs.pop(0), refs.pop(0), refs.pop(0)
+            sizes_out = (refs.pop(0), refs.pop(0))
+            log_weights_out = refs.pop(0)
             loglik = from_lanes(held[:, columns // PIECES :]) + from_lanes(arrived[:, columns // PIECES :])
             log_weights, weights, mean_spread = weigh(advance, loglik, gram[...])
             log_weights_out[...] = flipped(log_weights)
-            weights_out[...] = weights
             factor = scalars[:, 2:3] / mean_spread
-            factor_out[...] = factor
+            for half, size_out in enumerate(sizes_out):
+                width = columns // PIECES
+                narrow = tile_of(width, 512)
+                for piece in range(PIECES):
+                    begin = half_of(half, piece, variants)
+                    for start in range(0, width, narrow):
+                        there = pl.ds(pl.multiple_of(begin + start, narrow), narrow)
+                        c = cloud[:, there]
+                        center = jnp.sum(weights * c, axis=0, keepdims=True)
+                        spread = jnp.sum(weights * (c - center) ** 2, axis=0, keepdims=True) + 1e-06
+                        at = piece * width + start
+                        size_out[:, at : at + narrow] = spread * factor
+            size_in = sizes_out[KEEP]
     if which == KEEP:
         total = refs.pop(0)
     else:
@@ -352,19 +361,18 @@
             there = pl.ds(pl.multiple_of(first + start - block * width, narrow), narrow)
             here = slice(start, start + narrow)
             c = cloud[:, there] if start_first else cloud[:, here]
-            if start_first:
-                center = jnp.sum(weights * c, axis=0, keepdims=True)
-                spread = jnp.sum(weights * (c - center) ** 2, axis=0, keepdims=True) + 1e-06
-                size = spread * factor
-                size_out[:, here] = size
-            else:
-                size = size_in[:, here]
+            size = size_in[:, here]
             piece, at = divmod(start, columns // PIECES)
             slope = grads[piece][:, at : at + narrow].astype(F32)
+            if last:
+                c = c + jnp.where(approved, size * heat, 0.0) * slope
+                buffer[:, here] = c
+                chosen.append(c.astype(BF16))
+                continue
             rise = heat * slope - SHRINKAGE_LEVEL * c * lax.rsqrt(c * c + 1.0)
             proposal = c + size * rise + jnp.sqrt(2.0 * size) * noise[move, :, there]
             c = jnp.where(approved, proposal, c)
-            (buffer if last else moved)[:, here] = c
+            moved[:, here] = c
             chosen.append(c.astype(BF16))
         there = pl.ds(pl.multiple_of(first, width), width)
         if last:
@@ -395,6 +403,34 @@
         copy.wait()
 
 
+def drift_kernel(which, move, flags, noise, cloud, size_in, out):
+    variants = noise.shape[2]
+    columns = variants // 2
+    width = columns // PIECES
+    narrow = tile_of(width, 512)
+    approved = flipped(flags[move : move + 1, :].astype(F32)) > 0.5
+    for piece in range(PIECES):
+        first = half_of(which, piece, variants)
+        for start in range(0, width, narrow):
+            there = pl.ds(pl.multiple_of(first + start, narrow), narrow)
+            here = slice(piece * width + start, piece * width + start + narrow)
+            c, size = cloud[:, here], size_in[:, here]
+            pull = SHRINKAGE_LEVEL * c * lax.rsqrt(c * c + 1.0)
+            free = c - size * pull + jnp.sqrt(2.0 * size) * noise[move, :, there]
+            out[:, here] = jnp.where(approved, free, c)
+
+
+def drift(which, move, fixed, cloud, size):
+    return pl.pallas_call(
+        functools.partial(drift_kernel, which, move),
+        in_specs=[VMEM] * 4,
+        out_specs=VMEM,
+        out_shape=jax.ShapeDtypeStruct(cloud.shape, F32),
+        compiler_params=params(8),
+        name="drift",
+    )(fixed[1], fixed[2], cloud, size)
+
+
 def update(which, move, total_variants, fixed, centered, grads, cloud, extra, before, moved):
     flags = fixed[1]
     particles, variants = flags.shape[1], centered[0].shape[1]
@@ -410,11 +446,9 @@
     last = move == 1
     out_shape = [jax.ShapeDtypeStruct((particles, variants if last else columns), F32)]
     if not last:
-        out_shape.append(jax.ShapeDtypeStruct((1, columns), F32))
         if which == KEEP:
+            out_shape += [jax.ShapeDtypeStruct((1, columns), F32)] * 2
             out_shape.append(jax.ShapeDtypeStruct((1, particles), F32))
-            out_shape.append(jax.ShapeDtypeStruct((particles, 1), F32))
-            out_shape.append(jax.ShapeDtypeStruct((1, 1), F32))
     scratch = []
     if which == KEEP:
         out_shape.append(jax.ShapeDtypeStruct((people, particles), F32))
@@ -546,23 +580,26 @@
         summed = pair_sums([False] * PIECES, held, arrived, width)
         arriving = [swap_over_rows(each, piece, 0) for piece, each in enumerate(summed)]
         if first:
-            c_kept, size_kept, log_weights, weights, factor, total = update(
+            c_kept, size_kept, size_sent, log_weights, total = update(
                 KEEP, move, total_variants, fixed, centered, summed, walker_cloud,
                 [gram, arrived[0], held[0]], None, None,
             )
-            c_sent, size_sent, mine, other = update(
+            c_sent, mine, other = update(
                 SEND, move, total_variants, fixed, centered, arriving, walker_cloud,
-                [weights, factor], total, None,
+                [size_sent], total, None,
             )
         else:
             moved, total = update(
-                KEEP, move, total_variants, fixed, centered, summed, c_kept, [size_kept], None, None
+                KEEP, move, total_variants, fixed, centered, summed, free_kept, [size_kept], None, None
             )
             moved, mine, other = update(
-                SEND, move, total_variants, fixed, centered, arriving, c_sent, [size_sent], total, moved
+                SEND, move, total_variants, fixed, centered, arriving, free_sent, [size_sent], total, moved
             )
         sent = over_chips((mine + swap(other, "col", 1)).astype(BF16))
         if first:
+            free_kept = drift(KEEP, 1, fixed, c_kept, size_kept)
+            free_sent = drift(SEND, 1, fixed, c_sent, size_sent)
+            (free_kept, free_sent), sent = lax.optimization_barrier(((free_kept, free_sent), sent))
             own = residual_of(scale, status, sent)
             pairs = [own, swap(own, "col", 1)]
     loglik = last_loglik(scale, status, sent)

time: 117 us -> 116 us (level)
  transfers between devices with their start and end apart: 42 -> 42, of which waited for: 20 -> 20; matrix products, arithmetic and copies ran while one was open for 0% -> 0% of each run, Pallas kernels for 12% -> 13%
where the time goes in v5:
time: 116 us
  starting transfers between devices  46.1 us (40%)
  Pallas kernels  34.7 us (30%)
  waiting for transfers between devices  29.4 us (25%)
  between operations  2.93 us (3%)
  local copies, waits for them, and re-layouts  1.61 us (1%)
    ppermute x24, starting transfers between devices, swap_over_rows(): lax.ppermute(value, ('row', 'col'), [(row * columns + col, (row ^ order[p...  27.1 us
    ppermute x18, waiting for transfers between devices, swap(): return lax.ppermute(value, axis, [(i, i ^ distance) for i in range(size)])  24.3 us
    ppermute x18, starting transfers between devices, swap(): return lax.ppermute(value, axis, [(i, i ^ distance) for i in range(size)])  18.9 us
    pallas_call x1, Pallas kernels, center_and_first_logits(): pl.pallas_call(functools.partial(center_kernel, block, scale, total_varia...  13.1 us
    pallas_call x4, Pallas kernels, update(): pl.pallas_call(functools.partial(update_kernel, which, move, total_varian...  11.8 us
    pallas_call x16, Pallas kernels, gradient(): pl.pallas_call(functools.partial(gradient_kernel, len(pairs) // 2, which,...  7.88 us
    ppermute x24, waiting for transfers between devices, swap_over_rows(): lax.ppermute(value, ('row', 'col'), [(row * columns + col, (row ^ order[p...  5.1 us
  transfers between devices with their start and end apart: 42, of which 20 were waited for; matrix products, arithmetic and copies ran while one was open for 0% of the time, Pallas kernels for 13%

profile of v5, /device:TPU:0, one launch (start us, length us, event | category | flops | bytes accessed | tf_op | source)
XLA Modules:
  0.0 115.6 jit_solution(1740923226978940426)
XLA Ops:
  2.6 1.6 %copy-done.1 = f32[64,8192]{1,0:T(8,128)S(1)} copy-done((f32[64,8192]{1,0:T(8,128)S(1)}, f32[64,8192]{1,0:T(8,128)}, u32[]{:S(2)}) %copy-start.1) | copy-done | bytes 2097176
  4.2 13.1 %center_and_first_logits.1 = (bf16[1024,8192]{1,0:T(8,128)(2,1)S(1)}, f32[64,640]{1,0:T(8,128)S(1)}, f32[64,640]{1,0:T(8,128)S(1)}) custom-call(s32[1024,8192]{1,0:T(8,128)} %doses.1, f32[64,8192]{1,0:T(8,128)S(1)} %copy-done.1, f32[1,3]{1,0:T(1,128)S(1)} %maximum_bitcast_fusion._.scalars), custom_call_target="tpu_custom_call" | custom-call | flops 8589934592 | tf_op jit(solution)/shard_map/center_and_first_logits/pallas_call | solution.py:134
  19.0 5.0 %collective-permute-start.3 = (f16[64,640]{1,0:T(8,128)(2,1)S(1)}, f16[64,640]{1,0:T(8,128)(2,1)S(1)}, u32[]{:S(2)}, u32[]{:S(2)}) collective-permute-start(f16[64,640]{1,0:T(8,128)(2,1)S(1)} %fusion.1), channel_id=1, source_target_pairs={{0,6},{1,7},{2,4},{3,5},{4,2},{5,3},{6,0},{7,1},{8,14},{9,15},{10,... | collective-permute-start | bytes 245768 | tf_op jit(solution)/shard_map/ppermute | solution.py:479
  24.7 2.7 %collective-permute-done.3 = f16[64,640]{1,0:T(8,128)(2,1)S(1)} collective-permute-done((f16[64,640]{1,0:T(8,128)(2,1)S(1)}, f16[64,640]{1,0:T(8,128)(2,1)S(1)}, u32[]{:S(2)}, u32[]{:S(2)}) %collective-permute-start.3) | collective-permute-done | bytes 81952 | tf_op jit(solution)/shard_map/ppermute | solution.py:479
  27.4 3.8 %collective-permute-done.2 = f16[64,640]{1,0:T(8,128)(2,1)S(1)} collective-permute-done((f16[64,640]{1,0:T(8,128)(2,1)S(1)}, f16[64,640]{1,0:T(8,128)(2,1)S(1)}, u32[]{:S(2)}, u32[]{:S(2)}) %collective-permute-start.2) | collective-permute-done | bytes 81952 | tf_op jit(solution)/shard_map/ppermute | solution.py:479
  33.3 1.6 %collective-permute-start.5 = (bf16[64,1152]{1,0:T(8,128)(2,1)S(1)}, bf16[64,1152]{1,0:T(8,128)(2,1)S(1)}, u32[]{:S(2)}, u32[]{:S(2)}) collective-permute-start(bf16[64,1152]{1,0:T(8,128)(2,1)S(1)} %gradient.16), channel_id=1, source_target_pairs={{0,8},{1,9},{2,10},{3,11},{4,12},{5,13},{6,14},{7,15},{8,0},{9,1},... | collective-permute-start | bytes 442376 | tf_op jit(solution)/shard_map/ppermute | solution.py:505
  35.3 1.6 %collective-permute-start.7 = (bf16[64,1024]{1,0:T(8,128)(2,1)S(1)}, bf16[64,1024]{1,0:T(8,128)(2,1)S(1)}, u32[]{:S(2)}, u32[]{:S(2)}) collective-permute-start(bf16[64,1024]{1,0:T(8,128)(2,1)S(1)} %gradient.17), channel_id=1, source_target_pairs={{0,16},{1,17},{2,18},{3,19},{4,20},{5,21},{6,22},{7,23},{8,24},{9,... | collective-permute-start | bytes 393224 | tf_op jit(solution)/shard_map/ppermute | solution.py:505
  40.2 1.6 %collective-permute-start.6 = (bf16[64,1152]{1,0:T(8,128)(2,1)S(1)}, bf16[64,1152]{1,0:T(8,128)(2,1)S(1)}, u32[]{:S(2)}, u32[]{:S(2)}) collective-permute-start(bf16[64,1152]{1,0:T(8,128)(2,1)S(1)} %pair_sum.16.left.refs_8_), channel_id=1, source_target_pairs={{0,16},{1,17},{2,18},{3,19},{4,20},{5,21},{6,22},{7,23},{8,24},{9,... | collective-permute-start | bytes 442376 | tf_op jit(solution)/shard_map/ppermute | solution.py:505
  41.9 1.6 %collective-permute-start.8 = (bf16[64,1024]{1,0:T(8,128)(2,1)S(1)}, bf16[64,1024]{1,0:T(8,128)(2,1)S(1)}, u32[]{:S(2)}, u32[]{:S(2)}) collective-permute-start(bf16[64,1024]{1,0:T(8,128)(2,1)S(1)} %pair_sum.18.left), channel_id=1, source_target_pairs={{0,8},{1,9},{2,10},{3,11},{4,12},{5,13},{6,14},{7,15},{8,0},{9,1},... | collective-permute-start | bytes 393224 | tf_op jit(solution)/shard_map/ppermute | solution.py:505
  45.1 1.6 %collective-permute-start.12 = (bf16[64,1024]{1,0:T(8,128)(2,1)S(1)}, bf16[64,1024]{1,0:T(8,128)(2,1)S(1)}, u32[]{:S(2)}, u32[]{:S(2)}) collective-permute-start(bf16[64,1024]{1,0:T(8,128)(2,1)S(1)} %pair_sum.22.left), channel_id=1, source_target_pairs={{0,8},{1,9},{2,10},{3,11},{4,12},{5,13},{6,14},{7,15},{8,0},{9,1},... | collective-permute-start | bytes 393224 | tf_op jit(solution)/shard_map/ppermute | solution.py:505
  46.7 1.4 %collective-permute-done.6.right.refs_7_ = bf16[64,1152]{1,0:T(8,128)(2,1)S(1)} collective-permute-done((bf16[64,1152]{1,0:T(8,128)(2,1)S(1)}, bf16[64,1152]{1,0:T(8,128)(2,1)S(1)}, u32[]{:S(2)}, u32[]{:S(2)}) %collective-permute-start.6) | collective-permute-done | bytes 147488 | tf_op jit(solution)/shard_map/ppermute | solution.py:505
  48.1 1.4 %collective-permute-start.13 = (bf16[64,1024]{1,0:T(8,128)(2,1)S(1)}, bf16[64,1024]{1,0:T(8,128)(2,1)S(1)}, u32[]{:S(2)}, u32[]{:S(2)}) collective-permute-start(bf16[64,1024]{1,0:T(8,128)(2,1)S(1)} %pair_sum.17.refs_1_), channel_id=1, source_target_pairs={{0,8},{1,9},{2,10},{3,11},{4,12},{5,13},{6,14},{7,15},{8,0},{9,1},... | collective-permute-start | bytes 393224 | tf_op jit(solution)/shard_map/ppermute | solution.py:505
  50.1 1.5 %collective-permute-start.15 = (bf16[64,1024]{1,0:T(8,128)(2,1)S(1)}, bf16[64,1024]{1,0:T(8,128)(2,1)S(1)}, u32[]{:S(2)}, u32[]{:S(2)}) collective-permute-start(bf16[64,1024]{1,0:T(8,128)(2,1)S(1)} %pair_sum.21.refs_3_), channel_id=1, source_target_pairs={{0,8},{1,9},{2,10},{3,11},{4,12},{5,13},{6,14},{7,15},{8,0},{9,1},... | collective-permute-start | bytes 393224 | tf_op jit(solution)/shard_map/ppermute | solution.py:505
  52.8 3.4 %update_and_logits.4 = (f32[64,4096]{1,0:T(8,128)S(1)}, f32[1,4096]{1,0:T(1,128)S(1)}, f32[1,4096]{1,0:T(1,128)S(1)}, f32[1,64]{1,0:T(1,128)}, f32[1024,64]{1,0:T(8,128)S(1)}) custom-call(f32[1,3]{1,0:T(1,128)S(1)} %maximum_bitcast_fusion._.scalars, s32[2,64]{1,0:T(2,128)S(1)} %copy-done.3, f32[2,64,8192]{2,1,0:T(8,128)S(1)} %copy-done, ...), custom_call_target="tpu_custom_call" | custom-call | flops 2147483648 | tf_op jit(solution)/shard_map/update_and_logits/pallas_call | solution.py:464
  56.7 2.7 %update_and_logits.5 = (f32[64,4096]{1,0:T(8,128)S(1)}, f32[64,512]{1,0:T(8,128)S(1)}, f32[64,512]{1,0:T(8,128)S(1)}) custom-call(f32[1,3]{1,0:T(1,128)S(1)} %maximum_bitcast_fusion._.scalars, s32[2,64]{1,0:T(2,128)S(1)} %copy-done.3, f32[2,64,8192]{2,1,0:T(8,128)S(1)} %copy-done, bf16[1024,8192]{1,0:T(8,128)(2,1)S(1)} %get-tuple-element.63.refs_2_.refs_0_, ...), custom_call_target="tpu_custom_call" | custom-call | flops 2147483648 | tf_op jit(solution)/shard_map/update_and_logits/pallas_call | solution.py:464
  59.5 1.3 %collective-permute-done.17 = f32[64,512]{1,0:T(8,128)S(1)} collective-permute-done((f32[64,512]{1,0:T(8,128)S(1)}, f32[64,512]{1,0:T(8,128)S(1)}, u32[]{:S(2)}, u32[]{:S(2)}) %collective-permute-start.17) | collective-permute-done | bytes 131104 | tf_op jit(solution)/shard_map/ppermute | solution.py:479
  60.9 2.5 %collective-permute-start.20 = (bf16[64,512]{1,0:T(8,128)(2,1)S(1)}, bf16[64,512]{1,0:T(8,128)(2,1)S(1)}, u32[]{:S(2)}, u32[]{:S(2)}) collective-permute-start(bf16[64,512]{1,0:T(8,128)(2,1)S(1)} %add_convert_fusion.1.refs_0_), channel_id=1, source_target_pairs={{0,6},{1,7},{2,4},{3,5},{4,2},{5,3},{6,0},{7,1},{8,14},{9,15},{10,... | collective-permute-start | bytes 196616 | tf_op jit(solution)/shard_map/ppermute | solution.py:479
  63.4 1.9 %collective-permute-start.18 = (bf16[64,512]{1,0:T(8,128)(2,1)S(1)}, bf16[64,512]{1,0:T(8,128)(2,1)S(1)}, u32[]{:S(2)}, u32[]{:S(2)}) collective-permute-start(bf16[64,512]{1,0:T(8,128)(2,1)S(1)} %add_convert_fusion.1.refs_0_), channel_id=1, source_target_pairs={{0,2},{1,3},{2,0},{3,1},{4,6},{5,7},{6,4},{7,5},{8,10},{9,11},{10,... | collective-permute-start | bytes 196616 | tf_op jit(solution)/shard_map/ppermute | solution.py:479
  66.2 1.5 %collective-permute-done.20.refs_3_ = bf16[64,512]{1,0:T(8,128)(2,1)S(1)} collective-permute-done((bf16[64,512]{1,0:T(8,128)(2,1)S(1)}, bf16[64,512]{1,0:T(8,128)(2,1)S(1)}, u32[]{:S(2)}, u32[]{:S(2)}) %collective-permute-start.20) | collective-permute-done | bytes 65568 | tf_op jit(solution)/shard_map/ppermute | solution.py:479
  67.7 2.0 %collective-permute-done.19.refs_2_ = bf16[64,512]{1,0:T(8,128)(2,1)S(1)} collective-permute-done((bf16[64,512]{1,0:T(8,128)(2,1)S(1)}, bf16[64,512]{1,0:T(8,128)(2,1)S(1)}, u32[]{:S(2)}, u32[]{:S(2)}) %collective-permute-start.19) | collective-permute-done | bytes 65568 | tf_op jit(solution)/shard_map/ppermute | solution.py:479
  71.6 1.5 %collective-permute-start.22 = (bf16[64,1024]{1,0:T(8,128)(2,1)S(1)}, bf16[64,1024]{1,0:T(8,128)(2,1)S(1)}, u32[]{:S(2)}, u32[]{:S(2)}) collective-permute-start(bf16[64,1024]{1,0:T(8,128)(2,1)S(1)} %gradient.24), channel_id=1, source_target_pairs={{0,8},{1,9},{2,10},{3,11},{4,12},{5,13},{6,14},{7,15},{8,0},{9,1},... | collective-permute-start | bytes 393224 | tf_op jit(solution)/shard_map/ppermute | solution.py:505
  79.8 1.4 %collective-permute-start.26 = (bf16[64,1024]{1,0:T(8,128)(2,1)S(1)}, bf16[64,1024]{1,0:T(8,128)(2,1)S(1)}, u32[]{:S(2)}, u32[]{:S(2)}) collective-permute-start(bf16[64,1024]{1,0:T(8,128)(2,1)S(1)} %pair_sum.26.left), channel_id=1, source_target_pairs={{0,8},{1,9},{2,10},{3,11},{4,12},{5,13},{6,14},{7,15},{8,0},{9,1},... | collective-permute-start | bytes 393224 | tf_op jit(solution)/shard_map/ppermute | solution.py:505
  84.1 1.7 %collective-permute-done.23.right = bf16[64,1024]{1,0:T(8,128)(2,1)S(1)} collective-permute-done((bf16[64,1024]{1,0:T(8,128)(2,1)S(1)}, bf16[64,1024]{1,0:T(8,128)(2,1)S(1)}, u32[]{:S(2)}, u32[]{:S(2)}) %collective-permute-start.23) | collective-permute-done | bytes 131104 | tf_op jit(solution)/shard_map/ppermute | solution.py:505
  87.0 1.4 %collective-permute-start.27 = (bf16[64,1024]{1,0:T(8,128)(2,1)S(1)}, bf16[64,1024]{1,0:T(8,128)(2,1)S(1)}, u32[]{:S(2)}, u32[]{:S(2)}) collective-permute-start(bf16[64,1024]{1,0:T(8,128)(2,1)S(1)} %pair_sum.27.refs_2_), channel_id=1, source_target_pairs={{0,16},{1,17},{2,18},{3,19},{4,20},{5,21},{6,22},{7,23},{8,24},{9,... | collective-permute-start | bytes 393224 | tf_op jit(solution)/shard_map/ppermute | solution.py:505
  90.4 2.8 %update_and_logits.6 = (f32[64,8192]{1,0:T(8,128)}, f32[1024,64]{1,0:T(8,128)S(1)}) custom-call(f32[1,3]{1,0:T(1,128)S(1)} %maximum_bitcast_fusion._.scalars, s32[2,64]{1,0:T(2,128)S(1)} %copy-done.3, f32[2,64,8192]{2,1,0:T(8,128)S(1)} %copy-done, bf16[1024,8192]{1,0:T(8,128)(2,1)S(1)} %get-tuple-element.63.refs_2_.refs_0_, ...), custom_call_target="tpu_custom_call" | custom-call | flops 2147483648 | tf_op jit(solution)/shard_map/update_and_logits/pallas_call | solution.py:464
  94.4 2.8 %update_and_logits.7 = (f32[64,8192]{1,0:T(8,128)}, f32[64,512]{1,0:T(8,128)S(1)}, f32[64,512]{1,0:T(8,128)S(1)}) custom-call(f32[1,3]{1,0:T(1,128)S(1)} %maximum_bitcast_fusion._.scalars, s32[2,64]{1,0:T(2,128)S(1)} %copy-done.3, f32[2,64,8192]{2,1,0:T(8,128)S(1)} %copy-done, ...), custom_call_target="tpu_custom_call", output_to_operand_aliasing={{0}: (11, {})} | custom-call | flops 2147483648 | tf_op jit(solution)/shard_map/update_and_logits/pallas_call | solution.py:464
  97.3 1.3 %collective-permute-done.34 = f32[64,512]{1,0:T(8,128)S(1)} collective-permute-done((f32[64,512]{1,0:T(8,128)S(1)}, f32[64,512]{1,0:T(8,128)S(1)}, u32[]{:S(2)}, u32[]{:S(2)}) %collective-permute-start.34) | collective-permute-done | bytes 131104 | tf_op jit(solution)/shard_map/ppermute | solution.py:479
  98.7 2.5 %collective-permute-start.37 = (bf16[64,512]{1,0:T(8,128)(2,1)S(1)}, bf16[64,512]{1,0:T(8,128)(2,1)S(1)}, u32[]{:S(2)}, u32[]{:S(2)}) collective-permute-start(bf16[64,512]{1,0:T(8,128)(2,1)S(1)} %add_convert_fusion.refs_0_), channel_id=1, source_target_pairs={{0,6},{1,7},{2,4},{3,5},{4,2},{5,3},{6,0},{7,1},{8,14},{9,15},{10,... | collective-permute-start | bytes 196616 | tf_op jit(solution)/shard_map/ppermute | solution.py:479
  101.2 1.9 %collective-permute-start.35 = (bf16[64,512]{1,0:T(8,128)(2,1)S(1)}, bf16[64,512]{1,0:T(8,128)(2,1)S(1)}, u32[]{:S(2)}, u32[]{:S(2)}) collective-permute-start(bf16[64,512]{1,0:T(8,128)(2,1)S(1)} %add_convert_fusion.refs_0_), channel_id=1, source_target_pairs={{0,2},{1,3},{2,0},{3,1},{4,6},{5,7},{6,4},{7,5},{8,10},{9,11},{10,... | collective-permute-start | bytes 196616 | tf_op jit(solution)/shard_map/ppermute | solution.py:479
  103.2 2.4 %collective-permute-done.37.refs_3_ = bf16[64,512]{1,0:T(8,128)(2,1)S(1)} collective-permute-done((bf16[64,512]{1,0:T(8,128)(2,1)S(1)}, bf16[64,512]{1,0:T(8,128)(2,1)S(1)}, u32[]{:S(2)}, u32[]{:S(2)}) %collective-permute-start.37) | collective-permute-done | bytes 65568 | tf_op jit(solution)/shard_map/ppermute | solution.py:479
  105.5 2.0 %collective-permute-done.36.refs_2_ = bf16[64,512]{1,0:T(8,128)(2,1)S(1)} collective-permute-done((bf16[64,512]{1,0:T(8,128)(2,1)S(1)}, bf16[64,512]{1,0:T(8,128)(2,1)S(1)}, u32[]{:S(2)}, u32[]{:S(2)}) %collective-permute-start.36) | collective-permute-done | bytes 65568 | tf_op jit(solution)/shard_map/ppermute | solution.py:479
  108.9 1.9 %collective-permute-start.41 = (f32[1,64]{1,0:T(1,128)S(1)}, f32[1,64]{1,0:T(1,128)S(1)}, u32[]{:S(2)}, u32[]{:S(2)}) collective-permute-start(f32[1,64]{1,0:T(1,128)S(1)} %add.36), channel_id=1, source_target_pairs={{0,24},{8,16},{16,8},{24,0},{1,25},{9,17},{17,9},{25,1},{2,26},{10... | collective-permute-start | bytes 776 | tf_op jit(solution)/shard_map/ppermute | solution.py:479
  (110 shorter events, 35.1 us)
Async XLA Ops:
  19.0 8.4 %collective-permute-start.3 = (f16[64,640]{1,0:T(8,128)(2,1)S(1)}, f16[64,640]{1,0:T(8,128)(2,1)S(1)}, u32[]{:S(2)}, u32[]{:S(2)}) collective-permute-start(f16[64,640]{1,0:T(8,128)(2,1)S(1)} %fusion.1), channel_id=1, source_target_pairs={{0,6},{1,7},{2,4},{3,5},{4,2},{5,3},{6,0},{7,1},{8,14},{9,15},{10,... | collective-permute-start | bytes 245768 | tf_op jit(solution)/shard_map/ppermute | solution.py:479
  24.0 7.2 %collective-permute-start.2 = (f16[64,640]{1,0:T(8,128)(2,1)S(1)}, f16[64,640]{1,0:T(8,128)(2,1)S(1)}, u32[]{:S(2)}, u32[]{:S(2)}) collective-permute-start(f16[64,640]{1,0:T(8,128)(2,1)S(1)} %fusion.1), channel_id=1, source_target_pairs={{0,4},{1,5},{2,6},{3,7},{4,0},{5,1},{6,2},{7,3},{8,12},{9,13},{10,... | collective-permute-start | bytes 245768 | tf_op jit(solution)/shard_map/ppermute | solution.py:479
  24.0 7.2 %collective-permute-start.1 = (f16[64,640]{1,0:T(8,128)(2,1)S(1)}, f16[64,640]{1,0:T(8,128)(2,1)S(1)}, u32[]{:S(2)}, u32[]{:S(2)}) collective-permute-start(f16[64,640]{1,0:T(8,128)(2,1)S(1)} %fusion.1), channel_id=1, source_target_pairs={{0,2},{1,3},{2,0},{3,1},{4,6},{5,7},{6,4},{7,5},{8,10},{9,11},{10,... | collective-permute-start | bytes 245768 | tf_op jit(solution)/shard_map/ppermute | solution.py:479
  33.3 6.8 %collective-permute-start.5 = (bf16[64,1152]{1,0:T(8,128)(2,1)S(1)}, bf16[64,1152]{1,0:T(8,128)(2,1)S(1)}, u32[]{:S(2)}, u32[]{:S(2)}) collective-permute-start(bf16[64,1152]{1,0:T(8,128)(2,1)S(1)} %gradient.16), channel_id=1, source_target_pairs={{0,8},{1,9},{2,10},{3,11},{4,12},{5,13},{6,14},{7,15},{8,0},{9,1},... | collective-permute-start | bytes 442376 | tf_op jit(solution)/shard_map/ppermute | solution.py:505
  35.3 6.5 %collective-permute-start.7 = (bf16[64,1024]{1,0:T(8,128)(2,1)S(1)}, bf16[64,1024]{1,0:T(8,128)(2,1)S(1)}, u32[]{:S(2)}, u32[]{:S(2)}) collective-permute-start(bf16[64,1024]{1,0:T(8,128)(2,1)S(1)} %gradient.17), channel_id=1, source_target_pairs={{0,16},{1,17},{2,18},{3,19},{4,20},{5,21},{6,22},{7,23},{8,24},{9,... | collective-permute-start | bytes 393224 | tf_op jit(solution)/shard_map/ppermute | solution.py:505
  37.4 6.0 %collective-permute-start.9 = (bf16[64,1024]{1,0:T(8,128)(2,1)S(1)}, bf16[64,1024]{1,0:T(8,128)(2,1)S(1)}, u32[]{:S(2)}, u32[]{:S(2)}) collective-permute-start(bf16[64,1024]{1,0:T(8,128)(2,1)S(1)} %gradient.18), channel_id=1, source_target_pairs={{0,8},{1,9},{2,10},{3,11},{4,12},{5,13},{6,14},{7,15},{8,0},{9,1},... | collective-permute-start | bytes 393224 | tf_op jit(solution)/shard_map/ppermute | solution.py:505
  38.5 6.5 %collective-permute-start.11 = (bf16[64,1024]{1,0:T(8,128)(2,1)S(1)}, bf16[64,1024]{1,0:T(8,128)(2,1)S(1)}, u32[]{:S(2)}, u32[]{:S(2)}) collective-permute-start(bf16[64,1024]{1,0:T(8,128)(2,1)S(1)} %gradient.19), channel_id=1, source_target_pairs={{0,16},{1,17},{2,18},{3,19},{4,20},{5,21},{6,22},{7,23},{8,24},{9,... | collective-permute-start | bytes 393224 | tf_op jit(solution)/shard_map/ppermute | solution.py:505
  40.2 7.8 %collective-permute-start.6 = (bf16[64,1152]{1,0:T(8,128)(2,1)S(1)}, bf16[64,1152]{1,0:T(8,128)(2,1)S(1)}, u32[]{:S(2)}, u32[]{:S(2)}) collective-permute-start(bf16[64,1152]{1,0:T(8,128)(2,1)S(1)} %pair_sum.16.left.refs_8_), channel_id=1, source_target_pairs={{0,16},{1,17},{2,18},{3,19},{4,20},{5,21},{6,22},{7,23},{8,24},{9,... | collective-permute-start | bytes 442376 | tf_op jit(solution)/shard_map/ppermute | solution.py:505
  41.9 7.6 %collective-permute-start.8 = (bf16[64,1024]{1,0:T(8,128)(2,1)S(1)}, bf16[64,1024]{1,0:T(8,128)(2,1)S(1)}, u32[]{:S(2)}, u32[]{:S(2)}) collective-permute-start(bf16[64,1024]{1,0:T(8,128)(2,1)S(1)} %pair_sum.18.left), channel_id=1, source_target_pairs={{0,8},{1,9},{2,10},{3,11},{4,12},{5,13},{6,14},{7,15},{8,0},{9,1},... | collective-permute-start | bytes 393224 | tf_op jit(solution)/shard_map/ppermute | solution.py:505
  44.0 6.1 %collective-permute-start.10 = (bf16[64,1024]{1,0:T(8,128)(2,1)S(1)}, bf16[64,1024]{1,0:T(8,128)(2,1)S(1)}, u32[]{:S(2)}, u32[]{:S(2)}) collective-permute-start(bf16[64,1024]{1,0:T(8,128)(2,1)S(1)} %pair_sum.20.left), channel_id=1, source_target_pairs={{0,16},{1,17},{2,18},{3,19},{4,20},{5,21},{6,22},{7,23},{8,24},{9,... | collective-permute-start | bytes 393224 | tf_op jit(solution)/shard_map/ppermute | solution.py:505
  45.1 6.6 %collective-permute-start.12 = (bf16[64,1024]{1,0:T(8,128)(2,1)S(1)}, bf16[64,1024]{1,0:T(8,128)(2,1)S(1)}, u32[]{:S(2)}, u32[]{:S(2)}) collective-permute-start(bf16[64,1024]{1,0:T(8,128)(2,1)S(1)} %pair_sum.22.left), channel_id=1, source_target_pairs={{0,8},{1,9},{2,10},{3,11},{4,12},{5,13},{6,14},{7,15},{8,0},{9,1},... | collective-permute-start | bytes 393224 | tf_op jit(solution)/shard_map/ppermute | solution.py:505
  48.1 8.7 %collective-permute-start.13 = (bf16[64,1024]{1,0:T(8,128)(2,1)S(1)}, bf16[64,1024]{1,0:T(8,128)(2,1)S(1)}, u32[]{:S(2)}, u32[]{:S(2)}) collective-permute-start(bf16[64,1024]{1,0:T(8,128)(2,1)S(1)} %pair_sum.17.refs_1_), channel_id=1, source_target_pairs={{0,8},{1,9},{2,10},{3,11},{4,12},{5,13},{6,14},{7,15},{8,0},{9,1},... | collective-permute-start | bytes 393224 | tf_op jit(solution)/shard_map/ppermute | solution.py:505
  49.5 7.2 %collective-permute-start.14 = (bf16[64,1024]{1,0:T(8,128)(2,1)S(1)}, bf16[64,1024]{1,0:T(8,128)(2,1)S(1)}, u32[]{:S(2)}, u32[]{:S(2)}) collective-permute-start(bf16[64,1024]{1,0:T(8,128)(2,1)S(1)} %pair_sum.19.refs_2_), channel_id=1, source_target_pairs={{0,16},{1,17},{2,18},{3,19},{4,20},{5,21},{6,22},{7,23},{8,24},{9,... | collective-permute-start | bytes 393224 | tf_op jit(solution)/shard_map/ppermute | solution.py:505
  50.1 6.6 %collective-permute-start.15 = (bf16[64,1024]{1,0:T(8,128)(2,1)S(1)}, bf16[64,1024]{1,0:T(8,128)(2,1)S(1)}, u32[]{:S(2)}, u32[]{:S(2)}) collective-permute-start(bf16[64,1024]{1,0:T(8,128)(2,1)S(1)} %pair_sum.21.refs_3_), channel_id=1, source_target_pairs={{0,8},{1,9},{2,10},{3,11},{4,12},{5,13},{6,14},{7,15},{8,0},{9,1},... | collective-permute-start | bytes 393224 | tf_op jit(solution)/shard_map/ppermute | solution.py:505
  51.7 5.0 %collective-permute-start.16 = (bf16[64,1024]{1,0:T(8,128)(2,1)S(1)}, bf16[64,1024]{1,0:T(8,128)(2,1)S(1)}, u32[]{:S(2)}, u32[]{:S(2)}) collective-permute-start(bf16[64,1024]{1,0:T(8,128)(2,1)S(1)} %pair_sum.23.refs_4_), channel_id=1, source_target_pairs={{0,16},{1,17},{2,18},{3,19},{4,20},{5,21},{6,22},{7,23},{8,24},{9,... | collective-permute-start | bytes 393224 | tf_op jit(solution)/shard_map/ppermute | solution.py:505
  60.9 6.8 %collective-permute-start.20 = (bf16[64,512]{1,0:T(8,128)(2,1)S(1)}, bf16[64,512]{1,0:T(8,128)(2,1)S(1)}, u32[]{:S(2)}, u32[]{:S(2)}) collective-permute-start(bf16[64,512]{1,0:T(8,128)(2,1)S(1)} %add_convert_fusion.1.refs_0_), channel_id=1, source_target_pairs={{0,6},{1,7},{2,4},{3,5},{4,2},{5,3},{6,0},{7,1},{8,14},{9,15},{10,... | collective-permute-start | bytes 196616 | tf_op jit(solution)/shard_map/ppermute | solution.py:479
  63.4 6.3 %collective-permute-start.19 = (bf16[64,512]{1,0:T(8,128)(2,1)S(1)}, bf16[64,512]{1,0:T(8,128)(2,1)S(1)}, u32[]{:S(2)}, u32[]{:S(2)}) collective-permute-start(bf16[64,512]{1,0:T(8,128)(2,1)S(1)} %add_convert_fusion.1.refs_0_), channel_id=1, source_target_pairs={{0,4},{1,5},{2,6},{3,7},{4,0},{5,1},{6,2},{7,3},{8,12},{9,13},{10,... | collective-permute-start | bytes 196616 | tf_op jit(solution)/shard_map/ppermute | solution.py:479
  63.4 6.3 %collective-permute-start.18 = (bf16[64,512]{1,0:T(8,128)(2,1)S(1)}, bf16[64,512]{1,0:T(8,128)(2,1)S(1)}, u32[]{:S(2)}, u32[]{:S(2)}) collective-permute-start(bf16[64,512]{1,0:T(8,128)(2,1)S(1)} %add_convert_fusion.1.refs_0_), channel_id=1, source_target_pairs={{0,2},{1,3},{2,0},{3,1},{4,6},{5,7},{6,4},{7,5},{8,10},{9,11},{10,... | collective-permute-start | bytes 196616 | tf_op jit(solution)/shard_map/ppermute | solution.py:479
  71.6 7.0 %collective-permute-start.22 = (bf16[64,1024]{1,0:T(8,128)(2,1)S(1)}, bf16[64,1024]{1,0:T(8,128)(2,1)S(1)}, u32[]{:S(2)}, u32[]{:S(2)}) collective-permute-start(bf16[64,1024]{1,0:T(8,128)(2,1)S(1)} %gradient.24), channel_id=1, source_target_pairs={{0,8},{1,9},{2,10},{3,11},{4,12},{5,13},{6,14},{7,15},{8,0},{9,1},... | collective-permute-start | bytes 393224 | tf_op jit(solution)/shard_map/ppermute | solution.py:505
  73.7 6.2 %collective-permute-start.25 = (bf16[64,1024]{1,0:T(8,128)(2,1)S(1)}, bf16[64,1024]{1,0:T(8,128)(2,1)S(1)}, u32[]{:S(2)}, u32[]{:S(2)}) collective-permute-start(bf16[64,1024]{1,0:T(8,128)(2,1)S(1)} %gradient.25), channel_id=1, source_target_pairs={{0,16},{1,17},{2,18},{3,19},{4,20},{5,21},{6,22},{7,23},{8,24},{9,... | collective-permute-start | bytes 393224 | tf_op jit(solution)/shard_map/ppermute | solution.py:505
  75.3 5.9 %collective-permute-start.28 = (bf16[64,1024]{1,0:T(8,128)(2,1)S(1)}, bf16[64,1024]{1,0:T(8,128)(2,1)S(1)}, u32[]{:S(2)}, u32[]{:S(2)}) collective-permute-start(bf16[64,1024]{1,0:T(8,128)(2,1)S(1)} %gradient.26), channel_id=1, source_target_pairs={{0,8},{1,9},{2,10},{3,11},{4,12},{5,13},{6,14},{7,15},{8,0},{9,1},... | collective-permute-start | bytes 393224 | tf_op jit(solution)/shard_map/ppermute | solution.py:505
  76.6 6.9 %collective-permute-start.31 = (bf16[64,1024]{1,0:T(8,128)(2,1)S(1)}, bf16[64,1024]{1,0:T(8,128)(2,1)S(1)}, u32[]{:S(2)}, u32[]{:S(2)}) collective-permute-start(bf16[64,1024]{1,0:T(8,128)(2,1)S(1)} %gradient.27), channel_id=1, source_target_pairs={{0,16},{1,17},{2,18},{3,19},{4,20},{5,21},{6,22},{7,23},{8,24},{9,... | collective-permute-start | bytes 393224 | tf_op jit(solution)/shard_map/ppermute | solution.py:505
  78.7 7.2 %collective-permute-start.23 = (bf16[64,1024]{1,0:T(8,128)(2,1)S(1)}, bf16[64,1024]{1,0:T(8,128)(2,1)S(1)}, u32[]{:S(2)}, u32[]{:S(2)}) collective-permute-start(bf16[64,1024]{1,0:T(8,128)(2,1)S(1)} %pair_sum.24.left), channel_id=1, source_target_pairs={{0,16},{1,17},{2,18},{3,19},{4,20},{5,21},{6,22},{7,23},{8,24},{9,... | collective-permute-start | bytes 393224 | tf_op jit(solution)/shard_map/ppermute | solution.py:505
  79.8 7.1 %collective-permute-start.26 = (bf16[64,1024]{1,0:T(8,128)(2,1)S(1)}, bf16[64,1024]{1,0:T(8,128)(2,1)S(1)}, u32[]{:S(2)}, u32[]{:S(2)}) collective-permute-start(bf16[64,1024]{1,0:T(8,128)(2,1)S(1)} %pair_sum.26.left), channel_id=1, source_target_pairs={{0,8},{1,9},{2,10},{3,11},{4,12},{5,13},{6,14},{7,15},{8,0},{9,1},... | collective-permute-start | bytes 393224 | tf_op jit(solution)/shard_map/ppermute | solution.py:505
  81.8 6.6 %collective-permute-start.29 = (bf16[64,1024]{1,0:T(8,128)(2,1)S(1)}, bf16[64,1024]{1,0:T(8,128)(2,1)S(1)}, u32[]{:S(2)}, u32[]{:S(2)}) collective-permute-start(bf16[64,1024]{1,0:T(8,128)(2,1)S(1)} %pair_sum.28.left), channel_id=1, source_target_pairs={{0,16},{1,17},{2,18},{3,19},{4,20},{5,21},{6,22},{7,23},{8,24},{9,... | collective-permute-start | bytes 393224 | tf_op jit(solution)/shard_map/ppermute | solution.py:505
  83.5 5.8 %collective-permute-start.32 = (bf16[64,1024]{1,0:T(8,128)(2,1)S(1)}, bf16[64,1024]{1,0:T(8,128)(2,1)S(1)}, u32[]{:S(2)}, u32[]{:S(2)}) collective-permute-start(bf16[64,1024]{1,0:T(8,128)(2,1)S(1)} %pair_sum.30.left), channel_id=1, source_target_pairs={{0,8},{1,9},{2,10},{3,11},{4,12},{5,13},{6,14},{7,15},{8,0},{9,1},... | collective-permute-start | bytes 393224 | tf_op jit(solution)/shard_map/ppermute | solution.py:505
  85.9 8.5 %collective-permute-start.24 = (bf16[64,1024]{1,0:T(8,128)(2,1)S(1)}, bf16[64,1024]{1,0:T(8,128)(2,1)S(1)}, u32[]{:S(2)}, u32[]{:S(2)}) collective-permute-start(bf16[64,1024]{1,0:T(8,128)(2,1)S(1)} %pair_sum.25.refs_1_), channel_id=1, source_target_pairs={{0,8},{1,9},{2,10},{3,11},{4,12},{5,13},{6,14},{7,15},{8,0},{9,1},... | collective-permute-start | bytes 393224 | tf_op jit(solution)/shard_map/ppermute | solution.py:505
  87.0 7.4 %collective-permute-start.27 = (bf16[64,1024]{1,0:T(8,128)(2,1)S(1)}, bf16[64,1024]{1,0:T(8,128)(2,1)S(1)}, u32[]{:S(2)}, u32[]{:S(2)}) collective-permute-start(bf16[64,1024]{1,0:T(8,128)(2,1)S(1)} %pair_sum.27.refs_2_), channel_id=1, source_target_pairs={{0,16},{1,17},{2,18},{3,19},{4,20},{5,21},{6,22},{7,23},{8,24},{9,... | collective-permute-start | bytes 393224 | tf_op jit(solution)/shard_map/ppermute | solution.py:505
  88.4 6.0 %collective-permute-start.30 = (bf16[64,1024]{1,0:T(8,128)(2,1)S(1)}, bf16[64,1024]{1,0:T(8,128)(2,1)S(1)}, u32[]{:S(2)}, u32[]{:S(2)}) collective-permute-start(bf16[64,1024]{1,0:T(8,128)(2,1)S(1)} %pair_sum.29.refs_3_), channel_id=1, source_target_pairs={{0,8},{1,9},{2,10},{3,11},{4,12},{5,13},{6,14},{7,15},{8,0},{9,1},... | collective-permute-start | bytes 393224 | tf_op jit(solution)/shard_map/ppermute | solution.py:505
  98.7 6.8 %collective-permute-start.37 = (bf16[64,512]{1,0:T(8,128)(2,1)S(1)}, bf16[64,512]{1,0:T(8,128)(2,1)S(1)}, u32[]{:S(2)}, u32[]{:S(2)}) collective-permute-start(bf16[64,512]{1,0:T(8,128)(2,1)S(1)} %add_convert_fusion.refs_0_), channel_id=1, source_target_pairs={{0,6},{1,7},{2,4},{3,5},{4,2},{5,3},{6,0},{7,1},{8,14},{9,15},{10,... | collective-permute-start | bytes 196616 | tf_op jit(solution)/shard_map/ppermute | solution.py:479
  101.2 6.3 %collective-permute-start.36 = (bf16[64,512]{1,0:T(8,128)(2,1)S(1)}, bf16[64,512]{1,0:T(8,128)(2,1)S(1)}, u32[]{:S(2)}, u32[]{:S(2)}) collective-permute-start(bf16[64,512]{1,0:T(8,128)(2,1)S(1)} %add_convert_fusion.refs_0_), channel_id=1, source_target_pairs={{0,4},{1,5},{2,6},{3,7},{4,0},{5,1},{6,2},{7,3},{8,12},{9,13},{10,... | collective-permute-start | bytes 196616 | tf_op jit(solution)/shard_map/ppermute | solution.py:479
  101.2 6.3 %collective-permute-start.35 = (bf16[64,512]{1,0:T(8,128)(2,1)S(1)}, bf16[64,512]{1,0:T(8,128)(2,1)S(1)}, u32[]{:S(2)}, u32[]{:S(2)}) collective-permute-start(bf16[64,512]{1,0:T(8,128)(2,1)S(1)} %add_convert_fusion.refs_0_), channel_id=1, source_target_pairs={{0,2},{1,3},{2,0},{3,1},{4,6},{5,7},{6,4},{7,5},{8,10},{9,11},{10,... | collective-permute-start | bytes 196616 | tf_op jit(solution)/shard_map/ppermute | solution.py:479
  (14 other events, 70.4 us)

commit v6 on v5

--- a/solution.py
+++ b/solution.py
@@ -33,7 +33,7 @@
 def half_of(which, piece, variants):
     columns = variants // PIECES
     bits = row_bits()
-    bit = jnp.where(lax.rem(jnp.int32(piece), 2) == 0, bits[0], bits[-1])
+    bit = jnp.where(lax.rem(core_of() + piece, 2) == 0, bits[0], bits[-1])
     own = lax.rem(lax.div(lax.axis_index("row"), bit), 2)
     chosen = own if which == KEEP else 1 - own
     return pl.multiple_of(piece * columns + chosen * (columns // 2), columns // 2)
@@ -506,7 +506,7 @@
         value,
         ("row", "col"),
         [
-            (row * columns + col, (row ^ order[piece % 2]) * columns + col)
+            (row * columns + col, (row ^ order[(col + piece) % 2]) * columns + col)
             for row in range(rows)
             for col in range(columns)
         ],

time: 116 us -> 116 us (level)
  transfers between devices with their start and end apart: 42 -> 42, of which waited for: 20 -> 23; matrix products, arithmetic and copies ran while one was open for 0% -> 0% of each run, Pallas kernels for 13% -> 13%
where the time goes in v6:
time: 116 us; the launch traced here: 115 us
  starting transfers between devices  45.9 us (40%)
  Pallas kernels  35.2 us (30%)
  waiting for transfers between devices  29.1 us (25%)
  between operations  2.94 us (3%)
  local copies, waits for them, and re-layouts  1.61 us (1%)
    ppermute x24, starting transfers between devices, swap_over_rows(): lax.ppermute(value, ('row', 'col'), [(row * columns + col, (row ^ order[(...  26.9 us
    ppermute x18, waiting for transfers between devices, swap(): return lax.ppermute(value, axis, [(i, i ^ distance) for i in range(size)])  23.5 us
    ppermute x18, starting transfers between devices, swap(): return lax.ppermute(value, axis, [(i, i ^ distance) for i in range(size)])  19 us
    pallas_call x1, Pallas kernels, center_and_first_logits(): pl.pallas_call(functools.partial(center_kernel, block, scale, total_varia...  13.1 us
    pallas_call x4, Pallas kernels, update(): pl.pallas_call(functools.partial(update_kernel, which, move, total_varian...  12 us
    pallas_call x16, Pallas kernels, gradient(): pl.pallas_call(functools.partial(gradient_kernel, len(pairs) // 2, which,...  8.17 us
    ppermute x24, waiting for transfers between devices, swap_over_rows(): lax.ppermute(value, ('row', 'col'), [(row * columns + col, (row ^ order[(...  5.61 us
  transfers between devices with their start and end apart: 42, of which 23 were waited for; matrix products, arithmetic and copies ran while one was open for 0% of the time, Pallas kernels for 13%

profile of v6, /device:TPU:0, one launch (start us, length us, event | category | flops | bytes accessed | tf_op | source)
XLA Modules:
  0.0 115.5 jit_solution(5938885782097993340)
XLA Ops:
  2.6 1.6 %copy-done.1 = f32[64,8192]{1,0:T(8,128)S(1)} copy-done((f32[64,8192]{1,0:T(8,128)S(1)}, f32[64,8192]{1,0:T(8,128)}, u32[]{:S(2)}) %copy-start.1) | copy-done | bytes 2097176
  4.2 13.1 %center_and_first_logits.1 = (bf16[1024,8192]{1,0:T(8,128)(2,1)S(1)}, f32[64,640]{1,0:T(8,128)S(1)}, f32[64,640]{1,0:T(8,128)S(1)}) custom-call(s32[1024,8192]{1,0:T(8,128)} %doses.1, f32[64,8192]{1,0:T(8,128)S(1)} %copy-done.1, f32[1,3]{1,0:T(1,128)S(1)} %maximum_bitcast_fusion._.scalars), custom_call_target="tpu_custom_call" | custom-call | flops 8589934592 | tf_op jit(solution)/shard_map/center_and_first_logits/pallas_call | solution.py:134
  19.0 5.0 %collective-permute-start.3 = (f16[64,640]{1,0:T(8,128)(2,1)S(1)}, f16[64,640]{1,0:T(8,128)(2,1)S(1)}, u32[]{:S(2)}, u32[]{:S(2)}) collective-permute-start(f16[64,640]{1,0:T(8,128)(2,1)S(1)} %fusion.1), channel_id=1, source_target_pairs={{0,6},{1,7},{2,4},{3,5},{4,2},{5,3},{6,0},{7,1},{8,14},{9,15},{10,... | collective-permute-start | bytes 245768 | tf_op jit(solution)/shard_map/ppermute | solution.py:479
  24.7 2.7 %collective-permute-done.3 = f16[64,640]{1,0:T(8,128)(2,1)S(1)} collective-permute-done((f16[64,640]{1,0:T(8,128)(2,1)S(1)}, f16[64,640]{1,0:T(8,128)(2,1)S(1)}, u32[]{:S(2)}, u32[]{:S(2)}) %collective-permute-start.3) | collective-permute-done | bytes 81952 | tf_op jit(solution)/shard_map/ppermute | solution.py:479
  27.4 3.8 %collective-permute-done.2 = f16[64,640]{1,0:T(8,128)(2,1)S(1)} collective-permute-done((f16[64,640]{1,0:T(8,128)(2,1)S(1)}, f16[64,640]{1,0:T(8,128)(2,1)S(1)}, u32[]{:S(2)}, u32[]{:S(2)}) %collective-permute-start.2) | collective-permute-done | bytes 81952 | tf_op jit(solution)/shard_map/ppermute | solution.py:479
  33.3 1.6 %collective-permute-start.5 = (bf16[64,1152]{1,0:T(8,128)(2,1)S(1)}, bf16[64,1152]{1,0:T(8,128)(2,1)S(1)}, u32[]{:S(2)}, u32[]{:S(2)}) collective-permute-start(bf16[64,1152]{1,0:T(8,128)(2,1)S(1)} %gradient.16), channel_id=1, source_target_pairs={{0,8},{1,17},{2,10},{3,19},{4,12},{5,21},{6,14},{7,23},{8,0},{9,25... | collective-permute-start | bytes 442376 | tf_op jit(solution)/shard_map/ppermute | solution.py:505
  35.3 1.6 %collective-permute-start.7 = (bf16[64,1024]{1,0:T(8,128)(2,1)S(1)}, bf16[64,1024]{1,0:T(8,128)(2,1)S(1)}, u32[]{:S(2)}, u32[]{:S(2)}) collective-permute-start(bf16[64,1024]{1,0:T(8,128)(2,1)S(1)} %gradient.17), channel_id=1, source_target_pairs={{0,16},{1,9},{2,18},{3,11},{4,20},{5,13},{6,22},{7,15},{8,24},{9,1... | collective-permute-start | bytes 393224 | tf_op jit(solution)/shard_map/ppermute | solution.py:505
  40.3 1.6 %collective-permute-start.6 = (bf16[64,1152]{1,0:T(8,128)(2,1)S(1)}, bf16[64,1152]{1,0:T(8,128)(2,1)S(1)}, u32[]{:S(2)}, u32[]{:S(2)}) collective-permute-start(bf16[64,1152]{1,0:T(8,128)(2,1)S(1)} %pair_sum.16.left.refs_8_), channel_id=1, source_target_pairs={{0,16},{1,9},{2,18},{3,11},{4,20},{5,13},{6,22},{7,15},{8,24},{9,1... | collective-permute-start | bytes 442376 | tf_op jit(solution)/shard_map/ppermute | solution.py:505
  41.9 1.6 %collective-permute-start.8 = (bf16[64,1024]{1,0:T(8,128)(2,1)S(1)}, bf16[64,1024]{1,0:T(8,128)(2,1)S(1)}, u32[]{:S(2)}, u32[]{:S(2)}) collective-permute-start(bf16[64,1024]{1,0:T(8,128)(2,1)S(1)} %pair_sum.18.left), channel_id=1, source_target_pairs={{0,8},{1,17},{2,10},{3,19},{4,12},{5,21},{6,14},{7,23},{8,0},{9,25... | collective-permute-start | bytes 393224 | tf_op jit(solution)/shard_map/ppermute | solution.py:505
  45.2 1.9 %collective-permute-start.12 = (bf16[64,1024]{1,0:T(8,128)(2,1)S(1)}, bf16[64,1024]{1,0:T(8,128)(2,1)S(1)}, u32[]{:S(2)}, u32[]{:S(2)}) collective-permute-start(bf16[64,1024]{1,0:T(8,128)(2,1)S(1)} %pair_sum.22.left), channel_id=1, source_target_pairs={{0,8},{1,17},{2,10},{3,19},{4,12},{5,21},{6,14},{7,23},{8,0},{9,25... | collective-permute-start | bytes 393224 | tf_op jit(solution)/shard_map/ppermute | solution.py:505
  47.2 1.5 %collective-permute-start.13 = (bf16[64,1024]{1,0:T(8,128)(2,1)S(1)}, bf16[64,1024]{1,0:T(8,128)(2,1)S(1)}, u32[]{:S(2)}, u32[]{:S(2)}) collective-permute-start(bf16[64,1024]{1,0:T(8,128)(2,1)S(1)} %pair_sum.17.refs_1_), channel_id=1, source_target_pairs={{0,8},{1,17},{2,10},{3,19},{4,12},{5,21},{6,14},{7,23},{8,0},{9,25... | collective-permute-start | bytes 393224 | tf_op jit(solution)/shard_map/ppermute | solution.py:505
  49.3 1.5 %collective-permute-done.10.right = bf16[64,1024]{1,0:T(8,128)(2,1)S(1)} collective-permute-done((bf16[64,1024]{1,0:T(8,128)(2,1)S(1)}, bf16[64,1024]{1,0:T(8,128)(2,1)S(1)}, u32[]{:S(2)}, u32[]{:S(2)}) %collective-permute-start.10) | collective-permute-done | bytes 131104 | tf_op jit(solution)/shard_map/ppermute | solution.py:505
  51.6 1.4 %collective-permute-start.16 = (bf16[64,1024]{1,0:T(8,128)(2,1)S(1)}, bf16[64,1024]{1,0:T(8,128)(2,1)S(1)}, u32[]{:S(2)}, u32[]{:S(2)}) collective-permute-start(bf16[64,1024]{1,0:T(8,128)(2,1)S(1)} %pair_sum.23.refs_4_), channel_id=1, source_target_pairs={{0,16},{1,9},{2,18},{3,11},{4,20},{5,13},{6,22},{7,15},{8,24},{9,1... | collective-permute-start | bytes 393224 | tf_op jit(solution)/shard_map/ppermute | solution.py:505
  53.1 3.5 %update_and_logits.4 = (f32[64,4096]{1,0:T(8,128)S(1)}, f32[1,4096]{1,0:T(1,128)S(1)}, f32[1,4096]{1,0:T(1,128)S(1)}, f32[1,64]{1,0:T(1,128)}, f32[1024,64]{1,0:T(8,128)S(1)}) custom-call(f32[1,3]{1,0:T(1,128)S(1)} %maximum_bitcast_fusion._.scalars, s32[2,64]{1,0:T(2,128)S(1)} %copy-done.3, f32[2,64,8192]{2,1,0:T(8,128)S(1)} %copy-done, ...), custom_call_target="tpu_custom_call" | custom-call | flops 2147483648 | tf_op jit(solution)/shard_map/update_and_logits/pallas_call | solution.py:464
  56.7 2.8 %update_and_logits.5 = (f32[64,4096]{1,0:T(8,128)S(1)}, f32[64,512]{1,0:T(8,128)S(1)}, f32[64,512]{1,0:T(8,128)S(1)}) custom-call(f32[1,3]{1,0:T(1,128)S(1)} %maximum_bitcast_fusion._.scalars, s32[2,64]{1,0:T(2,128)S(1)} %copy-done.3, f32[2,64,8192]{2,1,0:T(8,128)S(1)} %copy-done, bf16[1024,8192]{1,0:T(8,128)(2,1)S(1)} %get-tuple-element.63.refs_2_.refs_0_, ...), custom_call_target="tpu_custom_call" | custom-call | flops 2147483648 | tf_op jit(solution)/shard_map/update_and_logits/pallas_call | solution.py:464
  60.9 2.5 %collective-permute-start.20 = (bf16[64,512]{1,0:T(8,128)(2,1)S(1)}, bf16[64,512]{1,0:T(8,128)(2,1)S(1)}, u32[]{:S(2)}, u32[]{:S(2)}) collective-permute-start(bf16[64,512]{1,0:T(8,128)(2,1)S(1)} %add_convert_fusion.1.refs_0_), channel_id=1, source_target_pairs={{0,6},{1,7},{2,4},{3,5},{4,2},{5,3},{6,0},{7,1},{8,14},{9,15},{10,... | collective-permute-start | bytes 196616 | tf_op jit(solution)/shard_map/ppermute | solution.py:479
  63.4 1.9 %collective-permute-start.18 = (bf16[64,512]{1,0:T(8,128)(2,1)S(1)}, bf16[64,512]{1,0:T(8,128)(2,1)S(1)}, u32[]{:S(2)}, u32[]{:S(2)}) collective-permute-start(bf16[64,512]{1,0:T(8,128)(2,1)S(1)} %add_convert_fusion.1.refs_0_), channel_id=1, source_target_pairs={{0,2},{1,3},{2,0},{3,1},{4,6},{5,7},{6,4},{7,5},{8,10},{9,11},{10,... | collective-permute-start | bytes 196616 | tf_op jit(solution)/shard_map/ppermute | solution.py:479
  66.2 1.5 %collective-permute-done.20.refs_3_ = bf16[64,512]{1,0:T(8,128)(2,1)S(1)} collective-permute-done((bf16[64,512]{1,0:T(8,128)(2,1)S(1)}, bf16[64,512]{1,0:T(8,128)(2,1)S(1)}, u32[]{:S(2)}, u32[]{:S(2)}) %collective-permute-start.20) | collective-permute-done | bytes 65568 | tf_op jit(solution)/shard_map/ppermute | solution.py:479
  67.7 2.0 %collective-permute-done.19.refs_2_ = bf16[64,512]{1,0:T(8,128)(2,1)S(1)} collective-permute-done((bf16[64,512]{1,0:T(8,128)(2,1)S(1)}, bf16[64,512]{1,0:T(8,128)(2,1)S(1)}, u32[]{:S(2)}, u32[]{:S(2)}) %collective-permute-start.19) | collective-permute-done | bytes 65568 | tf_op jit(solution)/shard_map/ppermute | solution.py:479
  71.8 1.5 %collective-permute-start.22 = (bf16[64,1024]{1,0:T(8,128)(2,1)S(1)}, bf16[64,1024]{1,0:T(8,128)(2,1)S(1)}, u32[]{:S(2)}, u32[]{:S(2)}) collective-permute-start(bf16[64,1024]{1,0:T(8,128)(2,1)S(1)} %gradient.24), channel_id=1, source_target_pairs={{0,8},{1,17},{2,10},{3,19},{4,12},{5,21},{6,14},{7,23},{8,0},{9,25... | collective-permute-start | bytes 393224 | tf_op jit(solution)/shard_map/ppermute | solution.py:505
  75.0 1.4 %collective-permute-start.28 = (bf16[64,1024]{1,0:T(8,128)(2,1)S(1)}, bf16[64,1024]{1,0:T(8,128)(2,1)S(1)}, u32[]{:S(2)}, u32[]{:S(2)}) collective-permute-start(bf16[64,1024]{1,0:T(8,128)(2,1)S(1)} %gradient.26), channel_id=1, source_target_pairs={{0,8},{1,17},{2,10},{3,19},{4,12},{5,21},{6,14},{7,23},{8,0},{9,25... | collective-permute-start | bytes 393224 | tf_op jit(solution)/shard_map/ppermute | solution.py:505
  81.7 1.8 %collective-permute-start.29 = (bf16[64,1024]{1,0:T(8,128)(2,1)S(1)}, bf16[64,1024]{1,0:T(8,128)(2,1)S(1)}, u32[]{:S(2)}, u32[]{:S(2)}) collective-permute-start(bf16[64,1024]{1,0:T(8,128)(2,1)S(1)} %pair_sum.28.left), channel_id=1, source_target_pairs={{0,16},{1,9},{2,18},{3,11},{4,20},{5,13},{6,22},{7,15},{8,24},{9,1... | collective-permute-start | bytes 393224 | tf_op jit(solution)/shard_map/ppermute | solution.py:505
  88.2 1.8 %collective-permute-start.30 = (bf16[64,1024]{1,0:T(8,128)(2,1)S(1)}, bf16[64,1024]{1,0:T(8,128)(2,1)S(1)}, u32[]{:S(2)}, u32[]{:S(2)}) collective-permute-start(bf16[64,1024]{1,0:T(8,128)(2,1)S(1)} %pair_sum.29.refs_3_), channel_id=1, source_target_pairs={{0,8},{1,17},{2,10},{3,19},{4,12},{5,21},{6,14},{7,23},{8,0},{9,25... | collective-permute-start | bytes 393224 | tf_op jit(solution)/shard_map/ppermute | solution.py:505
  90.4 2.8 %update_and_logits.6 = (f32[64,8192]{1,0:T(8,128)}, f32[1024,64]{1,0:T(8,128)S(1)}) custom-call(f32[1,3]{1,0:T(1,128)S(1)} %maximum_bitcast_fusion._.scalars, s32[2,64]{1,0:T(2,128)S(1)} %copy-done.3, f32[2,64,8192]{2,1,0:T(8,128)S(1)} %copy-done, bf16[1024,8192]{1,0:T(8,128)(2,1)S(1)} %get-tuple-element.63.refs_2_.refs_0_, ...), custom_call_target="tpu_custom_call" | custom-call | flops 2147483648 | tf_op jit(solution)/shard_map/update_and_logits/pallas_call | solution.py:464
  93.3 1.9 %collective-permute-done.33.refs_4_ = bf16[64,1024]{1,0:T(8,128)(2,1)S(1)} collective-permute-done((bf16[64,1024]{1,0:T(8,128)(2,1)S(1)}, bf16[64,1024]{1,0:T(8,128)(2,1)S(1)}, u32[]{:S(2)}, u32[]{:S(2)}) %collective-permute-start.33) | collective-permute-done | bytes 131104 | tf_op jit(solution)/shard_map/ppermute | solution.py:505
  95.2 2.8 %update_and_logits.7 = (f32[64,8192]{1,0:T(8,128)}, f32[64,512]{1,0:T(8,128)S(1)}, f32[64,512]{1,0:T(8,128)S(1)}) custom-call(f32[1,3]{1,0:T(1,128)S(1)} %maximum_bitcast_fusion._.scalars, s32[2,64]{1,0:T(2,128)S(1)} %copy-done.3, f32[2,64,8192]{2,1,0:T(8,128)S(1)} %copy-done, ...), custom_call_target="tpu_custom_call", output_to_operand_aliasing={{0}: (11, {})} | custom-call | flops 2147483648 | tf_op jit(solution)/shard_map/update_and_logits/pallas_call | solution.py:464
  99.5 2.5 %collective-permute-start.37 = (bf16[64,512]{1,0:T(8,128)(2,1)S(1)}, bf16[64,512]{1,0:T(8,128)(2,1)S(1)}, u32[]{:S(2)}, u32[]{:S(2)}) collective-permute-start(bf16[64,512]{1,0:T(8,128)(2,1)S(1)} %add_convert_fusion.refs_0_), channel_id=1, source_target_pairs={{0,6},{1,7},{2,4},{3,5},{4,2},{5,3},{6,0},{7,1},{8,14},{9,15},{10,... | collective-permute-start | bytes 196616 | tf_op jit(solution)/shard_map/ppermute | solution.py:479
  102.0 1.9 %collective-permute-start.35 = (bf16[64,512]{1,0:T(8,128)(2,1)S(1)}, bf16[64,512]{1,0:T(8,128)(2,1)S(1)}, u32[]{:S(2)}, u32[]{:S(2)}) collective-permute-start(bf16[64,512]{1,0:T(8,128)(2,1)S(1)} %add_convert_fusion.refs_0_), channel_id=1, source_target_pairs={{0,2},{1,3},{2,0},{3,1},{4,6},{5,7},{6,4},{7,5},{8,10},{9,11},{10,... | collective-permute-start | bytes 196616 | tf_op jit(solution)/shard_map/ppermute | solution.py:479
  103.9 2.4 %collective-permute-done.37.refs_3_ = bf16[64,512]{1,0:T(8,128)(2,1)S(1)} collective-permute-done((bf16[64,512]{1,0:T(8,128)(2,1)S(1)}, bf16[64,512]{1,0:T(8,128)(2,1)S(1)}, u32[]{:S(2)}, u32[]{:S(2)}) %collective-permute-start.37) | collective-permute-done | bytes 65568 | tf_op jit(solution)/shard_map/ppermute | solution.py:479
  106.3 2.0 %collective-permute-done.36.refs_2_ = bf16[64,512]{1,0:T(8,128)(2,1)S(1)} collective-permute-done((bf16[64,512]{1,0:T(8,128)(2,1)S(1)}, bf16[64,512]{1,0:T(8,128)(2,1)S(1)}, u32[]{:S(2)}, u32[]{:S(2)}) %collective-permute-start.36) | collective-permute-done | bytes 65568 | tf_op jit(solution)/shard_map/ppermute | solution.py:479
  109.7 1.4 %collective-permute-start.41 = (f32[1,64]{1,0:T(1,128)S(1)}, f32[1,64]{1,0:T(1,128)S(1)}, u32[]{:S(2)}, u32[]{:S(2)}) collective-permute-start(f32[1,64]{1,0:T(1,128)S(1)} %add.36), channel_id=1, source_target_pairs={{0,24},{8,16},{16,8},{24,0},{1,25},{9,17},{17,9},{25,1},{2,26},{10... | collective-permute-start | bytes 776 | tf_op jit(solution)/shard_map/ppermute | solution.py:479
  111.4 1.7 %collective-permute-start.39 = (f32[1,64]{1,0:T(1,128)S(1)}, f32[1,64]{1,0:T(1,128)S(1)}, u32[]{:S(2)}, u32[]{:S(2)}) collective-permute-start(f32[1,64]{1,0:T(1,128)S(1)} %add.36), channel_id=1, source_target_pairs={{0,8},{8,0},{16,24},{24,16},{1,9},{9,1},{17,25},{25,17},{2,10},{10... | collective-permute-start | bytes 776 | tf_op jit(solution)/shard_map/ppermute | solution.py:479
  (110 shorter events, 33.3 us)
Async XLA Ops:
  19.0 8.4 %collective-permute-start.3 = (f16[64,640]{1,0:T(8,128)(2,1)S(1)}, f16[64,640]{1,0:T(8,128)(2,1)S(1)}, u32[]{:S(2)}, u32[]{:S(2)}) collective-permute-start(f16[64,640]{1,0:T(8,128)(2,1)S(1)} %fusion.1), channel_id=1, source_target_pairs={{0,6},{1,7},{2,4},{3,5},{4,2},{5,3},{6,0},{7,1},{8,14},{9,15},{10,... | collective-permute-start | bytes 245768 | tf_op jit(solution)/shard_map/ppermute | solution.py:479
  24.0 7.2 %collective-permute-start.2 = (f16[64,640]{1,0:T(8,128)(2,1)S(1)}, f16[64,640]{1,0:T(8,128)(2,1)S(1)}, u32[]{:S(2)}, u32[]{:S(2)}) collective-permute-start(f16[64,640]{1,0:T(8,128)(2,1)S(1)} %fusion.1), channel_id=1, source_target_pairs={{0,4},{1,5},{2,6},{3,7},{4,0},{5,1},{6,2},{7,3},{8,12},{9,13},{10,... | collective-permute-start | bytes 245768 | tf_op jit(solution)/shard_map/ppermute | solution.py:479
  24.0 7.2 %collective-permute-start.1 = (f16[64,640]{1,0:T(8,128)(2,1)S(1)}, f16[64,640]{1,0:T(8,128)(2,1)S(1)}, u32[]{:S(2)}, u32[]{:S(2)}) collective-permute-start(f16[64,640]{1,0:T(8,128)(2,1)S(1)} %fusion.1), channel_id=1, source_target_pairs={{0,2},{1,3},{2,0},{3,1},{4,6},{5,7},{6,4},{7,5},{8,10},{9,11},{10,... | collective-permute-start | bytes 245768 | tf_op jit(solution)/shard_map/ppermute | solution.py:479
  33.3 6.9 %collective-permute-start.5 = (bf16[64,1152]{1,0:T(8,128)(2,1)S(1)}, bf16[64,1152]{1,0:T(8,128)(2,1)S(1)}, u32[]{:S(2)}, u32[]{:S(2)}) collective-permute-start(bf16[64,1152]{1,0:T(8,128)(2,1)S(1)} %gradient.16), channel_id=1, source_target_pairs={{0,8},{1,17},{2,10},{3,19},{4,12},{5,21},{6,14},{7,23},{8,0},{9,25... | collective-permute-start | bytes 442376 | tf_op jit(solution)/shard_map/ppermute | solution.py:505
  35.3 6.6 %collective-permute-start.7 = (bf16[64,1024]{1,0:T(8,128)(2,1)S(1)}, bf16[64,1024]{1,0:T(8,128)(2,1)S(1)}, u32[]{:S(2)}, u32[]{:S(2)}) collective-permute-start(bf16[64,1024]{1,0:T(8,128)(2,1)S(1)} %gradient.17), channel_id=1, source_target_pairs={{0,16},{1,9},{2,18},{3,11},{4,20},{5,13},{6,22},{7,15},{8,24},{9,1... | collective-permute-start | bytes 393224 | tf_op jit(solution)/shard_map/ppermute | solution.py:505
  37.4 6.4 %collective-permute-start.9 = (bf16[64,1024]{1,0:T(8,128)(2,1)S(1)}, bf16[64,1024]{1,0:T(8,128)(2,1)S(1)}, u32[]{:S(2)}, u32[]{:S(2)}) collective-permute-start(bf16[64,1024]{1,0:T(8,128)(2,1)S(1)} %gradient.18), channel_id=1, source_target_pairs={{0,8},{1,17},{2,10},{3,19},{4,12},{5,21},{6,14},{7,23},{8,0},{9,25... | collective-permute-start | bytes 393224 | tf_op jit(solution)/shard_map/ppermute | solution.py:505
  38.6 6.6 %collective-permute-start.11 = (bf16[64,1024]{1,0:T(8,128)(2,1)S(1)}, bf16[64,1024]{1,0:T(8,128)(2,1)S(1)}, u32[]{:S(2)}, u32[]{:S(2)}) collective-permute-start(bf16[64,1024]{1,0:T(8,128)(2,1)S(1)} %gradient.19), channel_id=1, source_target_pairs={{0,16},{1,9},{2,18},{3,11},{4,20},{5,13},{6,22},{7,15},{8,24},{9,1... | collective-permute-start | bytes 393224 | tf_op jit(solution)/shard_map/ppermute | solution.py:505
  40.3 6.9 %collective-permute-start.6 = (bf16[64,1152]{1,0:T(8,128)(2,1)S(1)}, bf16[64,1152]{1,0:T(8,128)(2,1)S(1)}, u32[]{:S(2)}, u32[]{:S(2)}) collective-permute-start(bf16[64,1152]{1,0:T(8,128)(2,1)S(1)} %pair_sum.16.left.refs_8_), channel_id=1, source_target_pairs={{0,16},{1,9},{2,18},{3,11},{4,20},{5,13},{6,22},{7,15},{8,24},{9,1... | collective-permute-start | bytes 442376 | tf_op jit(solution)/shard_map/ppermute | solution.py:505
  41.9 6.7 %collective-permute-start.8 = (bf16[64,1024]{1,0:T(8,128)(2,1)S(1)}, bf16[64,1024]{1,0:T(8,128)(2,1)S(1)}, u32[]{:S(2)}, u32[]{:S(2)}) collective-permute-start(bf16[64,1024]{1,0:T(8,128)(2,1)S(1)} %pair_sum.18.left), channel_id=1, source_target_pairs={{0,8},{1,17},{2,10},{3,19},{4,12},{5,21},{6,14},{7,23},{8,0},{9,25... | collective-permute-start | bytes 393224 | tf_op jit(solution)/shard_map/ppermute | solution.py:505
  44.4 6.5 %collective-permute-start.10 = (bf16[64,1024]{1,0:T(8,128)(2,1)S(1)}, bf16[64,1024]{1,0:T(8,128)(2,1)S(1)}, u32[]{:S(2)}, u32[]{:S(2)}) collective-permute-start(bf16[64,1024]{1,0:T(8,128)(2,1)S(1)} %pair_sum.20.left), channel_id=1, source_target_pairs={{0,16},{1,9},{2,18},{3,11},{4,20},{5,13},{6,22},{7,15},{8,24},{9,1... | collective-permute-start | bytes 393224 | tf_op jit(solution)/shard_map/ppermute | solution.py:505
  45.2 6.4 %collective-permute-start.12 = (bf16[64,1024]{1,0:T(8,128)(2,1)S(1)}, bf16[64,1024]{1,0:T(8,128)(2,1)S(1)}, u32[]{:S(2)}, u32[]{:S(2)}) collective-permute-start(bf16[64,1024]{1,0:T(8,128)(2,1)S(1)} %pair_sum.22.left), channel_id=1, source_target_pairs={{0,8},{1,17},{2,10},{3,19},{4,12},{5,21},{6,14},{7,23},{8,0},{9,25... | collective-permute-start | bytes 393224 | tf_op jit(solution)/shard_map/ppermute | solution.py:505
  47.2 9.5 %collective-permute-start.13 = (bf16[64,1024]{1,0:T(8,128)(2,1)S(1)}, bf16[64,1024]{1,0:T(8,128)(2,1)S(1)}, u32[]{:S(2)}, u32[]{:S(2)}) collective-permute-start(bf16[64,1024]{1,0:T(8,128)(2,1)S(1)} %pair_sum.17.refs_1_), channel_id=1, source_target_pairs={{0,8},{1,17},{2,10},{3,19},{4,12},{5,21},{6,14},{7,23},{8,0},{9,25... | collective-permute-start | bytes 393224 | tf_op jit(solution)/shard_map/ppermute | solution.py:505
  48.7 8.0 %collective-permute-start.14 = (bf16[64,1024]{1,0:T(8,128)(2,1)S(1)}, bf16[64,1024]{1,0:T(8,128)(2,1)S(1)}, u32[]{:S(2)}, u32[]{:S(2)}) collective-permute-start(bf16[64,1024]{1,0:T(8,128)(2,1)S(1)} %pair_sum.19.refs_2_), channel_id=1, source_target_pairs={{0,16},{1,9},{2,18},{3,11},{4,20},{5,13},{6,22},{7,15},{8,24},{9,1... | collective-permute-start | bytes 393224 | tf_op jit(solution)/shard_map/ppermute | solution.py:505
  50.9 5.8 %collective-permute-start.15 = (bf16[64,1024]{1,0:T(8,128)(2,1)S(1)}, bf16[64,1024]{1,0:T(8,128)(2,1)S(1)}, u32[]{:S(2)}, u32[]{:S(2)}) collective-permute-start(bf16[64,1024]{1,0:T(8,128)(2,1)S(1)} %pair_sum.21.refs_3_), channel_id=1, source_target_pairs={{0,8},{1,17},{2,10},{3,19},{4,12},{5,21},{6,14},{7,23},{8,0},{9,25... | collective-permute-start | bytes 393224 | tf_op jit(solution)/shard_map/ppermute | solution.py:505
  51.6 5.0 %collective-permute-start.16 = (bf16[64,1024]{1,0:T(8,128)(2,1)S(1)}, bf16[64,1024]{1,0:T(8,128)(2,1)S(1)}, u32[]{:S(2)}, u32[]{:S(2)}) collective-permute-start(bf16[64,1024]{1,0:T(8,128)(2,1)S(1)} %pair_sum.23.refs_4_), channel_id=1, source_target_pairs={{0,16},{1,9},{2,18},{3,11},{4,20},{5,13},{6,22},{7,15},{8,24},{9,1... | collective-permute-start | bytes 393224 | tf_op jit(solution)/shard_map/ppermute | solution.py:505
  60.9 6.8 %collective-permute-start.20 = (bf16[64,512]{1,0:T(8,128)(2,1)S(1)}, bf16[64,512]{1,0:T(8,128)(2,1)S(1)}, u32[]{:S(2)}, u32[]{:S(2)}) collective-permute-start(bf16[64,512]{1,0:T(8,128)(2,1)S(1)} %add_convert_fusion.1.refs_0_), channel_id=1, source_target_pairs={{0,6},{1,7},{2,4},{3,5},{4,2},{5,3},{6,0},{7,1},{8,14},{9,15},{10,... | collective-permute-start | bytes 196616 | tf_op jit(solution)/shard_map/ppermute | solution.py:479
  63.4 6.3 %collective-permute-start.19 = (bf16[64,512]{1,0:T(8,128)(2,1)S(1)}, bf16[64,512]{1,0:T(8,128)(2,1)S(1)}, u32[]{:S(2)}, u32[]{:S(2)}) collective-permute-start(bf16[64,512]{1,0:T(8,128)(2,1)S(1)} %add_convert_fusion.1.refs_0_), channel_id=1, source_target_pairs={{0,4},{1,5},{2,6},{3,7},{4,0},{5,1},{6,2},{7,3},{8,12},{9,13},{10,... | collective-permute-start | bytes 196616 | tf_op jit(solution)/shard_map/ppermute | solution.py:479
  63.4 6.3 %collective-permute-start.18 = (bf16[64,512]{1,0:T(8,128)(2,1)S(1)}, bf16[64,512]{1,0:T(8,128)(2,1)S(1)}, u32[]{:S(2)}, u32[]{:S(2)}) collective-permute-start(bf16[64,512]{1,0:T(8,128)(2,1)S(1)} %add_convert_fusion.1.refs_0_), channel_id=1, source_target_pairs={{0,2},{1,3},{2,0},{3,1},{4,6},{5,7},{6,4},{7,5},{8,10},{9,11},{10,... | collective-permute-start | bytes 196616 | tf_op jit(solution)/shard_map/ppermute | solution.py:479
  71.8 6.9 %collective-permute-start.22 = (bf16[64,1024]{1,0:T(8,128)(2,1)S(1)}, bf16[64,1024]{1,0:T(8,128)(2,1)S(1)}, u32[]{:S(2)}, u32[]{:S(2)}) collective-permute-start(bf16[64,1024]{1,0:T(8,128)(2,1)S(1)} %gradient.24), channel_id=1, source_target_pairs={{0,8},{1,17},{2,10},{3,19},{4,12},{5,21},{6,14},{7,23},{8,0},{9,25... | collective-permute-start | bytes 393224 | tf_op jit(solution)/shard_map/ppermute | solution.py:505
  73.8 6.3 %collective-permute-start.25 = (bf16[64,1024]{1,0:T(8,128)(2,1)S(1)}, bf16[64,1024]{1,0:T(8,128)(2,1)S(1)}, u32[]{:S(2)}, u32[]{:S(2)}) collective-permute-start(bf16[64,1024]{1,0:T(8,128)(2,1)S(1)} %gradient.25), channel_id=1, source_target_pairs={{0,16},{1,9},{2,18},{3,11},{4,20},{5,13},{6,22},{7,15},{8,24},{9,1... | collective-permute-start | bytes 393224 | tf_op jit(solution)/shard_map/ppermute | solution.py:505
  75.0 6.2 %collective-permute-start.28 = (bf16[64,1024]{1,0:T(8,128)(2,1)S(1)}, bf16[64,1024]{1,0:T(8,128)(2,1)S(1)}, u32[]{:S(2)}, u32[]{:S(2)}) collective-permute-start(bf16[64,1024]{1,0:T(8,128)(2,1)S(1)} %gradient.26), channel_id=1, source_target_pairs={{0,8},{1,17},{2,10},{3,19},{4,12},{5,21},{6,14},{7,23},{8,0},{9,25... | collective-permute-start | bytes 393224 | tf_op jit(solution)/shard_map/ppermute | solution.py:505
  76.9 7.1 %collective-permute-start.31 = (bf16[64,1024]{1,0:T(8,128)(2,1)S(1)}, bf16[64,1024]{1,0:T(8,128)(2,1)S(1)}, u32[]{:S(2)}, u32[]{:S(2)}) collective-permute-start(bf16[64,1024]{1,0:T(8,128)(2,1)S(1)} %gradient.27), channel_id=1, source_target_pairs={{0,16},{1,9},{2,18},{3,11},{4,20},{5,13},{6,22},{7,15},{8,24},{9,1... | collective-permute-start | bytes 393224 | tf_op jit(solution)/shard_map/ppermute | solution.py:505
  78.7 6.2 %collective-permute-start.23 = (bf16[64,1024]{1,0:T(8,128)(2,1)S(1)}, bf16[64,1024]{1,0:T(8,128)(2,1)S(1)}, u32[]{:S(2)}, u32[]{:S(2)}) collective-permute-start(bf16[64,1024]{1,0:T(8,128)(2,1)S(1)} %pair_sum.24.left), channel_id=1, source_target_pairs={{0,16},{1,9},{2,18},{3,11},{4,20},{5,13},{6,22},{7,15},{8,24},{9,1... | collective-permute-start | bytes 393224 | tf_op jit(solution)/shard_map/ppermute | solution.py:505
  80.2 6.1 %collective-permute-start.26 = (bf16[64,1024]{1,0:T(8,128)(2,1)S(1)}, bf16[64,1024]{1,0:T(8,128)(2,1)S(1)}, u32[]{:S(2)}, u32[]{:S(2)}) collective-permute-start(bf16[64,1024]{1,0:T(8,128)(2,1)S(1)} %pair_sum.26.left), channel_id=1, source_target_pairs={{0,8},{1,17},{2,10},{3,19},{4,12},{5,21},{6,14},{7,23},{8,0},{9,25... | collective-permute-start | bytes 393224 | tf_op jit(solution)/shard_map/ppermute | solution.py:505
  81.7 6.4 %collective-permute-start.29 = (bf16[64,1024]{1,0:T(8,128)(2,1)S(1)}, bf16[64,1024]{1,0:T(8,128)(2,1)S(1)}, u32[]{:S(2)}, u32[]{:S(2)}) collective-permute-start(bf16[64,1024]{1,0:T(8,128)(2,1)S(1)} %pair_sum.28.left), channel_id=1, source_target_pairs={{0,16},{1,9},{2,18},{3,11},{4,20},{5,13},{6,22},{7,15},{8,24},{9,1... | collective-permute-start | bytes 393224 | tf_op jit(solution)/shard_map/ppermute | solution.py:505
  84.1 6.0 %collective-permute-start.32 = (bf16[64,1024]{1,0:T(8,128)(2,1)S(1)}, bf16[64,1024]{1,0:T(8,128)(2,1)S(1)}, u32[]{:S(2)}, u32[]{:S(2)}) collective-permute-start(bf16[64,1024]{1,0:T(8,128)(2,1)S(1)} %pair_sum.30.left), channel_id=1, source_target_pairs={{0,8},{1,17},{2,10},{3,19},{4,12},{5,21},{6,14},{7,23},{8,0},{9,25... | collective-permute-start | bytes 393224 | tf_op jit(solution)/shard_map/ppermute | solution.py:505
  84.9 10.2 %collective-permute-start.24 = (bf16[64,1024]{1,0:T(8,128)(2,1)S(1)}, bf16[64,1024]{1,0:T(8,128)(2,1)S(1)}, u32[]{:S(2)}, u32[]{:S(2)}) collective-permute-start(bf16[64,1024]{1,0:T(8,128)(2,1)S(1)} %pair_sum.25.refs_1_), channel_id=1, source_target_pairs={{0,8},{1,17},{2,10},{3,19},{4,12},{5,21},{6,14},{7,23},{8,0},{9,25... | collective-permute-start | bytes 393224 | tf_op jit(solution)/shard_map/ppermute | solution.py:505
  86.3 8.9 %collective-permute-start.27 = (bf16[64,1024]{1,0:T(8,128)(2,1)S(1)}, bf16[64,1024]{1,0:T(8,128)(2,1)S(1)}, u32[]{:S(2)}, u32[]{:S(2)}) collective-permute-start(bf16[64,1024]{1,0:T(8,128)(2,1)S(1)} %pair_sum.27.refs_2_), channel_id=1, source_target_pairs={{0,16},{1,9},{2,18},{3,11},{4,20},{5,13},{6,22},{7,15},{8,24},{9,1... | collective-permute-start | bytes 393224 | tf_op jit(solution)/shard_map/ppermute | solution.py:505
  88.2 7.0 %collective-permute-start.30 = (bf16[64,1024]{1,0:T(8,128)(2,1)S(1)}, bf16[64,1024]{1,0:T(8,128)(2,1)S(1)}, u32[]{:S(2)}, u32[]{:S(2)}) collective-permute-start(bf16[64,1024]{1,0:T(8,128)(2,1)S(1)} %pair_sum.29.refs_3_), channel_id=1, source_target_pairs={{0,8},{1,17},{2,10},{3,19},{4,12},{5,21},{6,14},{7,23},{8,0},{9,25... | collective-permute-start | bytes 393224 | tf_op jit(solution)/shard_map/ppermute | solution.py:505
  99.5 6.8 %collective-permute-start.37 = (bf16[64,512]{1,0:T(8,128)(2,1)S(1)}, bf16[64,512]{1,0:T(8,128)(2,1)S(1)}, u32[]{:S(2)}, u32[]{:S(2)}) collective-permute-start(bf16[64,512]{1,0:T(8,128)(2,1)S(1)} %add_convert_fusion.refs_0_), channel_id=1, source_target_pairs={{0,6},{1,7},{2,4},{3,5},{4,2},{5,3},{6,0},{7,1},{8,14},{9,15},{10,... | collective-permute-start | bytes 196616 | tf_op jit(solution)/shard_map/ppermute | solution.py:479
  102.0 6.3 %collective-permute-start.36 = (bf16[64,512]{1,0:T(8,128)(2,1)S(1)}, bf16[64,512]{1,0:T(8,128)(2,1)S(1)}, u32[]{:S(2)}, u32[]{:S(2)}) collective-permute-start(bf16[64,512]{1,0:T(8,128)(2,1)S(1)} %add_convert_fusion.refs_0_), channel_id=1, source_target_pairs={{0,4},{1,5},{2,6},{3,7},{4,0},{5,1},{6,2},{7,3},{8,12},{9,13},{10,... | collective-permute-start | bytes 196616 | tf_op jit(solution)/shard_map/ppermute | solution.py:479
  102.0 6.3 %collective-permute-start.35 = (bf16[64,512]{1,0:T(8,128)(2,1)S(1)}, bf16[64,512]{1,0:T(8,128)(2,1)S(1)}, u32[]{:S(2)}, u32[]{:S(2)}) collective-permute-start(bf16[64,512]{1,0:T(8,128)(2,1)S(1)} %add_convert_fusion.refs_0_), channel_id=1, source_target_pairs={{0,2},{1,3},{2,0},{3,1},{4,6},{5,7},{6,4},{7,5},{8,10},{9,11},{10,... | collective-permute-start | bytes 196616 | tf_op jit(solution)/shard_map/ppermute | solution.py:479
  (14 other events, 70.5 us)
